TPU v7x, 32 devices: a whole 2x2x4 slice. The times are simulated.
32 devices in a mesh: wide: 8 (over z, core), narrow: 4 (over y, x).
Axes of the slice: x: 2, y: 2, z: 4, core: 2. Of those that a mesh axis runs over, the one named last changes fastest.
Arguments:
- tokens: bfloat16 [24576, 1152], P(('wide', 'narrow')), may hold values from -6 to 6
- condition: float32 [12, 1152], replicated, may hold values from -6 to 6
- frame_clip: int32 [96], P('wide'), may hold values from 0 to 11, never falling along the last dimension, each value on 1 to 16 neighbouring positions
- mod_weight: bfloat16 [1152, 6, 1152], P('wide', None, 'narrow'), may hold values from -0.1875 to 0.1875
- mod_bias: bfloat16 [6, 1152], P(None, 'narrow'), may hold values from -3 to 3
- project_weight: bfloat16 [1152, 3, 1152], P('wide', None, 'narrow'), may hold values from -0.1875 to 0.1875
- project_bias: bfloat16 [2, 1152], P(None, 'narrow'), may hold values from -3 to 3
- merge_weight: bfloat16 [1152, 1152], P('narrow', 'wide'), may hold values from -1 to 1
- merge_bias: bfloat16 [1152], P('narrow'), may hold values from -3 to 3
- up_weight: bfloat16 [1152, 4608], P('wide', 'narrow'), may hold values from -0.1875 to 0.1875
- up_bias: bfloat16 [4608], P('narrow'), may hold values from -3 to 3
- down_weight: bfloat16 [4608, 1152], P('narrow', 'wide'), may hold values from -0.1875 to 0.1875
- down_bias: bfloat16 [1152], P('narrow'), may hold values from -3 to 3
- out_cotangent: bfloat16 [24576, 1152], P(('wide', 'narrow')), may hold values from -6 to 6
Outputs:
- output: bfloat16 [24576, 1152], P(('wide', 'narrow'))
- tokens_grad: float32 [24576, 1152], P(('wide', 'narrow'))
- condition_grad: float32 [12, 1152], replicated
- mod_weight_grad: float32 [1152, 6, 1152], P('wide', None, 'narrow')
- mod_bias_grad: float32 [6, 1152], P(None, 'narrow')
- project_weight_grad: float32 [1152, 3, 1152], P('wide', None, 'narrow')
- project_bias_grad: float32 [2, 1152], P(None, 'narrow')
- merge_weight_grad: float32 [1152, 1152], P('narrow', 'wide')
- merge_bias_grad: float32 [1152], P('narrow')
- up_weight_grad: float32 [1152, 4608], P('wide', 'narrow')
- up_bias_grad: float32 [4608], P('narrow')
- down_weight_grad: float32 [4608, 1152], P('narrow', 'wide')
- down_bias_grad: float32 [1152], P('narrow')
Inputs may be any that keep to these rules, and one draw needn't show every extreme that they name: frame_clip[f] is the clip of frame f; the numbers never fall along the frames, each clip holds 1 to 16 frames.
All inputs are finite; a program needn't handle non-finite values.
Results may differ from a plain program's by a relative error of at most 0.019.
Values may be sent and summed in bfloat16 or wider, within the bound.
No kernel may reach another device: no remote copies, remote signals or barrier semaphores. Data moves between devices by JAX's collectives and lax.ppermute only.
A program may use at most 256 MiB of HBM per device.

v0:
```python
import jax
import jax.numpy as jnp
from jax import lax
from jax.sharding import PartitionSpec as P

D = 1152
HEADS = 16
PATCHES = 256


epsilon = 1e-06
highest = lax.Precision.HIGHEST


def normalize(values_in):
    center = jnp.mean(values_in, axis=1)
    spread = jnp.mean(values_in * values_in, axis=1) - center * center
    inverse = lax.rsqrt(spread + epsilon)
    return (inverse, (values_in - center[:, None]) * inverse[:, None])


def norm_back(incoming, normed, inverse):
    first = jnp.mean(incoming, axis=1)
    second = jnp.mean(incoming * normed, axis=1)
    return inverse[:, None] * (incoming - first[:, None] - normed * second[:, None])


def gather_rows(piece):
    return lax.all_gather(piece, "narrow", axis=0, tiled=True)


def gather_grads(piece):
    return lax.all_gather(piece, "narrow", axis=0, tiled=True)


def sum_out(partial_sum):
    return lax.psum_scatter(partial_sum, "narrow", scatter_dimension=0, tiled=True)


def sum_in(partial_sum):
    return lax.psum_scatter(partial_sum, "narrow", scatter_dimension=0, tiled=True)


def gelu_values(upper):
    return jax.nn.gelu(upper, approximate=True)


def gelu_grad_rounded(upper, incoming):
    unused, pullback = jax.vjp(gelu_values, upper)
    return pullback(incoming)[0].astype(jnp.bfloat16)


def scores_of(query, keys, scale):
    return jnp.einsum("fshe,fthe->fhst", query, keys, preferred_element_type=jnp.float32) * scale


def attend(query, keys, values, scale):
    scores = scores_of(query, keys, scale)
    top_score = jnp.max(scores, axis=-1, keepdims=True)
    logsum = top_score + jnp.log(jnp.sum(jnp.exp(scores - top_score), axis=-1, keepdims=True))
    weights = jnp.exp(scores - logsum).astype(jnp.bfloat16)
    result = jnp.einsum("fhst,fthe->fshe", weights, values, preferred_element_type=jnp.float32)
    return (result, logsum)


def attend_back(query, keys, values, logsum, result_grad, scale):
    softmax_out = jnp.exp(scores_of(query, keys, scale) - logsum)
    rounded = softmax_out.astype(jnp.bfloat16)
    value_grad = jnp.einsum(
        "fhst,fshe->fthe", rounded, result_grad, preferred_element_type=jnp.float32
    )
    weight_grad = jnp.einsum(
        "fshe,fthe->fhst", result_grad, values, preferred_element_type=jnp.float32
    )
    score_grad = softmax_out * (
        weight_grad - jnp.sum(softmax_out * weight_grad, axis=-1, keepdims=True)
    )
    score_grad = score_grad.astype(jnp.bfloat16)
    query_grad = (
        jnp.einsum("fhst,fthe->fshe", score_grad, keys, preferred_element_type=jnp.float32) * scale
    )
    key_grad = (
        jnp.einsum("fhst,fshe->fthe", score_grad, query, preferred_element_type=jnp.float32) * scale
    )
    return (query_grad, key_grad, value_grad)


def into_place(local, position):
    width = local.shape[-1]
    empty = jnp.zeros(local.shape[:-1] + (width * lax.axis_size("narrow"),), jnp.float32)
    return lax.dynamic_update_slice_in_dim(empty, local, position * width, local.ndim - 1)


def from_place(whole, width, position):
    return lax.dynamic_slice_in_dim(whole, position * width, width, whole.ndim - 1)


def shards(
    tokens,
    condition,
    frame_clip,
    mod_weight,
    mod_bias,
    project_weight,
    project_bias,
    merge_weight,
    merge_bias,
    up_weight,
    up_bias,
    down_weight,
    down_bias,
    out_cotangent,
):
    inputs = tokens.astype(jnp.float32)
    rows_here, full_width = inputs.shape
    narrow_count = lax.axis_size("narrow")
    position = lax.axis_index("narrow")
    group_rows = rows_here * narrow_count
    frames_group = group_rows // PATCHES
    part_width = full_width // narrow_count
    head_size = D // HEADS
    heads_here = HEADS // narrow_count
    scale = head_size ** (-0.5)
    mod_full, project_full, up_full, merge_full, down_full = (
        lax.all_gather(mod_weight, "wide", axis=0, tiled=True),
        lax.all_gather(project_weight, "wide", axis=0, tiled=True),
        lax.all_gather(up_weight, "wide", axis=0, tiled=True),
        lax.all_gather(merge_weight, "wide", axis=1, tiled=True),
        lax.all_gather(down_weight, "wide", axis=1, tiled=True),
    )
    active = jax.nn.silu(condition).astype(jnp.bfloat16)
    mode_slice = jnp.einsum("cd,dki->cki", active, mod_full, preferred_element_type=jnp.float32)
    mode_slice = mode_slice + mod_bias.astype(jnp.float32)[None]
    modes, merge_bias_full, down_bias_full = (
        lax.all_gather(mode_slice, "narrow", axis=2, tiled=True),
        lax.all_gather(merge_bias.astype(jnp.float32), "narrow", axis=0, tiled=True),
        lax.all_gather(down_bias.astype(jnp.float32), "narrow", axis=0, tiled=True),
    )
    clip_count = condition.shape[0]
    frames_wide = frame_clip.shape[0]
    row_frame = (position * rows_here + jnp.arange(rows_here, dtype=jnp.int32)) // PATCHES
    frame_pick = row_frame[:, None] == jnp.arange(frames_wide, dtype=jnp.int32)[None, :]
    row_clip = jnp.sum(jnp.where(frame_pick, frame_clip[None, :], 0), axis=1)
    picker = (row_clip[:, None] == jnp.arange(clip_count, dtype=jnp.int32)[None, :]).astype(
        jnp.float32
    )
    token_mod = jnp.dot(
        picker, modes.reshape(clip_count, 6 * full_width), precision=highest
    ).reshape(rows_here, 6, full_width)
    shift_a = token_mod[:, 0]
    scale_a = token_mod[:, 1]
    gate_a = token_mod[:, 2]
    shift_b = token_mod[:, 3]
    scale_b = token_mod[:, 4]
    gate_b = token_mod[:, 5]
    inverse_a, normed_a = normalize(inputs)
    hidden_a = (normed_a * (1.0 + scale_a) + shift_a).astype(jnp.bfloat16)
    wide_a = gather_rows(hidden_a)
    project = jnp.einsum("td,dki->tki", wide_a, project_full, preferred_element_type=jnp.float32)
    biases = project_bias.astype(jnp.float32)
    query = (project[:, 0] + biases[0]).astype(jnp.bfloat16)
    keys = project[:, 1].astype(jnp.bfloat16)
    values = (project[:, 2] + biases[1]).astype(jnp.bfloat16)
    framed = (frames_group, PATCHES, heads_here, head_size)
    query_f = query.reshape(framed)
    keys_f = keys.reshape(framed)
    values_f = values.reshape(framed)
    attended, logsum = attend(query_f, keys_f, values_f, scale)
    attended = attended.reshape(group_rows, part_width).astype(jnp.bfloat16)
    merged = sum_out(jnp.dot(attended, merge_full, preferred_element_type=jnp.float32))
    branch_a = merged + merge_bias_full
    middle = inputs + gate_a * branch_a
    inverse_b, normed_b = normalize(middle)
    hidden_b = (normed_b * (1.0 + scale_b) + shift_b).astype(jnp.bfloat16)
    wide_b = gather_rows(hidden_b)
    upper = jnp.dot(wide_b, up_full, preferred_element_type=jnp.float32) + up_bias.astype(
        jnp.float32
    )
    gelu_out = gelu_values(upper).astype(jnp.bfloat16)
    core = sum_out(jnp.dot(gelu_out, down_full, preferred_element_type=jnp.float32))
    branch_b = core + down_bias_full
    output = (middle + gate_b * branch_b).astype(jnp.bfloat16)
    grad_out = out_cotangent.astype(jnp.float32)
    gated_out = gate_b * grad_out
    down_bias_grad = jnp.sum(gated_out, axis=0)
    core_grad = gated_out.astype(jnp.bfloat16)
    wide_grad_b = gather_grads(core_grad)
    gelu_grad = jnp.einsum("td,fd->tf", wide_grad_b, down_full, preferred_element_type=jnp.float32)
    down_part = jnp.einsum("tf,td->fd", gelu_out, wide_grad_b, preferred_element_type=jnp.float32)
    upper_grad = gelu_grad_rounded(upper, gelu_grad)
    up_bias_grad = jnp.sum(upper_grad.astype(jnp.float32), axis=0)
    up_part = jnp.einsum("td,tf->df", wide_b, upper_grad, preferred_element_type=jnp.float32)
    hidden_b_grad = sum_in(
        jnp.einsum("tf,df->td", upper_grad, up_full, preferred_element_type=jnp.float32)
    )
    middle_grad = grad_out + norm_back(hidden_b_grad * (1.0 + scale_b), normed_b, inverse_b)
    gated_middle = gate_a * middle_grad
    merge_bias_grad = jnp.sum(gated_middle, axis=0)
    merged_grad = gated_middle.astype(jnp.bfloat16)
    wide_grad_a = gather_grads(merged_grad)
    attended_grad = jnp.einsum(
        "td,id->ti", wide_grad_a, merge_full, preferred_element_type=jnp.float32
    )
    attended_grad = attended_grad.astype(jnp.bfloat16)
    merge_part = jnp.einsum("ti,td->id", attended, wide_grad_a, preferred_element_type=jnp.float32)
    query_grad, key_grad, value_grad = attend_back(
        query_f, keys_f, values_f, logsum, attended_grad.reshape(framed), scale
    )
    query_grad = query_grad.reshape(group_rows, part_width).astype(jnp.bfloat16)
    key_grad = key_grad.reshape(group_rows, part_width).astype(jnp.bfloat16)
    value_grad = value_grad.reshape(group_rows, part_width).astype(jnp.bfloat16)
    triple_grad = jnp.stack([query_grad, key_grad, value_grad], axis=1)
    project_bias_grad = jnp.stack(
        [
            jnp.sum(query_grad.astype(jnp.float32), axis=0),
            jnp.sum(value_grad.astype(jnp.float32), axis=0),
        ]
    )
    project_part = jnp.einsum(
        "td,tki->dki", wide_a, triple_grad, preferred_element_type=jnp.float32
    )
    hidden_a_grad = sum_in(
        jnp.einsum("tki,dki->td", triple_grad, project_full, preferred_element_type=jnp.float32)
    )
    tokens_grad = middle_grad + norm_back(hidden_a_grad * (1.0 + scale_a), normed_a, inverse_a)
    token_mod_grad = jnp.stack(
        [
            hidden_a_grad,
            hidden_a_grad * normed_a,
            middle_grad * branch_a,
            hidden_b_grad,
            hidden_b_grad * normed_b,
            grad_out * branch_b,
        ],
        axis=1,
    )
    clip_grad = jnp.einsum("rc,rki->cki", picker, token_mod_grad, precision=highest)
    clip_slice = lax.psum_scatter(
        clip_grad.astype(jnp.bfloat16), "narrow", scatter_dimension=2, tiled=True
    ).astype(jnp.float32)
    mod_bias_part = jnp.sum(clip_slice, axis=0)
    mod_part = jnp.einsum("cd,cki->dki", active.astype(jnp.float32), clip_slice, precision=highest)
    active_grad = jnp.einsum(
        "cki,dki->cd", clip_slice, mod_full.astype(jnp.float32), precision=highest
    )
    unused, silu_pullback = jax.vjp(jax.nn.silu, condition)
    condition_part = silu_pullback(active_grad)[0]
    mod_weight_grad, project_weight_grad, up_weight_grad, merge_weight_grad, down_weight_grad = (
        lax.psum_scatter(
            mod_part.astype(jnp.bfloat16), "wide", scatter_dimension=0, tiled=True
        ).astype(jnp.float32),
        lax.psum_scatter(
            project_part.astype(jnp.bfloat16), "wide", scatter_dimension=0, tiled=True
        ).astype(jnp.float32),
        lax.psum_scatter(
            up_part.astype(jnp.bfloat16), "wide", scatter_dimension=0, tiled=True
        ).astype(jnp.float32),
        lax.psum_scatter(
            merge_part.astype(jnp.bfloat16), "wide", scatter_dimension=1, tiled=True
        ).astype(jnp.float32),
        lax.psum_scatter(
            down_part.astype(jnp.bfloat16), "wide", scatter_dimension=1, tiled=True
        ).astype(jnp.float32),
    )
    summed = lax.psum(
        (
            condition_part,
            into_place(mod_bias_part, position),
            into_place(project_bias_grad, position),
            merge_bias_grad,
            into_place(up_bias_grad, position),
            down_bias_grad,
        ),
        ("wide", "narrow"),
    )
    condition_grad = summed[0]
    mod_bias_grad = from_place(summed[1], part_width, position)
    project_bias_out = from_place(summed[2], part_width, position)
    merge_bias_out = from_place(summed[3], part_width, position)
    up_bias_out = from_place(summed[4], up_bias.shape[0], position)
    down_bias_out = from_place(summed[5], part_width, position)
    return (
        output,
        tokens_grad,
        condition_grad,
        mod_weight_grad,
        mod_bias_grad,
        project_weight_grad,
        project_bias_out,
        merge_weight_grad,
        merge_bias_out,
        up_weight_grad,
        up_bias_out,
        down_weight_grad,
        down_bias_out,
    )


def solution(mesh):
    placed = (
        P(("wide", "narrow"), None),
        P(),
        P("wide"),
        P("wide", None, "narrow"),
        P(None, "narrow"),
        P("wide", None, "narrow"),
        P(None, "narrow"),
        P("narrow", "wide"),
        P("narrow"),
        P("wide", "narrow"),
        P("narrow"),
        P("narrow", "wide"),
        P("narrow"),
        P(("wide", "narrow"), None),
    )
    return jax.shard_map(
        shards,
        mesh=mesh,
        in_specs=placed,
        out_specs=(
            P(("wide", "narrow"), None),
            P(("wide", "narrow"), None),
            P(),
            P("wide", None, "narrow"),
            P(None, "narrow"),
            P("wide", None, "narrow"),
            P(None, "narrow"),
            P("narrow", "wide"),
            P("narrow"),
            P("wide", "narrow"),
            P("narrow"),
            P("narrow", "wide"),
            P("narrow"),
        ),
        check_vma=False,
    )
```

profile of v0, /device:TPU:0, one launch (start us, length us, event | category | flops | bytes accessed | tf_op | source)
XLA Modules:
  0.0 1667.6 jit_solution(6557990877418631258)
XLA Ops:
  12.3 56.6 %all-gather.9.cloned.1.call-done = bf16[1152,6,288]{2,0,1:T(8,128)(2,1)} async-done(((bf16[144,6,288]{2,0,1:T(8,128)(2,1)}), bf16[1152,6,288]{2,0,1:T(8,128)(2,1)}) %all-gather.9.cloned.1.call-update) | async-done | bytes 3981328 | tf_op jit(solution)/shard_map/all_gather | solution.py:125
  72.7 45.5 %all_gather.37 = f32[12,6,1152]{0,1,2:T(8,128)} all-gather(f32[12,6,288]{0,1,2:T(8,128)S(1)} %copy.77), channel_id=1, replica_groups=mesh['wide'=8,'narrow'=4] {'narrow'}, dimensions={2}, use_global_device_ids=true | all-gather | bytes 414720 | tf_op jit(solution)/shard_map/all_gather | solution.py:135
  121.9 8.7 fusion.55
  140.0 16.1 all_gather.40
  156.1 58.3 %all-gather.11.cloned.1.call-done = bf16[3072,1152]{1,0:T(8,128)(2,1)} async-done(((bf16[768,1152]{1,0:T(8,128)(2,1)}), bf16[3072,1152]{1,0:T(8,128)(2,1)}) %all-gather.11.cloned.1.call-update) | async-done | bytes 7077904 | tf_op jit(solution)/shard_map/all_gather | solution.py:29
  214.4 10.5 fusion.10
  275.0 16.0 all-reduce.3
  291.0 115.8 %reduce-scatter.13.cloned.1.call-done = f32[768,1152]{1,0:T(8,128)} async-done(((f32[3072,1152]{1,0:T(8,128)}), f32[768,1152]{1,0:T(8,128)}) %reduce-scatter.13.cloned.1.call-update) | async-done | bytes 3538960 | tf_op jit(solution)/shard_map/reduce_scatter | solution.py:37
  419.8 22.7 %all-gather.19.cloned.1.call-done = bf16[1152,1152]{0,1:T(8,128)(2,1)} async-done(((bf16[1152,144]{0,1:T(8,128)(2,1)}), bf16[1152,1152]{0,1:T(8,128)(2,1)}) %all-gather.19.cloned.1.call-update) | async-done | bytes 2654224 | tf_op jit(solution)/shard_map/all_gather | solution.py:129
  442.5 78.0 %all-gather.21.cloned.1.call-done = bf16[3072,1152]{1,0:T(8,128)(2,1)} async-done(((bf16[768,1152]{1,0:T(8,128)(2,1)}), bf16[3072,1152]{1,0:T(8,128)(2,1)}) %all-gather.21.cloned.1.call-update) | async-done | bytes 7077904 | tf_op jit(solution)/shard_map/all_gather | solution.py:33
  520.5 16.1 fusion.78
  536.6 19.7 %all-gather.17.cloned.1.call-done = bf16[1152,1152]{1,0:T(8,128)(2,1)} async-done(((bf16[144,1152]{1,0:T(8,128)(2,1)}), bf16[1152,1152]{1,0:T(8,128)(2,1)}) %all-gather.17.cloned.1.call-update) | async-done | bytes 2654224 | tf_op jit(solution)/shard_map/all_gather | solution.py:127
  556.3 78.1 %all-gather.15.cloned.1.call-done = bf16[3072,1152]{1,0:T(8,128)(2,1)} async-done(((bf16[768,1152]{1,0:T(8,128)(2,1)}), bf16[3072,1152]{1,0:T(8,128)(2,1)}) %all-gather.15.cloned.1.call-update) | async-done | bytes 7077904 | tf_op jit(solution)/shard_map/all_gather | solution.py:29
  634.5 25.4 %convert_reduce_fusion = (f32[1152]{0:T(1024)}, bf16[3072,1152]{1,0:T(8,128)(2,1)S(1)}, f32[3072,1152]{1,0:T(8,128)}) fusion(f32[3072,1152]{1,0:T(8,128)} %fusion.78, f32[1152]{0:T(1024)S(1)} %convert_element_type.195, bf16[3072,1152]{1,0:T(8,128)(2,1)} %all-gather.15.cloned.1.call-done, bf16[1152,1152]{1,0:T(8,128)(2,1)} %all-gather.17.cloned.1.call-done), kind=kOutput, calls=%fused_computation.9 | convolution fusion | flops 8235121664 | bytes 45130752 | tf_op jit(solution)/shard_map/dot_general | solution.py:176
  662.8 12.7 fusion.79
  675.5 19.5 %fusion.73 = f32[3072,1152]{1,0:T(8,128)} fusion(bf16[1152,1152]{0,1:T(8,128)(2,1)} %all-gather.19.cloned.1.call-done, f32[3072,1152]{1,0:T(8,128)} %get-tuple-element.51), kind=kOutput, calls=%fused_computation.148 | convolution fusion | flops 8185577472 | bytes 30965760 | tf_op jit(solution)/shard_map/dot_general | solution.py:180
  695.2 114.1 %reduce-scatter.17.cloned.1.call-done = f32[768,1152]{1,0:T(8,128)} async-done(((f32[3072,1152]{1,0:T(8,128)}), f32[768,1152]{1,0:T(8,128)}) %reduce-scatter.17.cloned.1.call-update) | async-done | bytes 3538960 | tf_op jit(solution)/shard_map/reduce_scatter | solution.py:41
  814.0 131.9 %reduce-scatter.15.cloned.1.call-done = f32[768,1152]{1,0:T(8,128)} async-done(((f32[3072,1152]{1,0:T(8,128)}), f32[768,1152]{1,0:T(8,128)}) %reduce-scatter.15.cloned.1.call-update) | async-done | bytes 3538960 | tf_op jit(solution)/shard_map/reduce_scatter | solution.py:37
  945.9 10.9 fusion.42
  956.9 76.8 %all-gather.23.cloned.1.call-done = bf16[3072,1152]{1,0:T(8,128)(2,1)} async-done(((bf16[768,1152]{1,0:T(8,128)(2,1)}), bf16[3072,1152]{1,0:T(8,128)(2,1)}) %all-gather.23.cloned.1.call-update) | async-done | bytes 7077904 | tf_op jit(solution)/shard_map/all_gather | solution.py:33
  1045.0 10.4 convert_reduce_fusion.2
  1055.4 15.2 multiply_reduce_fusion
  1114.4 13.6 convolution_bitcast_fusion
  1128.0 133.7 %reduce-scatter.19.cloned.1.call-done = f32[768,1152]{1,0:T(8,128)} async-done(((f32[3072,1152]{1,0:T(8,128)}), f32[768,1152]{1,0:T(8,128)}) %reduce-scatter.19.cloned.1.call-update) | async-done | bytes 3538960 | tf_op jit(solution)/shard_map/reduce_scatter | solution.py:41
  1285.3 17.5 %convolution_convert_fusion = bf16[1152,1152]{0,1:T(8,128)(2,1)} fusion(bf16[3072,1152]{1,0:T(8,128)(2,1)} %all-gather.21.cloned.1.call-done, f32[3072,1152]{1,0:T(8,128)} %get-tuple-element.51), kind=kOutput, calls=%fused_computation.19 | convolution fusion | flops 8186904576 | bytes 23887872 | tf_op jit(solution)/shard_map/tf,td->fd/dot_general | solution.py:189
  1302.9 14.7 convolution_convert_fusion.1
  1325.0 14.4 fusion.12
  1366.2 22.5 %reduce-scatter.27.cloned.1.call-done = bf16[144,1152]{1,0:T(8,128)(2,1)} async-done(((bf16[1152,1152]{1,0:T(8,128)(2,1)}), bf16[144,1152]{1,0:T(8,128)(2,1)}) %reduce-scatter.27.cloned.1.call-update) | async-done | bytes 331792 | tf_op jit(solution)/shard_map/reduce_scatter | solution.py:255
  1390.5 31.7 %reduce-scatter.25.cloned.1.call-done = bf16[288,144]{0,1:T(8,128)(2,1)} async-done(((bf16[288,1152]{0,1:T(8,128)(2,1)}), bf16[288,144]{0,1:T(8,128)(2,1)}) %reduce-scatter.25.cloned.1.call-update) | async-done | bytes 82960 | tf_op jit(solution)/shard_map/reduce_scatter | solution.py:258
  1423.8 36.8 %reduce-scatter.23.cloned.1.call-done = bf16[144,3,288]{2,0,1:T(8,128)(2,1)} async-done(((bf16[1152,3,288]{2,0,1:T(8,128)(2,1)}), bf16[144,3,288]{2,0,1:T(8,128)(2,1)}) %reduce-scatter.23.cloned.1.call-update) | async-done | bytes 248848 | tf_op jit(solution)/shard_map/reduce_scatter | solution.py:252
  1468.4 124.3 %all-reduce.6.cloned.1.call-done = (f32[12,1152]{1,0:T(8,128)}, f32[6,1152]{1,0:T(8,128)}, f32[2,1152]{1,0:T(2,128)}, f32[1152]{0:T(1024)}, f32[4608]{0:T(1024)}, /*index=5*/f32[1152]{0:T(1024)}) async-done(((f32[12,1152]{1,0:T(8,128)}, f32[6,1152]{1,0:T(8,128)}, f32[2,1152]{1,0:T(2,128)}, f32[1152]{0:T(1024)}, f32[4608]{0:T(1024)}, /*index=5*/f32[1152]{0:T(1024)}), (f32[12,1152]{1,0:T(8,128)}, ...) | async-done | bytes 119824 | tf_op jit(solution)/shard_map/psum | solution.py:265
  1599.5 57.6 %reduce-scatter.21.cloned.1.call-done = bf16[144,6,288]{2,0,1:T(8,128)(2,1)} async-done(((bf16[1152,6,288]{2,0,1:T(8,128)(2,1)}), bf16[144,6,288]{2,0,1:T(8,128)(2,1)}) %reduce-scatter.21.cloned.1.call-update) | async-done | bytes 497680 | tf_op jit(solution)/shard_map/reduce_scatter | solution.py:249
  (238 shorter events, 226.2 us)
Async XLA Ops:
  7.2 61.7 %all-gather.9.cloned.1.call-start = ((), (), s32[]{:S(2)}) async-start(), calls=%async_computation.10 | async-start | bytes 5971968 | tf_op jit(solution)/shard_map/all_gather | solution.py:125
  7.9 148.2 %all-gather.13.cloned.1.call-start = ((), (), s32[]{:S(2)}) async-start(), calls=%async_computation.12 | async-start | bytes 2985984 | tf_op jit(solution)/shard_map/all_gather | solution.py:126
  8.7 205.8 %all-gather.11.cloned.1.call-start = ((), (), s32[]{:S(2)}) async-start(), calls=%async_computation.11 | async-start | bytes 8847360 | tf_op jit(solution)/shard_map/all_gather | solution.py:29
  10.2 111.7 %copy-start.33 = (s32[768]{0:T(1024)}, s32[768]{0:T(1024)S(1)}, u32[]{:S(2)}) copy-start(s32[768]{0:T(1024)S(1)} %select_reduce_fusion) | copy-start | bytes 9220
  12.3 118.3 %copy-start.29 = (f32[768]{0:T(1024)}, f32[768]{0:T(1024)S(1)}, u32[]{:S(2)}) copy-start(f32[768]{0:T(1024)S(1)} %get-tuple-element.47) | copy-start | bytes 9220
  12.3 118.3 %copy-start.31 = (f32[768]{0:T(1024)}, f32[768]{0:T(1024)S(1)}, u32[]{:S(2)}) copy-start(f32[768]{0:T(1024)S(1)} %get-tuple-element.48) | copy-start | bytes 9220
  139.7 267.1 %reduce-scatter.13.cloned.1.call-start = ((), (), s32[]{:S(2)}) async-start(), calls=%async_computation.13 | async-start | bytes 17694720 | tf_op jit(solution)/shard_map/reduce_scatter | solution.py:37
  156.1 108.1 %copy-start.22 = (bf16[288,1152]{0,1:T(8,128)(2,1)}, bf16[288,1152]{0,1:T(8,128)(2,1)S(1)}, u32[]{:S(2)}) copy-start(bf16[288,1152]{0,1:T(8,128)(2,1)S(1)} %all_gather.40) | copy-start | bytes 1990660
  272.9 169.6 %all-gather.19.cloned.1.call-start = ((), (), s32[]{:S(2)}) async-start(), calls=%async_computation.16 | async-start | bytes 2985984 | tf_op jit(solution)/shard_map/all_gather | solution.py:129
  273.5 247.0 %all-gather.21.cloned.1.call-start = ((), (), s32[]{:S(2)}) async-start(), calls=%async_computation.18 | async-start | bytes 8847360 | tf_op jit(solution)/shard_map/all_gather | solution.py:33
  291.0 120.4 %copy-start.35 = (f32[1152]{0:T(1024)}, f32[1152]{0:T(1024)S(1)}, u32[]{:S(2)}) copy-start(f32[1152]{0:T(1024)S(1)} %get-tuple-element.33) | copy-start | bytes 13828
  417.6 138.8 %all-gather.17.cloned.1.call-start = ((), (), s32[]{:S(2)}) async-start(), calls=%async_computation.15 | async-start | bytes 2985984 | tf_op jit(solution)/shard_map/all_gather | solution.py:127
  418.3 216.1 %all-gather.15.cloned.1.call-start = ((), (), s32[]{:S(2)}) async-start(), calls=%async_computation.14 | async-start | bytes 8847360 | tf_op jit(solution)/shard_map/all_gather | solution.py:29
  419.1 390.2 %reduce-scatter.17.cloned.1.call-start = ((), (), s32[]{:S(2)}) async-start(), calls=%async_computation.19 | async-start | bytes 17694720 | tf_op jit(solution)/shard_map/reduce_scatter | solution.py:41
  634.5 28.3 %copy-start.45 = (bf16[1152,1152]{1,0:T(8,128)(2,1)S(1)}, bf16[1152,1152]{1,0:T(8,128)(2,1)}, u32[]{:S(2)}) copy-start(bf16[1152,1152]{1,0:T(8,128)(2,1)} %all-gather.17.cloned.1.call-done) | copy-start | bytes 7962628
  675.5 270.4 %reduce-scatter.15.cloned.1.call-start = ((), (), s32[]{:S(2)}) async-start(), calls=%async_computation.17 | async-start | bytes 17694720 | tf_op jit(solution)/shard_map/reduce_scatter | solution.py:37
  695.1 250.8 %copy-start.37 = (f32[1152]{0:T(1024)S(1)}, f32[1152]{0:T(1024)}, u32[]{:S(2)}) copy-start(f32[1152]{0:T(1024)} %get-tuple-element.34) | copy-start | bytes 13828
  695.1 338.6 %all-gather.23.cloned.1.call-start = ((), (), s32[]{:S(2)}) async-start(), calls=%async_computation.20 | async-start | bytes 8847360 | tf_op jit(solution)/shard_map/all_gather | solution.py:33
  956.9 304.9 %reduce-scatter.19.cloned.1.call-start = ((), (), s32[]{:S(2)}) async-start(), calls=%async_computation.21 | async-start | bytes 17694720 | tf_op jit(solution)/shard_map/reduce_scatter | solution.py:41
  1045.0 25.6 %slice-start = ((s8[12582912]{0:T(1024)(128)(4,1)}), s8[4194304]{0:T(1024)(128)(4,1)S(1)}, s32[]{:S(2)}) async-start(s8[12582912]{0:T(1024)(128)(4,1)} %bitcast.161), calls=%async_computation.29 | async-start | bytes 8388608
  1045.0 25.6 %slice-start.1 = ((s8[12582912]{0:T(1024)(128)(4,1)}), s8[4194304]{0:T(1024)(128)(4,1)S(1)}, s32[]{:S(2)}) async-start(s8[12582912]{0:T(1024)(128)(4,1)} %bitcast.161), calls=%async_computation.30 | async-start | bytes 8388608
  1128.0 136.2 %copy-start.30 = (f32[768]{0:T(1024)S(1)}, f32[768]{0:T(1024)}, u32[]{:S(2)}) copy-start(f32[768]{0:T(1024)} %copy-done.29) | copy-start | bytes 9220
  1128.0 136.2 %copy-start.32 = (f32[768]{0:T(1024)S(1)}, f32[768]{0:T(1024)}, u32[]{:S(2)}) copy-start(f32[768]{0:T(1024)} %copy-done.31) | copy-start | bytes 9220
  1128.0 225.3 %reduce-scatter.31.cloned.1.call-start = ((), (), s32[]{:S(2)}) async-start(), calls=%async_computation.27 | async-start | bytes 368640
  1285.3 79.0 %reduce-scatter.29.cloned.1.call-start = ((), (), s32[]{:S(2)}) async-start(), calls=%async_computation.26 | async-start | bytes 2985984 | tf_op jit(solution)/shard_map/reduce_scatter | solution.py:261
  1302.9 85.8 %reduce-scatter.27.cloned.1.call-start = ((), (), s32[]{:S(2)}) async-start(), calls=%async_computation.25 | async-start | bytes 2985984 | tf_op jit(solution)/shard_map/reduce_scatter | solution.py:255
  1317.6 104.6 %reduce-scatter.25.cloned.1.call-start = ((), (), s32[]{:S(2)}) async-start(), calls=%async_computation.24 | async-start | bytes 995328 | tf_op jit(solution)/shard_map/reduce_scatter | solution.py:258
  1324.9 17.3 %copy-start.40 = (f32[4,72]{1,0:T(4,128)S(1)}, f32[4,72]{1,0:T(4,128)}, u32[]{:S(2)}) copy-start(f32[4,72]{1,0:T(4,128)} %get-tuple-element.56) | copy-start | bytes 3460
  1324.9 135.6 %reduce-scatter.23.cloned.1.call-start = ((), (), s32[]{:S(2)}) async-start(), calls=%async_computation.23 | async-start | bytes 2985984 | tf_op jit(solution)/shard_map/reduce_scatter | solution.py:252
  1325.0 20.5 %copy-start.10 = (bf16[768,1152]{1,0:T(8,128)(2,1)S(1)}, bf16[768,1152]{1,0:T(8,128)(2,1)}, u32[]{:S(2)}) copy-start(bf16[768,1152]{1,0:T(8,128)(2,1)} %param.27) | copy-start | bytes 5308420
  1339.4 253.3 %all-reduce.6.cloned.1.call-start = ((), (), s32[]{:S(2)}) async-start(), calls=%async_computation.28 | async-start | bytes 313344 | tf_op jit(solution)/shard_map/psum | solution.py:265
  1360.2 296.9 %reduce-scatter.21.cloned.1.call-start = ((), (), s32[]{:S(2)}) async-start(), calls=%async_computation.22 | async-start | bytes 5971968 | tf_op jit(solution)/shard_map/reduce_scatter | solution.py:249
  (38 other events, 193.3 us)
Sparse Core Ops, SparseCore 0:
  9.6 59.2 all-gather.8
  70.5 32.9 all-gather.12
  139.8 74.5 all-gather.10
  273.0 133.7 reduce-scatter.12
  408.3 34.1 all-gather.18
  444.8 75.6 all-gather.20
  522.1 34.1 all-gather.16
  558.8 75.6 all-gather.14
  675.6 133.5 reduce-scatter.16
  812.3 133.6 reduce-scatter.14
  957.0 76.6 all-gather.22
  1128.1 133.5 reduce-scatter.18
  1285.4 24.2 reduce-scatter.30
  1311.8 37.8 reduce-scatter.28
  1351.9 36.7 reduce-scatter.26
  1391.4 30.7 reduce-scatter.24
  1424.5 36.0 reduce-scatter.22
  1469.1 123.5 all-reduce.5
  1595.1 61.9 reduce-scatter.20
where the time goes:
time: 1680 us; the launch traced here: 1670 us
  waiting for transfers between devices  1160 us (69%)
  matrix products  235 us (14%)
  local copies, waits for them, and re-layouts  101 us (6%)
  blocking collectives  77.6 us (5%)
  other arithmetic  75.2 us (4%)
    reduce_scatter x2, waiting for transfers between devices, sum_in(): lax.psum_scatter(partial_sum, 'narrow', scatter_dimension=0, tiled=True)  248 us
    reduce_scatter x2, waiting for transfers between devices, sum_out(): lax.psum_scatter(partial_sum, 'narrow', scatter_dimension=0, tiled=True)  248 us
    all_gather x2, waiting for transfers between devices, gather_grads(): return lax.all_gather(piece, 'narrow', axis=0, tiled=True)  155 us
    all_gather x2, waiting for transfers between devices, gather_rows(): return lax.all_gather(piece, 'narrow', axis=0, tiled=True)  136 us
    psum x1, waiting for transfers between devices, shards(): lax.psum((condition_part, into_place(mod_bias_part, position), into_place...  124 us
    reduce_scatter x1, waiting for transfers between devices, shards(): lax.psum_scatter(mod_part.astype(jnp.bfloat16), 'wide', scatter_dimension...  57.6 us
    all_gather x1, waiting for transfers between devices, shards(): lax.all_gather(mod_weight, 'wide', axis=0, tiled=True)  56.6 us
    all_gather x1, blocking collectives, shards(): lax.all_gather(mode_slice, 'narrow', axis=2, tiled=True)  45.5 us
  transfers between devices with their start and end apart: 19, of which 16 were waited for; matrix products, arithmetic and copies ran while one was open for 10% of the time, Pallas kernels for 0%

commit v1 on v0

v1 whole, which is shorter than its diff:
```python
import functools
import math

import jax
import jax.numpy as jnp
from jax import lax
from jax.experimental import pallas as pl
from jax.experimental.pallas import tpu as pltpu
from jax.sharding import PartitionSpec as P

HEAD = 72
PATCHES = 256
EPSILON = 1e-06
MIB = 1 << 20
F32 = jnp.float32
BF16 = jnp.bfloat16


def bits_of(size):
    return [1 << k for k in range(size.bit_length() - 1)]


def swap(block, axis, bit):
    count = lax.axis_size(axis)
    return lax.ppermute(block, axis, [(i, i ^ bit) for i in range(count)])


def my_bit(axis, bit):
    return (lax.axis_index(axis) // bit) % 2


def normalize(values):
    center = jnp.mean(values, axis=-1, keepdims=True)
    spread = jnp.mean(values * values, axis=-1, keepdims=True) - center * center
    inverse = lax.rsqrt(spread + EPSILON)
    return inverse, (values - center) * inverse


def norm_back(incoming, normed, inverse):
    first = jnp.mean(incoming, axis=-1, keepdims=True)
    second = jnp.mean(incoming * normed, axis=-1, keepdims=True)
    return inverse * (incoming - first - normed * second)


def gelu_both(upper):
    c0 = math.sqrt(2.0 / math.pi)
    square = upper * upper
    inner = c0 * upper * (1.0 + 0.044715 * square)
    tanh = jnp.tanh(inner)
    half = 0.5 * (1.0 + tanh)
    slope = half + 0.5 * upper * (1.0 - tanh * tanh) * (c0 * (1.0 + 0.134145 * square))
    return upper * half, slope


def dot(a, b, ca, cb):
    return lax.dot_general(a, b, (((ca,), (cb,)), ((), ())), preferred_element_type=F32)


def attend_kernel(heads, qkv_ref, out_ref):
    part = heads * HEAD
    scale = HEAD ** (-0.5)
    results = []
    for h in range(heads):
        q = qkv_ref[0, :, h * HEAD : (h + 1) * HEAD]
        k = qkv_ref[0, :, part + h * HEAD : part + (h + 1) * HEAD]
        v = qkv_ref[0, :, 2 * part + h * HEAD : 2 * part + (h + 1) * HEAD]
        s = dot(q, k, 1, 1)
        top = jnp.max(s, axis=1, keepdims=True)
        p = jnp.exp((s - top) * scale)
        total = jnp.sum(p, axis=1, keepdims=True)
        results.append(dot(p.astype(BF16), v, 1, 0) / total)
    out_ref[0] = jnp.concatenate(results, axis=1).astype(BF16)


def attend(qkv, heads):
    groups, rows, cols = qkv.shape
    part = heads * HEAD
    return pl.pallas_call(
        functools.partial(attend_kernel, heads),
        grid=(groups, rows // PATCHES),
        in_specs=[pl.BlockSpec((1, PATCHES, cols), lambda n, f: (n, f, 0))],
        out_specs=pl.BlockSpec((1, PATCHES, part), lambda n, f: (n, f, 0)),
        out_shape=jax.ShapeDtypeStruct((groups, rows, part), BF16),
        compiler_params=pltpu.CompilerParams(vmem_limit_bytes=32 * MIB),
        cost_estimate=pl.CostEstimate(
            flops=groups * rows * heads * PATCHES * 128 * 4,
            bytes_accessed=2 * groups * rows * (cols + part),
            transcendentals=groups * rows * heads * PATCHES,
        ),
        name="attend",
    )(qkv)


def attend_back_kernel(heads, qkv_ref, grad_ref, out_ref):
    part = heads * HEAD
    scale = HEAD ** (-0.5)
    dqs, dks, dvs = [], [], []
    for h in range(heads):
        q = qkv_ref[0, :, h * HEAD : (h + 1) * HEAD]
        k = qkv_ref[0, :, part + h * HEAD : part + (h + 1) * HEAD]
        v = qkv_ref[0, :, 2 * part + h * HEAD : 2 * part + (h + 1) * HEAD]
        g = grad_ref[0, :, h * HEAD : (h + 1) * HEAD]
        s = dot(q, k, 1, 1)
        top = jnp.max(s, axis=1, keepdims=True)
        p = jnp.exp((s - top) * scale)
        total = jnp.sum(p, axis=1, keepdims=True)
        p = p * (1.0 / total)
        dvs.append(dot(p.astype(BF16), g, 0, 0))
        dp = dot(g, v, 1, 1)
        mixed = p * dp
        ds = (mixed - p * jnp.sum(mixed, axis=1, keepdims=True)).astype(BF16)
        dqs.append(dot(ds, k, 1, 0) * scale)
        dks.append(dot(ds, q, 0, 0) * scale)
    out_ref[0] = jnp.concatenate(dqs + dks + dvs, axis=1).astype(BF16)


def attend_back(qkv, grad, heads):
    groups, rows, cols = qkv.shape
    part = heads * HEAD
    return pl.pallas_call(
        functools.partial(attend_back_kernel, heads),
        grid=(groups, rows // PATCHES),
        in_specs=[
            pl.BlockSpec((1, PATCHES, cols), lambda n, f: (n, f, 0)),
            pl.BlockSpec((1, PATCHES, part), lambda n, f: (n, f, 0)),
        ],
        out_specs=pl.BlockSpec((1, PATCHES, cols), lambda n, f: (n, f, 0)),
        out_shape=jax.ShapeDtypeStruct((groups, rows, cols), BF16),
        compiler_params=pltpu.CompilerParams(vmem_limit_bytes=32 * MIB),
        cost_estimate=pl.CostEstimate(
            flops=groups * rows * heads * PATCHES * 128 * 10,
            bytes_accessed=2 * groups * rows * (2 * cols + part),
            transcendentals=groups * rows * heads * PATCHES,
        ),
        name="attend_back",
    )(qkv, grad)


def widen(block, axis, bit, dim):
    other = swap(block, axis, bit)
    upper = my_bit(axis, bit) == 1
    return jnp.concatenate(
        [jnp.where(upper, other, block), jnp.where(upper, block, other)], axis=dim
    )


def dims_of():
    return [("narrow", bit) for bit in reversed(bits_of(lax.axis_size("narrow")))] + [
        ("wide", bit) for bit in reversed(bits_of(lax.axis_size("wide")))
    ]


def gather_chunk(shard):
    rows, cols = shard.shape
    dims = dims_of()
    place = {key: i for i, key in enumerate(dims)}
    cut = max(16, rows // 2 // 16 * 16)
    narrow = [key for key in dims if key[0] == "narrow"]
    wide = [key for key in dims if key[0] == "wide"]
    block = shard.reshape([1] * len(dims) + [rows, cols])
    for key in wide[:-1]:
        block = widen(block, *key, place[key])
    first, second = block[..., :cut, :], block[..., cut:, :]
    for key, other in zip(narrow, reversed(narrow)):
        first = widen(first, *key, place[key])
        second = widen(second, *other, place[other])
    first = widen(first, *wide[-1], place[wide[-1]])
    second = widen(second, *wide[-1], place[wide[-1]])
    whole = jnp.concatenate([first, second], axis=-2)
    narrow_count, wide_count = lax.axis_size("narrow"), lax.axis_size("wide")
    return whole.reshape(narrow_count, wide_count * rows, cols)


def halve(block, axis, bit, dim):
    mine = my_bit(axis, bit)
    kept = lax.dynamic_slice_in_dim(block, mine, 1, dim)
    sent = lax.dynamic_slice_in_dim(block, 1 - mine, 1, dim)
    return (kept.astype(F32) + swap(sent, axis, bit).astype(F32)).astype(block.dtype)


def scatter_chunk(grad):
    narrow_count, wide_count = lax.axis_size("narrow"), lax.axis_size("wide")
    rows, cols = grad.shape[1] // wide_count, grad.shape[2]
    dims = dims_of()
    place = {key: i for i, key in enumerate(dims)}
    cut = max(16, rows // 2 // 16 * 16)
    narrow = [key for key in dims if key[0] == "narrow"]
    wide = [key for key in dims if key[0] == "wide"]
    block = grad.reshape([2] * len(dims) + [rows, cols])
    block = halve(block, *wide[-1], place[wide[-1]])
    first, second = block[..., :cut, :], block[..., cut:, :]
    for key, other in zip(narrow, reversed(narrow)):
        first = halve(first, *key, place[key])
        second = halve(second, *other, place[other])
    block = jnp.concatenate([first, second], axis=-2)
    for key in reversed(wide[:-1]):
        block = halve(block, *key, place[key])
    return block.reshape(rows, cols).astype(F32)


def sum_over(block, axis):
    for bit in bits_of(lax.axis_size(axis)):
        block = block + swap(block, axis, bit)
    return block


def collect(block, axis):
    block = block[None]
    for bit in bits_of(lax.axis_size(axis)):
        block = widen(block, axis, bit, 0)
    return block


def share(block, count):
    for bit in bits_of(count):
        groups, rows, cols = block.shape
        pair = block.reshape(2, groups // 2, rows, cols)
        mine = my_bit("narrow", bit)
        kept = lax.dynamic_index_in_dim(pair, mine, 0, False)
        got = swap(lax.dynamic_index_in_dim(pair, 1 - mine, 0, False), "narrow", bit)
        block = jnp.concatenate(
            [jnp.where(mine == 1, got, kept), jnp.where(mine == 1, kept, got)], axis=1
        )
    return block


def unshare(block, count):
    for bit in reversed(bits_of(count)):
        groups, rows, cols = block.shape
        pair = block.reshape(groups, 2, rows // 2, cols)
        mine = my_bit("narrow", bit)
        kept = lax.dynamic_index_in_dim(pair, mine, 1, False)
        got = swap(lax.dynamic_index_in_dim(pair, 1 - mine, 1, False), "narrow", bit)
        block = jnp.concatenate(
            [jnp.where(mine == 1, got, kept), jnp.where(mine == 1, kept, got)], axis=0
        )
    return block


def shards(
    tokens,
    condition,
    frame_clip,
    mod_weight,
    mod_bias,
    project_weight,
    project_bias,
    merge_weight,
    merge_bias,
    up_weight,
    up_bias,
    down_weight,
    down_bias,
    out_cotangent,
):
    rows, width = tokens.shape
    wide_count, narrow_count = lax.axis_size("wide"), lax.axis_size("narrow")
    wide_me, narrow_me = lax.axis_index("wide"), lax.axis_index("narrow")
    depth = width // wide_count
    part = width // narrow_count
    units = up_weight.shape[1]
    heads = part // HEAD
    clips = condition.shape[0]
    span = math.gcd(rows, PATCHES)
    spans = rows // span
    sharing = PATCHES // span

    attn_shard = jnp.concatenate(
        [project_weight.reshape(depth, 3 * part), merge_weight.T], axis=1
    )
    attn_w = gather_chunk(attn_shard)
    up_w = gather_chunk(up_weight)
    down_w = gather_chunk(down_weight.T)
    project_w = attn_w[:, :, : 3 * part]
    merge_w = attn_w[:, :, 3 * part :]

    active = jax.nn.silu(condition).astype(BF16)
    active_mine = lax.dynamic_slice_in_dim(active, wide_me * depth, depth, 1)
    mode_part = jnp.einsum("cd,dki->cki", active_mine, mod_weight, preferred_element_type=F32)
    mode_part = sum_over(mode_part, "wide") + mod_bias.astype(F32)[None]
    unit_rows = units // part
    small = jnp.concatenate(
        [
            mode_part.reshape(clips * 6, part),
            project_bias.astype(F32),
            merge_bias.astype(F32)[None],
            down_bias.astype(F32)[None],
            up_bias.astype(F32).reshape(unit_rows, part),
        ],
        axis=0,
    )
    small = collect(small, "narrow")
    modes = small[:, : clips * 6].reshape(narrow_count, clips, 6, part)
    at = clips * 6
    bias_q = small[:, at]
    bias_v = small[:, at + 1]
    merge_bias_full = small[:, at + 2].reshape(width)
    down_bias_full = small[:, at + 3].reshape(width)
    up_bias_full = small[:, at + 4 :].reshape(narrow_count, units)

    span_frame = (narrow_me * rows + jnp.arange(spans, dtype=jnp.int32) * span) // PATCHES
    span_clip = jnp.sum(
        jnp.where(
            span_frame[:, None] == jnp.arange(frame_clip.shape[0], dtype=jnp.int32)[None],
            frame_clip[None],
            0,
        ),
        axis=1,
    )
    span_modes = jnp.concatenate(
        [lax.dynamic_slice_in_dim(modes, span_clip[s], 1, 1) for s in range(spans)], axis=1
    )
    span_modes = span_modes.transpose(1, 2, 0, 3).reshape(spans, 6, 1, width)
    shift_a, scale_a, gate_a, shift_b, scale_b, gate_b = [span_modes[:, i] for i in range(6)]

    inputs = tokens.astype(F32).reshape(spans, span, width)
    inverse_a, normed_a = normalize(inputs)
    hidden_a = (normed_a * (1.0 + scale_a) + shift_a).astype(BF16).reshape(rows, width)
    qkv_bias = jnp.concatenate([bias_q, jnp.zeros_like(bias_q), bias_v], axis=1)
    qkv = jnp.einsum("td,ndc->ntc", hidden_a, project_w, preferred_element_type=F32)
    qkv = (qkv + qkv_bias[:, None]).astype(BF16)
    qkv_frames = share(qkv, sharing)
    attended = unshare(attend(qkv_frames, heads), sharing)
    merged = jnp.einsum("nti,ndi->td", attended, merge_w, preferred_element_type=F32)
    branch_a = (merged + merge_bias_full).reshape(spans, span, width)
    middle = inputs + gate_a * branch_a
    inverse_b, normed_b = normalize(middle)
    hidden_b = (normed_b * (1.0 + scale_b) + shift_b).astype(BF16).reshape(rows, width)
    upper = jnp.einsum("td,ndf->ntf", hidden_b, up_w, preferred_element_type=F32)
    gelu_out, slope = gelu_both(upper + up_bias_full[:, None])
    gelu_out, slope = gelu_out.astype(BF16), slope.astype(BF16)
    core = jnp.einsum("ntf,ndf->td", gelu_out, down_w, preferred_element_type=F32)
    branch_b = (core + down_bias_full).reshape(spans, span, width)
    output = (middle + gate_b * branch_b).astype(BF16).reshape(rows, width)

    grad_out = out_cotangent.astype(F32).reshape(spans, span, width)
    gated_out = gate_b * grad_out
    down_bias_grad = jnp.sum(gated_out, axis=(0, 1))
    core_grad = gated_out.astype(BF16).reshape(rows, width)
    down_part = jnp.einsum("td,ntf->ndf", core_grad, gelu_out, preferred_element_type=F32)
    down_grad = scatter_chunk(down_part.astype(BF16))
    gelu_grad = jnp.einsum("td,ndf->ntf", core_grad, down_w, preferred_element_type=F32)
    upper_grad = (gelu_grad * slope.astype(F32)).astype(BF16)
    up_bias_grad = jnp.sum(upper_grad.astype(F32), axis=1)
    up_part = jnp.einsum("td,ntf->ndf", hidden_b, upper_grad, preferred_element_type=F32)
    up_grad = scatter_chunk(up_part.astype(BF16))
    hidden_b_grad = jnp.einsum("ntf,ndf->td", upper_grad, up_w, preferred_element_type=F32)
    hidden_b_grad = hidden_b_grad.reshape(spans, span, width)
    middle_grad = grad_out + norm_back(hidden_b_grad * (1.0 + scale_b), normed_b, inverse_b)

    gated_middle = gate_a * middle_grad
    merge_bias_grad = jnp.sum(gated_middle, axis=(0, 1))
    merged_grad = gated_middle.astype(BF16).reshape(rows, width)
    attended_grad = jnp.einsum("td,ndi->nti", merged_grad, merge_w, preferred_element_type=F32)
    attended_grad = share(attended_grad.astype(BF16), sharing)
    merge_part = jnp.einsum("td,nti->ndi", merged_grad, attended, preferred_element_type=F32)
    qkv_grad = unshare(attend_back(qkv_frames, attended_grad, heads), sharing)
    qkv_sums = jnp.sum(qkv_grad.astype(F32), axis=1)
    project_part = jnp.einsum("td,ntc->ndc", hidden_a, qkv_grad, preferred_element_type=F32)
    attn_part = jnp.concatenate([project_part.astype(BF16), merge_part.astype(BF16)], axis=2)
    attn_grad = scatter_chunk(attn_part)
    hidden_a_grad = jnp.einsum("ntc,ndc->td", qkv_grad, project_w, preferred_element_type=F32)
    hidden_a_grad = hidden_a_grad.reshape(spans, span, width)
    tokens_grad = middle_grad + norm_back(hidden_a_grad * (1.0 + scale_a), normed_a, inverse_a)

    span_grad = jnp.stack(
        [
            jnp.sum(hidden_a_grad, axis=1),
            jnp.sum(hidden_a_grad * normed_a, axis=1),
            jnp.sum(middle_grad * branch_a, axis=1),
            jnp.sum(hidden_b_grad, axis=1),
            jnp.sum(hidden_b_grad * normed_b, axis=1),
            jnp.sum(grad_out * branch_b, axis=1),
        ],
        axis=1,
    )
    hits = span_clip[None, :] == jnp.arange(clips, dtype=jnp.int32)[:, None]
    clip_grad = jnp.sum(jnp.where(hits[:, :, None, None], span_grad[None], 0.0), axis=1)
    clip_grad = clip_grad.reshape(clips * 6, narrow_count, part).transpose(1, 0, 2)
    packed = jnp.concatenate(
        [
            clip_grad,
            qkv_sums[:, None, :part],
            qkv_sums[:, None, 2 * part :],
            merge_bias_grad.reshape(narrow_count, 1, part),
            down_bias_grad.reshape(narrow_count, 1, part),
            up_bias_grad.reshape(narrow_count, unit_rows, part),
        ],
        axis=1,
    )
    depth_rows = packed.shape[1]
    packed = packed.reshape([2] * len(bits_of(narrow_count)) + [depth_rows, part])
    for place, bit in enumerate(reversed(bits_of(narrow_count))):
        packed = halve(packed, "narrow", bit, place)
    packed = sum_over(packed.reshape(depth_rows, part), "wide")
    clip_slice = packed[: clips * 6].reshape(clips, 6, part)
    mod_bias_grad = jnp.sum(clip_slice, axis=0)
    mod_weight_grad = jnp.einsum(
        "cd,cki->dki", active_mine.astype(F32), clip_slice, precision=lax.Precision.HIGHEST
    )
    active_grad = jnp.einsum(
        "cki,dki->cd", clip_slice, mod_weight.astype(F32), precision=lax.Precision.HIGHEST
    )
    active_grad = collect(sum_over(active_grad, "narrow"), "wide")
    active_grad = active_grad.transpose(1, 0, 2).reshape(clips, width)
    unused, silu_pullback = jax.vjp(jax.nn.silu, condition)
    condition_grad = silu_pullback(active_grad)[0]

    return (
        output,
        tokens_grad.reshape(rows, width),
        condition_grad,
        mod_weight_grad,
        mod_bias_grad,
        attn_grad[:, : 3 * part].reshape(depth, 3, part),
        packed[at : at + 2],
        attn_grad[:, 3 * part :].T,
        packed[at + 2],
        up_grad,
        packed[at + 4 :].reshape(units),
        down_grad.T,
        packed[at + 3],
    )


def solution(mesh):
    both = P(("wide", "narrow"), None)
    ins = (
        both,
        P(),
        P("wide"),
        P("wide", None, "narrow"),
        P(None, "narrow"),
        P("wide", None, "narrow"),
        P(None, "narrow"),
        P("narrow", "wide"),
        P("narrow"),
        P("wide", "narrow"),
        P("narrow"),
        P("narrow", "wide"),
        P("narrow"),
        both,
    )
    outs = (
        both,
        both,
        P(),
        P("wide", None, "narrow"),
        P(None, "narrow"),
        P("wide", None, "narrow"),
        P(None, "narrow"),
        P("narrow", "wide"),
        P("narrow"),
        P("wide", "narrow"),
        P("narrow"),
        P("narrow", "wide"),
        P("narrow"),
    )
    return jax.shard_map(shards, mesh=mesh, in_specs=ins, out_specs=outs, check_vma=False)
```

time: 1680 us -> 852 us (0.51)
  waiting for transfers between devices: 1160 us -> 354 us
  matrix products: 235 us -> 150 us
  blocking collectives: 77.6 us -> 0 us
  starting transfers between devices: 0.77 us -> 63.9 us
  other arithmetic: 75.2 us -> 132 us
  Pallas kernels: 0 us -> 56.1 us
  local copies, waits for them, and re-layouts: 101 us -> 77.4 us
    reduce_scatter x9 -> x0, waiting for transfers between devices: 644 us -> none  [the longest x2 248 us: sum_in(): lax.psum_scatter(partial_sum, 'narrow', scatter_dimension=0, tiled=True)]
    all_gather x8 -> x0, waiting for transfers between devices: 390 us -> none  [the longest x2 155 us: gather_grads(): return lax.all_gather(piece, 'narrow', axis=0, tiled=True)]
    ppermute x0 -> x60, waiting for transfers between devices: none -> 354 us  [swap(): return lax.ppermute(block, axis, [(i, i ^ bit) for i in range(count)])]
    psum x1 -> x0, waiting for transfers between devices: 124 us -> none  [shards(): lax.psum((condition_part, into_place(mod_bias_part, position), into_place...]
    dot_general x23 -> x15, matrix products: 235 us -> 150 us  [the longest x1 23.5 us: shards(): jnp.einsum('td,ndf->ntf', core_grad, down_w, preferred_element_type=F32)]
    ppermute x0 -> x60, starting transfers between devices: none -> 63.9 us  [swap(): return lax.ppermute(block, axis, [(i, i ^ bit) for i in range(count)])]
    all_gather x2 -> x0, blocking collectives: 61.6 us -> none  [the longest x1 45.5 us: shards(): lax.all_gather(mode_slice, 'narrow', axis=2, tiled=True)]
    pallas_call x0 -> x2, Pallas kernels: none -> 56.1 us  [the longest x1 35.9 us: attend_back(): pl.pallas_call(functools.partial(attend_back_kernel, heads), grid=(groups...]
  transfers between devices with their start and end apart: 19 -> 60, of which waited for: 16 -> 34; matrix products, arithmetic and copies ran while one was open for 10% -> 25% of each run, Pallas kernels for 0% -> 2%
where the time goes in v1:
time: 852 us; the launch traced here: 842 us
  waiting for transfers between devices  354 us (42%)
  matrix products  150 us (18%)
  other arithmetic  132 us (15%)
  local copies, waits for them, and re-layouts  77.4 us (9%)
  starting transfers between devices  63.9 us (8%)
  Pallas kernels  56.1 us (7%)
    ppermute x60, waiting for transfers between devices, swap(): return lax.ppermute(block, axis, [(i, i ^ bit) for i in range(count)])  354 us
    ppermute x60, starting transfers between devices, swap(): return lax.ppermute(block, axis, [(i, i ^ bit) for i in range(count)])  63.9 us
    pallas_call x1, Pallas kernels, attend_back(): pl.pallas_call(functools.partial(attend_back_kernel, heads), grid=(groups...  35.9 us
    select_n x27, other arithmetic, widen(): jnp.where(upper, other, block)  25.5 us
    convert_element_type x18, other arithmetic, halve(): (kept.astype(F32) + swap(sent, axis, bit).astype(F32)).astype(block.dtype)  25.1 us
    unnamed x153, local copies, waits for them, and re-layouts  24.3 us
    dot_general x1, matrix products, shards(): jnp.einsum('td,ndf->ntf', core_grad, down_w, preferred_element_type=F32)  23.5 us
    pallas_call x1, Pallas kernels, attend(): pl.pallas_call(functools.partial(attend_kernel, heads), grid=(groups, row...  20.2 us
  transfers between devices with their start and end apart: 60, of which 34 were waited for; matrix products, arithmetic and copies ran while one was open for 25% of the time, Pallas kernels for 2%

profile of v1, /device:TPU:0, one launch (start us, length us, event | category | flops | bytes accessed | tf_op | source)
XLA Modules:
  0.0 842.0 jit_solution(13448289532597643016)
XLA Ops:
  18.3 14.5 %collective-permute-done.1 = f32[12,6,288]{2,0,1:T(8,128)} collective-permute-done((f32[12,6,288]{2,0,1:T(8,128)S(1)}, f32[12,6,288]{2,0,1:T(8,128)}, u32[]{:S(2)}, u32[]{:S(2)}) %collective-permute-start.1) | collective-permute-done | bytes 82976 | tf_op jit(solution)/shard_map/ppermute | solution.py:25
  45.3 12.8 %collective-permute-done.2 = f32[12,6,288]{2,0,1:T(8,128)} collective-permute-done((f32[12,6,288]{2,0,1:T(8,128)S(1)}, f32[12,6,288]{2,0,1:T(8,128)}, u32[]{:S(2)}, u32[]{:S(2)}) %collective-permute-start.2) | collective-permute-done | bytes 82976 | tf_op jit(solution)/shard_map/ppermute | solution.py:25
  111.0 10.7 %collective-permute-done.15 = bf16[1,1,2,2,1,64,1152]{6,5,4,3,2,1,0:T(8,128)(2,1)S(1)} collective-permute-done((bf16[1,1,2,2,1,64,1152]{6,5,4,3,2,1,0:T(8,128)(2,1)S(1)}, bf16[1,1,2,2,1,64,1152]{6,5,4,3,2,1,0:T(8,128)(2,1)S(1)}, u32[]{:S(2)}, u32[]{:S(2)}) %collective-permute-start.15) | collective-permute-done | bytes 589856 | tf_op jit(solution)/shard_map/ppermute | solution.py:25
  122.7 8.0 collective-permute-done.23
  135.7 13.5 %collective-permute-done.26 = bf16[1,1,2,2,1,80,1152]{6,5,4,3,2,1,0:T(8,128)(2,1)S(1)} collective-permute-done((bf16[1,1,2,2,1,80,1152]{6,5,4,3,2,1,0:T(8,128)(2,1)S(1)}, bf16[1,1,2,2,1,80,1152]{6,5,4,3,2,1,0:T(8,128)(2,1)S(1)}, u32[]{:S(2)}, u32[]{:S(2)}) %collective-permute-start.26) | collective-permute-done | bytes 737312 | tf_op jit(solution)/shard_map/ppermute | solution.py:25
  150.1 24.3 %collective-permute-done.8 = bf16[2,1,2,2,1,64,1152]{6,5,4,3,2,1,0:T(8,128)(2,1)S(1)} collective-permute-done((bf16[2,1,2,2,1,64,1152]{6,5,4,3,2,1,0:T(8,128)(2,1)S(1)}, bf16[2,1,2,2,1,64,1152]{6,5,4,3,2,1,0:T(8,128)(2,1)S(1)}, u32[]{:S(2)}, u32[]{:S(2)}) %collective-permute-start.8) | collective-permute-done | bytes 1179680 | tf_op jit(solution)/shard_map/ppermute | solution.py:25
  175.0 24.8 %collective-permute-done.16 = bf16[2,1,2,2,1,64,1152]{6,5,4,3,2,1,0:T(8,128)(2,1)S(1)} collective-permute-done((bf16[2,1,2,2,1,64,1152]{6,5,4,3,2,1,0:T(8,128)(2,1)S(1)}, bf16[2,1,2,2,1,64,1152]{6,5,4,3,2,1,0:T(8,128)(2,1)S(1)}, u32[]{:S(2)}, u32[]{:S(2)}) %collective-permute-start.16) | collective-permute-done | bytes 1179680 | tf_op jit(solution)/shard_map/ppermute | solution.py:25
  200.8 18.5 %collective-permute-done.24 = bf16[2,1,2,2,1,64,1152]{6,5,4,3,2,1,0:T(8,128)(2,1)S(1)} collective-permute-done((bf16[2,1,2,2,1,64,1152]{6,5,4,3,2,1,0:T(8,128)(2,1)S(1)}, bf16[2,1,2,2,1,64,1152]{6,5,4,3,2,1,0:T(8,128)(2,1)S(1)}, u32[]{:S(2)}, u32[]{:S(2)}) %collective-permute-start.24) | collective-permute-done | bytes 1179680 | tf_op jit(solution)/shard_map/ppermute | solution.py:25
  249.3 20.2 %attend.1 = bf16[4,768,288]{2,1,0:T(8,128)(2,1)S(1)} custom-call(bf16[4,768,864]{2,1,0:T(8,128)(2,1)S(1)} %fusion.14.qkv_ref), custom_call_target="tpu_custom_call" | custom-call | flops 1610612736 | bytes 7077888 | tf_op jit(solution)/shard_map/attend/pallas_call | solution.py:78
  284.0 11.9 %fusion.36 = f32[4,1152,768]{1,2,0:T(8,128)} fusion(bf16[4,1152,1152]{2,1,0:T(8,128)(2,1)S(1)} %bitcast.266, bf16[768,1152]{1,0:T(8,128)(2,1)S(1)} %fusion.21), kind=kOutput, calls=%fused_computation.108 | convolution fusion | flops 8153726976 | bytes 26542080 | tf_op jit(solution)/shard_map/td,ndf->ntf/dot_general | solution.py:329
  295.9 15.3 %convolution_convert_fusion = bf16[4,1152,1152]{1,2,0:T(8,128)(2,1)} fusion(bf16[768,1152]{1,0:T(8,128)(2,1)} %get-tuple-element.116, f32[4,1152,768]{1,2,0:T(8,128)} %fusion.36, f32[4,1152]{1,0:T(4,128)S(1)} %copy-done.47), kind=kOutput, calls=%fused_computation | convolution fusion | flops 8194424832 | bytes 26560512 | tf_op jit(solution)/shard_map/td,ntf->ndf/dot_general | solution.py:340
  319.5 23.5 %fusion.1 = (bf16[768,1152,4]{1,0,2:T(8,128)(2,1)}, f32[4,1152,768]{1,2,0:T(8,128)}) fusion(f32[4,1152,768]{1,2,0:T(8,128)} %fusion.36, f32[1152,4]{0,1:T(4,128)S(1)} %bitcast.283, bf16[4,1152,1152]{2,1,0:T(8,128)(2,1)} %bitcast.268, bf16[768,1152]{1,0:T(8,128)(2,1)} %get-tuple-element.116), kind=kOutput, calls=%fused_computation.6 | convolution fusion | flops 8228044800 | bytes 47794176 | tf_op jit(solution)/shard_map/td,ndf->ntf/dot_general | solution.py:342
  343.1 18.7 %multiply_reduce_fusion.1 = (f32[3,1152]{1,0:T(4,128)S(1)}, f32[3,256]{1,0:T(4,128)S(1)}, f32[3,256]{1,0:T(4,128)S(1)}, f32[3,1152]{1,0:T(4,128)S(1)}, f32[3,256...) fusion(f32[3,1152]{1,0:T(4,128)S(1)} %copy-done.44, f32[3,256]{1,0:T(4,128)S(1)} %add_rsqrt_fusion.1, ...), kind=kOutput, calls=%fused_computation.57 | convolution fusion | flops 8164335104 | bytes 33687552 | tf_op jit(solution)/shard_map/ntf,ndf->td/dot_general | solution.py:347
  361.8 18.3 %fusion.15 = f32[768,1152]{1,0:T(8,128)} fusion(bf16[4,1152,1152]{2,1,0:T(8,128)(2,1)} %bitcast.269, f32[1152]{0:T(1024)S(1)} %copy-done.60, f32[4,1152,768]{1,2,0:T(8,128)} %fusion.36, f32[4,1152]{1,0:T(4,128)S(1)} %copy-done.47), kind=kOutput, calls=%fused_computation.43 | convolution fusion | flops 8190001152 | bytes 28334592 | tf_op jit(solution)/shard_map/ntf,ndf->td/dot_general | solution.py:332
  404.1 35.9 %attend_back.1 = bf16[4,768,864]{2,1,0:T(8,128)(2,1)S(1)} custom-call(bf16[4,768,864]{2,1,0:T(8,128)(2,1)S(1)} %copy-done.3, bf16[4,768,288]{2,1,0:T(8,128)(2,1)S(1)} %bitcast.246), custom_call_target="tpu_custom_call" | custom-call | flops 4026531840 | bytes 12386304 | tf_op jit(solution)/shard_map/attend_back/pallas_call | solution.py:120
  442.5 9.5 %fusion.9 = bf16[4,1152,864]{1,2,0:T(8,128)(2,1)} fusion(bf16[4,768,864]{2,1,0:T(8,128)(2,1)S(1)} %attend_back.1, bf16[768,1152]{1,0:T(8,128)(2,1)S(1)} %copy-done.36), kind=kOutput, calls=%fused_computation.31 | convolution fusion | flops 6119276544 | bytes 15040512 | tf_op jit(solution)/shard_map/td,ntc->ndc/dot_general | solution.py:359
  452.0 17.5 %fusion.24 = (f32[768]{0:T(1024)S(1)}, f32[768]{0:T(1024)S(1)}, bf16[768,1152]{1,0:T(8,128)(2,1)}, f32[768,1152,1]{1,0,2:T(8,128)}) fusion(f32[3,1152]{1,0:T(4,128)S(1)} %copy-done.41, f32[768]{0:T(1024)S(1)} %copy-done.54, f32[768]{0:T(1024)S(1)} %copy-done.50, bf16[768,1152]{1,0:T(8,128)(2,1)S(1)} %copy-done.9, f32[768,1152]{1,0:T(8,128)} %fusion.15, ...), kind=kOutput, calls=%fused_computation.71 | convolution fusion | flops 6125910016 | bytes 27972096 | tf_op jit(solution)/shard_map/ntc,ndc->td/dot_general | solution.py:362
  474.7 16.1 %convert_reduce_fusion = (f32[4,1152]{1,0:T(4,128)S(1)}, bf16[4,768,1152]{2,1,0:T(8,128)(2,1)}) fusion(f32[4,1152,768]{1,2,0:T(8,128)} %fusion.36, f32[4,1152]{1,0:T(4,128)S(1)} %copy-done.47, f32[4,1152,768]{1,2,0:T(8,128)} %get-tuple-element.178), kind=kLoop, calls=%fused_computation.18 | loop fusion | flops 81391104 | bytes 35426304 | tf_op jit(solution)/shard_map/reduce_sum | solution.py:344
  490.8 12.2 %convolution_convert_fusion.1 = bf16[4,1152,1152]{1,2,0:T(8,128)(2,1)S(1)} fusion(bf16[4,768,1152]{2,1,0:T(8,128)(2,1)} %get-tuple-element.84, bf16[768,1152]{1,0:T(8,128)(2,1)S(1)} %copy-done.34), kind=kOutput, calls=%fused_computation.1 | convolution fusion | flops 8159035392 | bytes 19464192 | tf_op jit(solution)/shard_map/td,ntf->ndf/dot_general | solution.py:345
  517.5 15.2 %copy.121 = bf16[4,1152,1152]{2,1,0:T(8,128)(2,1)} copy(bf16[4,1152,1152]{1,2,0:T(8,128)(2,1)} %pad_maximum_fusion) | data formatting | bytes 21233664 | tf_op jit(solution)/shard_map/concatenate | solution.py:360
  605.4 8.4 add_convert_fusion.3
  635.8 23.4 %collective-permute-done.47 = bf16[1,2,2,2,1,64,1152]{6,5,4,3,2,1,0:T(8,128)(2,1)S(1)} collective-permute-done((bf16[1,2,2,2,1,64,1152]{6,5,4,3,2,1,0:T(8,128)(2,1)S(1)}, bf16[1,2,2,2,1,64,1152]{6,5,4,3,2,1,0:T(8,128)(2,1)S(1)}, u32[]{:S(2)}, u32[]{:S(2)}) %collective-permute-start.47) | collective-permute-done | bytes 1179680 | tf_op jit(solution)/shard_map/ppermute | solution.py:25
  659.6 21.8 %collective-permute-done.40 = bf16[1,2,2,2,1,64,1152]{6,5,4,3,2,1,0:T(8,128)(2,1)S(1)} collective-permute-done((bf16[1,2,2,2,1,64,1152]{6,5,4,3,2,1,0:T(8,128)(2,1)S(1)}, bf16[1,2,2,2,1,64,1152]{6,5,4,3,2,1,0:T(8,128)(2,1)S(1)}, u32[]{:S(2)}, u32[]{:S(2)}) %collective-permute-start.40) | collective-permute-done | bytes 1179680 | tf_op jit(solution)/shard_map/ppermute | solution.py:25
  684.3 8.9 %collective-permute-done.49 = bf16[2,1,2,2,1,80,1152]{6,5,4,3,2,1,0:T(8,128)(2,1)S(1)} collective-permute-done((bf16[2,1,2,2,1,80,1152]{6,5,4,3,2,1,0:T(8,128)(2,1)S(1)}, bf16[2,1,2,2,1,80,1152]{6,5,4,3,2,1,0:T(8,128)(2,1)S(1)}, u32[]{:S(2)}, u32[]{:S(2)}) %collective-permute-start.49) | collective-permute-done | bytes 1474592 | tf_op jit(solution)/shard_map/ppermute | solution.py:25
  694.7 30.1 %collective-permute-done.42 = bf16[2,1,2,2,1,80,1152]{6,5,4,3,2,1,0:T(8,128)(2,1)S(1)} collective-permute-done((bf16[2,1,2,2,1,80,1152]{6,5,4,3,2,1,0:T(8,128)(2,1)S(1)}, bf16[2,1,2,2,1,80,1152]{6,5,4,3,2,1,0:T(8,128)(2,1)S(1)}, u32[]{:S(2)}, u32[]{:S(2)}) %collective-permute-start.42) | collective-permute-done | bytes 1474592 | tf_op jit(solution)/shard_map/ppermute | solution.py:25
  726.5 11.0 %collective-permute-done.55 = bf16[1,1,2,2,1,64,1152]{6,5,4,3,2,1,0:T(8,128)(2,1)S(1)} collective-permute-done((bf16[1,1,2,2,1,64,1152]{6,5,4,3,2,1,0:T(8,128)(2,1)S(1)}, bf16[1,1,2,2,1,64,1152]{6,5,4,3,2,1,0:T(8,128)(2,1)S(1)}, u32[]{:S(2)}, u32[]{:S(2)}) %collective-permute-start.55) | collective-permute-done | bytes 589856 | tf_op jit(solution)/shard_map/ppermute | solution.py:25
  738.7 11.4 %collective-permute-done.48 = bf16[1,1,2,2,1,64,1152]{6,5,4,3,2,1,0:T(8,128)(2,1)S(1)} collective-permute-done((bf16[1,1,2,2,1,64,1152]{6,5,4,3,2,1,0:T(8,128)(2,1)S(1)}, bf16[1,1,2,2,1,64,1152]{6,5,4,3,2,1,0:T(8,128)(2,1)S(1)}, u32[]{:S(2)}, u32[]{:S(2)}) %collective-permute-start.48) | collective-permute-done | bytes 589856 | tf_op jit(solution)/shard_map/ppermute | solution.py:25
  750.2 9.3 %collective-permute-done.41 = bf16[1,1,2,2,1,64,1152]{6,5,4,3,2,1,0:T(8,128)(2,1)S(1)} collective-permute-done((bf16[1,1,2,2,1,64,1152]{6,5,4,3,2,1,0:T(8,128)(2,1)S(1)}, bf16[1,1,2,2,1,64,1152]{6,5,4,3,2,1,0:T(8,128)(2,1)S(1)}, u32[]{:S(2)}, u32[]{:S(2)}) %collective-permute-start.41) | collective-permute-done | bytes 589856 | tf_op jit(solution)/shard_map/ppermute | solution.py:25
  764.0 17.4 %collective-permute-done.58 = bf16[1,1,2,1,1,144,1152]{6,5,4,3,2,1,0:T(8,128)(2,1)S(1)} collective-permute-done((bf16[1,1,2,1,1,144,1152]{6,5,4,3,2,1,0:T(8,128)(2,1)S(1)}, bf16[1,1,2,1,1,144,1152]{6,5,4,3,2,1,0:T(8,128)(2,1)S(1)}, u32[]{:S(2)}, u32[]{:S(2)}) %collective-permute-start.58) | collective-permute-done | bytes 663584 | tf_op jit(solution)/shard_map/ppermute | solution.py:25
  783.7 19.0 %collective-permute-done.51 = bf16[1,1,2,1,1,144,1152]{6,5,4,3,2,1,0:T(8,128)(2,1)S(1)} collective-permute-done((bf16[1,1,2,1,1,144,1152]{6,5,4,3,2,1,0:T(8,128)(2,1)S(1)}, bf16[1,1,2,1,1,144,1152]{6,5,4,3,2,1,0:T(8,128)(2,1)S(1)}, u32[]{:S(2)}, u32[]{:S(2)}) %collective-permute-start.51) | collective-permute-done | bytes 663584 | tf_op jit(solution)/shard_map/ppermute | solution.py:25
  803.7 9.6 %collective-permute-done.44 = bf16[1,1,2,1,1,144,1152]{6,5,4,3,2,1,0:T(8,128)(2,1)S(1)} collective-permute-done((bf16[1,1,2,1,1,144,1152]{6,5,4,3,2,1,0:T(8,128)(2,1)S(1)}, bf16[1,1,2,1,1,144,1152]{6,5,4,3,2,1,0:T(8,128)(2,1)S(1)}, u32[]{:S(2)}, u32[]{:S(2)}) %collective-permute-start.44) | collective-permute-done | bytes 663584 | tf_op jit(solution)/shard_map/ppermute | solution.py:25
  817.4 20.2 %collective-permute-done.45 = bf16[1,1,1,1,1,144,1152]{6,5,4,3,2,1,0:T(8,128)(2,1)S(1)} collective-permute-done((bf16[1,1,1,1,1,144,1152]{6,5,4,3,2,1,0:T(8,128)(2,1)S(1)}, bf16[1,1,1,1,1,144,1152]{6,5,4,3,2,1,0:T(8,128)(2,1)S(1)}, u32[]{:S(2)}, u32[]{:S(2)}) %collective-permute-start.45) | collective-permute-done | bytes 331808 | tf_op jit(solution)/shard_map/ppermute | solution.py:25
  (463 shorter events, 301.5 us)
Async XLA Ops:
  4.1 57.4 %collective-permute-start.5 = (bf16[1,1,1,1,1,144,1152]{6,5,4,3,2,1,0:T(8,128)(2,1)}, bf16[1,1,1,1,1,144,1152]{6,5,4,3,2,1,0:T(8,128)(2,1)S(1)}, u32[]{:S(2)}, u32[]{:S(2)}) collective-permute-start(bf16[1,1,1,1,1,144,1152]{6,5,4,3,2,1,0:T(8,128)(2,1)} %maximum_bitcast_fusion), channel_id=1, source_target_pairs={{0,16},{4,20},{8,24},{12,28},{16,0},{20,4},{24,8},{28,12},{1,17},{... | collective-permute-start | bytes 995336 | tf_op jit(solution)/shard_map/ppermute | solution.py:25
  8.1 55.2 %collective-permute-start.13 = (bf16[1,1,1,1,1,144,1152]{6,5,4,3,2,1,0:T(8,128)(2,1)}, bf16[1,1,1,1,1,144,1152]{6,5,4,3,2,1,0:T(8,128)(2,1)}, u32[]{:S(2)}, u32[]{:S(2)}) collective-permute-start(bf16[1,1,1,1,1,144,1152]{6,5,4,3,2,1,0:T(8,128)(2,1)} %bitcast.282), channel_id=1, source_target_pairs={{0,16},{4,20},{8,24},{12,28},{16,0},{20,4},{24,8},{28,12},{1,17},{... | collective-permute-start | bytes 995336 | tf_op jit(solution)/shard_map/ppermute | solution.py:25
  10.2 56.7 %collective-permute-start.21 = (bf16[1,1,1,1,1,144,1152]{6,5,4,3,2,1,0:T(8,128)(2,1)}, bf16[1,1,1,1,1,144,1152]{6,5,4,3,2,1,0:T(8,128)(2,1)}, u32[]{:S(2)}, u32[]{:S(2)}) collective-permute-start(bf16[1,1,1,1,1,144,1152]{6,5,4,3,2,1,0:T(8,128)(2,1)} %bitcast.25), channel_id=1, source_target_pairs={{0,16},{4,20},{8,24},{12,28},{16,0},{20,4},{24,8},{28,12},{1,17},{... | collective-permute-start | bytes 995336 | tf_op jit(solution)/shard_map/ppermute | solution.py:25
  70.6 36.4 %collective-permute-start.22 = (bf16[1,1,2,1,1,144,1152]{6,5,4,3,2,1,0:T(8,128)(2,1)}, bf16[1,1,2,1,1,144,1152]{6,5,4,3,2,1,0:T(8,128)(2,1)}, u32[]{:S(2)}, u32[]{:S(2)}) collective-permute-start(bf16[1,1,2,1,1,144,1152]{6,5,4,3,2,1,0:T(8,128)(2,1)} %pad_maximum_fusion.18), channel_id=1, source_target_pairs={{0,8},{4,12},{8,0},{12,4},{16,24},{20,28},{24,16},{28,20},{1,9},{5... | collective-permute-start | bytes 1990664 | tf_op jit(solution)/shard_map/ppermute | solution.py:25
  98.1 33.8 %collective-permute-start.10 = (bf16[1,1,2,2,1,80,1152]{6,5,4,3,2,1,0:T(8,128)(2,1)S(1)}, bf16[1,1,2,2,1,80,1152]{6,5,4,3,2,1,0:T(8,128)(2,1)S(1)}, u32[]{:S(2)}, u32[]{:S(2)}) collective-permute-start(bf16[1,1,2,2,1,80,1152]{6,5,4,3,2,1,0:T(8,128)(2,1)S(1)} %pad_maximum_fusion.15), channel_id=1, source_target_pairs={{0,1},{1,0},{2,3},{3,2},{4,5},{5,4},{6,7},{7,6},{8,9},{9,8},{10,11... | collective-permute-start | bytes 2211848 | tf_op jit(solution)/shard_map/ppermute | solution.py:25
  98.8 34.9 %collective-permute-start.18 = (bf16[1,1,2,2,1,80,1152]{6,5,4,3,2,1,0:T(8,128)(2,1)S(1)}, bf16[1,1,2,2,1,80,1152]{6,5,4,3,2,1,0:T(8,128)(2,1)S(1)}, u32[]{:S(2)}, u32[]{:S(2)}) collective-permute-start(bf16[1,1,2,2,1,80,1152]{6,5,4,3,2,1,0:T(8,128)(2,1)S(1)} %pad_maximum_fusion.14), channel_id=1, source_target_pairs={{0,1},{1,0},{2,3},{3,2},{4,5},{5,4},{6,7},{7,6},{8,9},{9,8},{10,11... | collective-permute-start | bytes 2211848 | tf_op jit(solution)/shard_map/ppermute | solution.py:25
  110.0 39.2 %collective-permute-start.26 = (bf16[1,1,2,2,1,80,1152]{6,5,4,3,2,1,0:T(8,128)(2,1)S(1)}, bf16[1,1,2,2,1,80,1152]{6,5,4,3,2,1,0:T(8,128)(2,1)S(1)}, u32[]{:S(2)}, u32[]{:S(2)}) collective-permute-start(bf16[1,1,2,2,1,80,1152]{6,5,4,3,2,1,0:T(8,128)(2,1)S(1)} %pad_maximum_fusion.13), channel_id=1, source_target_pairs={{0,1},{1,0},{2,3},{3,2},{4,5},{5,4},{6,7},{7,6},{8,9},{9,8},{10,11... | collective-permute-start | bytes 2211848 | tf_op jit(solution)/shard_map/ppermute | solution.py:25
  121.7 52.7 %collective-permute-start.8 = (bf16[2,1,2,2,1,64,1152]{6,5,4,3,2,1,0:T(8,128)(2,1)S(1)}, bf16[2,1,2,2,1,64,1152]{6,5,4,3,2,1,0:T(8,128)(2,1)S(1)}, u32[]{:S(2)}, u32[]{:S(2)}) collective-permute-start(bf16[2,1,2,2,1,64,1152]{6,5,4,3,2,1,0:T(8,128)(2,1)S(1)} %pad_maximum_fusion.10), channel_id=1, source_target_pairs={{0,1},{1,0},{2,3},{3,2},{4,5},{5,4},{6,7},{7,6},{8,9},{9,8},{10,11... | collective-permute-start | bytes 3538952 | tf_op jit(solution)/shard_map/ppermute | solution.py:25
  130.7 69.0 %collective-permute-start.16 = (bf16[2,1,2,2,1,64,1152]{6,5,4,3,2,1,0:T(8,128)(2,1)S(1)}, bf16[2,1,2,2,1,64,1152]{6,5,4,3,2,1,0:T(8,128)(2,1)S(1)}, u32[]{:S(2)}, u32[]{:S(2)}) collective-permute-start(bf16[2,1,2,2,1,64,1152]{6,5,4,3,2,1,0:T(8,128)(2,1)S(1)} %pad_maximum_fusion.11), channel_id=1, source_target_pairs={{0,1},{1,0},{2,3},{3,2},{4,5},{5,4},{6,7},{7,6},{8,9},{9,8},{10,11... | collective-permute-start | bytes 3538952 | tf_op jit(solution)/shard_map/ppermute | solution.py:25
  131.9 87.4 %collective-permute-start.24 = (bf16[2,1,2,2,1,64,1152]{6,5,4,3,2,1,0:T(8,128)(2,1)S(1)}, bf16[2,1,2,2,1,64,1152]{6,5,4,3,2,1,0:T(8,128)(2,1)S(1)}, u32[]{:S(2)}, u32[]{:S(2)}) collective-permute-start(bf16[2,1,2,2,1,64,1152]{6,5,4,3,2,1,0:T(8,128)(2,1)S(1)} %pad_maximum_fusion.12), channel_id=1, source_target_pairs={{0,1},{1,0},{2,3},{3,2},{4,5},{5,4},{6,7},{7,6},{8,9},{9,8},{10,11... | collective-permute-start | bytes 3538952 | tf_op jit(solution)/shard_map/ppermute | solution.py:25
  133.7 86.2 %collective-permute-start.11 = (bf16[1,2,2,2,1,80,1152]{6,5,4,3,2,1,0:T(8,128)(2,1)S(1)}, bf16[1,2,2,2,1,80,1152]{6,5,4,3,2,1,0:T(8,128)(2,1)S(1)}, u32[]{:S(2)}, u32[]{:S(2)}) collective-permute-start(bf16[1,2,2,2,1,80,1152]{6,5,4,3,2,1,0:T(8,128)(2,1)S(1)} %pad_maximum_fusion.7), channel_id=1, source_target_pairs={{0,2},{1,3},{2,0},{3,1},{4,6},{5,7},{6,4},{7,5},{8,10},{9,11},{10,... | collective-permute-start | bytes 4423688 | tf_op jit(solution)/shard_map/ppermute | solution.py:25
  149.2 71.3 %collective-permute-start.19 = (bf16[1,2,2,2,1,80,1152]{6,5,4,3,2,1,0:T(8,128)(2,1)S(1)}, bf16[1,2,2,2,1,80,1152]{6,5,4,3,2,1,0:T(8,128)(2,1)S(1)}, u32[]{:S(2)}, u32[]{:S(2)}) collective-permute-start(bf16[1,2,2,2,1,80,1152]{6,5,4,3,2,1,0:T(8,128)(2,1)S(1)} %pad_maximum_fusion.8), channel_id=1, source_target_pairs={{0,2},{1,3},{2,0},{3,1},{4,6},{5,7},{6,4},{7,5},{8,10},{9,11},{10,... | collective-permute-start | bytes 4423688 | tf_op jit(solution)/shard_map/ppermute | solution.py:25
  174.5 52.6 %collective-permute-start.27 = (bf16[1,2,2,2,1,80,1152]{6,5,4,3,2,1,0:T(8,128)(2,1)S(1)}, bf16[1,2,2,2,1,80,1152]{6,5,4,3,2,1,0:T(8,128)(2,1)S(1)}, u32[]{:S(2)}, u32[]{:S(2)}) collective-permute-start(bf16[1,2,2,2,1,80,1152]{6,5,4,3,2,1,0:T(8,128)(2,1)S(1)} %pad_maximum_fusion.9), channel_id=1, source_target_pairs={{0,2},{1,3},{2,0},{3,1},{4,6},{5,7},{6,4},{7,5},{8,10},{9,11},{10,... | collective-permute-start | bytes 4423688 | tf_op jit(solution)/shard_map/ppermute | solution.py:25
  227.0 46.3 %collective-permute-start.20 = (bf16[2,2,2,2,1,80,1152]{6,5,4,3,2,1,0:T(8,128)(2,1)}, bf16[2,2,2,2,1,80,1152]{6,5,4,3,2,1,0:T(8,128)(2,1)}, u32[]{:S(2)}, u32[]{:S(2)}) collective-permute-start(bf16[2,2,2,2,1,80,1152]{6,5,4,3,2,1,0:T(8,128)(2,1)} %pad_maximum_fusion.2), channel_id=1, source_target_pairs={{0,4},{4,0},{8,12},{12,8},{16,20},{20,16},{24,28},{28,24},{1,5},{5... | collective-permute-start | bytes 8847368 | tf_op jit(solution)/shard_map/ppermute | solution.py:25
  229.9 81.4 %collective-permute-start.28 = (bf16[2,2,2,2,1,80,1152]{6,5,4,3,2,1,0:T(8,128)(2,1)}, bf16[2,2,2,2,1,80,1152]{6,5,4,3,2,1,0:T(8,128)(2,1)}, u32[]{:S(2)}, u32[]{:S(2)}) collective-permute-start(bf16[2,2,2,2,1,80,1152]{6,5,4,3,2,1,0:T(8,128)(2,1)} %pad_maximum_fusion.3), channel_id=1, source_target_pairs={{0,4},{4,0},{8,12},{12,8},{16,20},{20,16},{24,28},{28,24},{1,5},{5... | collective-permute-start | bytes 8847368 | tf_op jit(solution)/shard_map/ppermute | solution.py:25
  474.6 122.0 %collective-permute-start.53 = (bf16[2,2,2,2,1,144,1152]{6,5,4,3,2,1,0:T(8,128)(2,1)}, bf16[2,2,2,2,1,144,1152]{6,5,4,3,2,1,0:T(8,128)(2,1)}, u32[]{:S(2)}, u32[]{:S(2)}) collective-permute-start(bf16[2,2,2,2,1,144,1152]{6,5,4,3,2,1,0:T(8,128)(2,1)} %constant_dynamic-slice_fusion.5), channel_id=1, source_target_pairs={{0,4},{4,0},{8,12},{12,8},{16,20},{20,16},{24,28},{28,24},{1,5},{5... | collective-permute-start | bytes 15925256 | tf_op jit(solution)/shard_map/ppermute | solution.py:25
  509.1 96.3 %collective-permute-start.46 = (bf16[2,2,2,2,1,144,1152]{6,5,4,3,2,1,0:T(8,128)(2,1)}, bf16[2,2,2,2,1,144,1152]{6,5,4,3,2,1,0:T(8,128)(2,1)}, u32[]{:S(2)}, u32[]{:S(2)}) collective-permute-start(bf16[2,2,2,2,1,144,1152]{6,5,4,3,2,1,0:T(8,128)(2,1)} %constant_dynamic-slice_fusion.11), channel_id=1, source_target_pairs={{0,4},{4,0},{8,12},{12,8},{16,20},{20,16},{24,28},{28,24},{1,5},{5... | collective-permute-start | bytes 15925256 | tf_op jit(solution)/shard_map/ppermute | solution.py:25
  550.9 62.9 %collective-permute-start.39 = (bf16[2,2,2,2,1,144,1152]{6,5,4,3,2,1,0:T(8,128)(2,1)}, bf16[2,2,2,2,1,144,1152]{6,5,4,3,2,1,0:T(8,128)(2,1)}, u32[]{:S(2)}, u32[]{:S(2)}) collective-permute-start(bf16[2,2,2,2,1,144,1152]{6,5,4,3,2,1,0:T(8,128)(2,1)} %constant_dynamic-slice_fusion.17), channel_id=1, source_target_pairs={{0,4},{4,0},{8,12},{12,8},{16,20},{20,16},{24,28},{28,24},{1,5},{5... | collective-permute-start | bytes 15925256 | tf_op jit(solution)/shard_map/ppermute | solution.py:25
  626.3 56.0 %collective-permute-start.56 = (bf16[2,1,2,2,1,80,1152]{6,5,4,3,2,1,0:T(8,128)(2,1)S(1)}, bf16[2,1,2,2,1,80,1152]{6,5,4,3,2,1,0:T(8,128)(2,1)S(1)}, u32[]{:S(2)}, u32[]{:S(2)}) collective-permute-start(bf16[2,1,2,2,1,80,1152]{6,5,4,3,2,1,0:T(8,128)(2,1)S(1)} %constant_dynamic-slice_fusion.2), channel_id=1, source_target_pairs={{0,1},{1,0},{2,3},{3,2},{4,5},{5,4},{6,7},{7,6},{8,9},{9,8},{10,11... | collective-permute-start | bytes 4423688 | tf_op jit(solution)/shard_map/ppermute | solution.py:25
  627.0 32.3 %collective-permute-start.47 = (bf16[1,2,2,2,1,64,1152]{6,5,4,3,2,1,0:T(8,128)(2,1)S(1)}, bf16[1,2,2,2,1,64,1152]{6,5,4,3,2,1,0:T(8,128)(2,1)S(1)}, u32[]{:S(2)}, u32[]{:S(2)}) collective-permute-start(bf16[1,2,2,2,1,64,1152]{6,5,4,3,2,1,0:T(8,128)(2,1)S(1)} %constant_dynamic-slice_fusion.10), channel_id=1, source_target_pairs={{0,2},{1,3},{2,0},{3,1},{4,6},{5,7},{6,4},{7,5},{8,10},{9,11},{10,... | collective-permute-start | bytes 3538952 | tf_op jit(solution)/shard_map/ppermute | solution.py:25
  628.3 64.9 %collective-permute-start.49 = (bf16[2,1,2,2,1,80,1152]{6,5,4,3,2,1,0:T(8,128)(2,1)S(1)}, bf16[2,1,2,2,1,80,1152]{6,5,4,3,2,1,0:T(8,128)(2,1)S(1)}, u32[]{:S(2)}, u32[]{:S(2)}) collective-permute-start(bf16[2,1,2,2,1,80,1152]{6,5,4,3,2,1,0:T(8,128)(2,1)S(1)} %constant_dynamic-slice_fusion.8), channel_id=1, source_target_pairs={{0,1},{1,0},{2,3},{3,2},{4,5},{5,4},{6,7},{7,6},{8,9},{9,8},{10,11... | collective-permute-start | bytes 4423688 | tf_op jit(solution)/shard_map/ppermute | solution.py:25
  629.9 51.5 %collective-permute-start.40 = (bf16[1,2,2,2,1,64,1152]{6,5,4,3,2,1,0:T(8,128)(2,1)S(1)}, bf16[1,2,2,2,1,64,1152]{6,5,4,3,2,1,0:T(8,128)(2,1)S(1)}, u32[]{:S(2)}, u32[]{:S(2)}) collective-permute-start(bf16[1,2,2,2,1,64,1152]{6,5,4,3,2,1,0:T(8,128)(2,1)S(1)} %constant_dynamic-slice_fusion.16), channel_id=1, source_target_pairs={{0,2},{1,3},{2,0},{3,1},{4,6},{5,7},{6,4},{7,5},{8,10},{9,11},{10,... | collective-permute-start | bytes 3538952 | tf_op jit(solution)/shard_map/ppermute | solution.py:25
  634.1 90.7 %collective-permute-start.42 = (bf16[2,1,2,2,1,80,1152]{6,5,4,3,2,1,0:T(8,128)(2,1)S(1)}, bf16[2,1,2,2,1,80,1152]{6,5,4,3,2,1,0:T(8,128)(2,1)S(1)}, u32[]{:S(2)}, u32[]{:S(2)}) collective-permute-start(bf16[2,1,2,2,1,80,1152]{6,5,4,3,2,1,0:T(8,128)(2,1)S(1)} %constant_dynamic-slice_fusion.14), channel_id=1, source_target_pairs={{0,1},{1,0},{2,3},{3,2},{4,5},{5,4},{6,7},{7,6},{8,9},{9,8},{10,11... | collective-permute-start | bytes 4423688 | tf_op jit(solution)/shard_map/ppermute | solution.py:25
  659.3 78.2 %collective-permute-start.55 = (bf16[1,1,2,2,1,64,1152]{6,5,4,3,2,1,0:T(8,128)(2,1)S(1)}, bf16[1,1,2,2,1,64,1152]{6,5,4,3,2,1,0:T(8,128)(2,1)S(1)}, u32[]{:S(2)}, u32[]{:S(2)}) collective-permute-start(bf16[1,1,2,2,1,64,1152]{6,5,4,3,2,1,0:T(8,128)(2,1)S(1)} %constant_dynamic-slice_fusion.3), channel_id=1, source_target_pairs={{0,1},{1,0},{2,3},{3,2},{4,5},{5,4},{6,7},{7,6},{8,9},{9,8},{10,11... | collective-permute-start | bytes 1769480 | tf_op jit(solution)/shard_map/ppermute | solution.py:25
  681.4 68.7 %collective-permute-start.48 = (bf16[1,1,2,2,1,64,1152]{6,5,4,3,2,1,0:T(8,128)(2,1)S(1)}, bf16[1,1,2,2,1,64,1152]{6,5,4,3,2,1,0:T(8,128)(2,1)S(1)}, u32[]{:S(2)}, u32[]{:S(2)}) collective-permute-start(bf16[1,1,2,2,1,64,1152]{6,5,4,3,2,1,0:T(8,128)(2,1)S(1)} %constant_dynamic-slice_fusion.9), channel_id=1, source_target_pairs={{0,1},{1,0},{2,3},{3,2},{4,5},{5,4},{6,7},{7,6},{8,9},{9,8},{10,11... | collective-permute-start | bytes 1769480 | tf_op jit(solution)/shard_map/ppermute | solution.py:25
  682.3 77.2 %collective-permute-start.41 = (bf16[1,1,2,2,1,64,1152]{6,5,4,3,2,1,0:T(8,128)(2,1)S(1)}, bf16[1,1,2,2,1,64,1152]{6,5,4,3,2,1,0:T(8,128)(2,1)S(1)}, u32[]{:S(2)}, u32[]{:S(2)}) collective-permute-start(bf16[1,1,2,2,1,64,1152]{6,5,4,3,2,1,0:T(8,128)(2,1)S(1)} %constant_dynamic-slice_fusion.15), channel_id=1, source_target_pairs={{0,1},{1,0},{2,3},{3,2},{4,5},{5,4},{6,7},{7,6},{8,9},{9,8},{10,11... | collective-permute-start | bytes 1769480 | tf_op jit(solution)/shard_map/ppermute | solution.py:25
  693.2 66.5 %collective-permute-start.57 = (bf16[1,1,2,2,1,80,1152]{6,5,4,3,2,1,0:T(8,128)(2,1)S(1)}, bf16[1,1,2,2,1,80,1152]{6,5,4,3,2,1,0:T(8,128)(2,1)S(1)}, u32[]{:S(2)}, u32[]{:S(2)}) collective-permute-start(bf16[1,1,2,2,1,80,1152]{6,5,4,3,2,1,0:T(8,128)(2,1)S(1)} %constant_dynamic-slice_fusion.1), channel_id=1, source_target_pairs={{0,2},{1,3},{2,0},{3,1},{4,6},{5,7},{6,4},{7,5},{8,10},{9,11},{10,... | collective-permute-start | bytes 2211848 | tf_op jit(solution)/shard_map/ppermute | solution.py:25
  724.8 36.5 %collective-permute-start.50 = (bf16[1,1,2,2,1,80,1152]{6,5,4,3,2,1,0:T(8,128)(2,1)S(1)}, bf16[1,1,2,2,1,80,1152]{6,5,4,3,2,1,0:T(8,128)(2,1)S(1)}, u32[]{:S(2)}, u32[]{:S(2)}) collective-permute-start(bf16[1,1,2,2,1,80,1152]{6,5,4,3,2,1,0:T(8,128)(2,1)S(1)} %constant_dynamic-slice_fusion.7), channel_id=1, source_target_pairs={{0,2},{1,3},{2,0},{3,1},{4,6},{5,7},{6,4},{7,5},{8,10},{9,11},{10,... | collective-permute-start | bytes 2211848 | tf_op jit(solution)/shard_map/ppermute | solution.py:25
  761.6 41.2 %collective-permute-start.51 = (bf16[1,1,2,1,1,144,1152]{6,5,4,3,2,1,0:T(8,128)(2,1)S(1)}, bf16[1,1,2,1,1,144,1152]{6,5,4,3,2,1,0:T(8,128)(2,1)S(1)}, u32[]{:S(2)}, u32[]{:S(2)}) collective-permute-start(bf16[1,1,2,1,1,144,1152]{6,5,4,3,2,1,0:T(8,128)(2,1)S(1)} %fusion.45), channel_id=1, source_target_pairs={{0,8},{4,12},{8,0},{12,4},{16,24},{20,28},{24,16},{28,20},{1,9},{5... | collective-permute-start | bytes 1990664 | tf_op jit(solution)/shard_map/ppermute | solution.py:25
  762.7 50.6 %collective-permute-start.44 = (bf16[1,1,2,1,1,144,1152]{6,5,4,3,2,1,0:T(8,128)(2,1)S(1)}, bf16[1,1,2,1,1,144,1152]{6,5,4,3,2,1,0:T(8,128)(2,1)S(1)}, u32[]{:S(2)}, u32[]{:S(2)}) collective-permute-start(bf16[1,1,2,1,1,144,1152]{6,5,4,3,2,1,0:T(8,128)(2,1)S(1)} %fusion.47), channel_id=1, source_target_pairs={{0,8},{4,12},{8,0},{12,4},{16,24},{20,28},{24,16},{28,20},{1,9},{5... | collective-permute-start | bytes 1990664 | tf_op jit(solution)/shard_map/ppermute | solution.py:25
  781.7 34.8 %collective-permute-start.59 = (bf16[1,1,1,1,1,144,1152]{6,5,4,3,2,1,0:T(8,128)(2,1)S(1)}, bf16[1,1,1,1,1,144,1152]{6,5,4,3,2,1,0:T(8,128)(2,1)S(1)}, u32[]{:S(2)}, u32[]{:S(2)}) collective-permute-start(bf16[1,1,1,1,1,144,1152]{6,5,4,3,2,1,0:T(8,128)(2,1)S(1)} %constant_dynamic-slice_fusion), channel_id=1, source_target_pairs={{0,16},{4,20},{8,24},{12,28},{16,0},{20,4},{24,8},{28,12},{1,17},{... | collective-permute-start | bytes 995336 | tf_op jit(solution)/shard_map/ppermute | solution.py:25
  803.7 36.2 %collective-permute-start.52 = (bf16[1,1,1,1,1,144,1152]{6,5,4,3,2,1,0:T(8,128)(2,1)}, bf16[1,1,1,1,1,144,1152]{6,5,4,3,2,1,0:T(8,128)(2,1)}, u32[]{:S(2)}, u32[]{:S(2)}) collective-permute-start(bf16[1,1,1,1,1,144,1152]{6,5,4,3,2,1,0:T(8,128)(2,1)} %constant_dynamic-slice_fusion.6), channel_id=1, source_target_pairs={{0,16},{4,20},{8,24},{12,28},{16,0},{20,4},{24,8},{28,12},{1,17},{... | collective-permute-start | bytes 995336 | tf_op jit(solution)/shard_map/ppermute | solution.py:25
  (102 other events, 1374.7 us)

commit v2 on v1

v2 whole, which is shorter than its diff:
```python
import functools
import math

import jax
import jax.numpy as jnp
from jax import lax
from jax.experimental import pallas as pl
from jax.experimental.pallas import tpu as pltpu
from jax.sharding import PartitionSpec as P

HEAD = 72
PATCHES = 256
EPSILON = 1e-06
MIB = 1 << 20
F32 = jnp.float32
BF16 = jnp.bfloat16


def bits_of(size):
    return [1 << k for k in range(size.bit_length() - 1)]


def swap(block, axis, bit):
    count = lax.axis_size(axis)
    return lax.ppermute(block, axis, [(i, i ^ bit) for i in range(count)])


def my_bit(axis, bit):
    return (lax.axis_index(axis) // bit) % 2


def tied(*values):
    return lax.optimization_barrier(values)


def dot(a, b, ca, cb):
    return lax.dot_general(a, b, (((ca,), (cb,)), ((), ())), preferred_element_type=F32)


def row_mean(values):
    return jnp.mean(values, axis=1, keepdims=True)


def normalize(values):
    center = row_mean(values)
    inverse = lax.rsqrt(row_mean(values * values) - center * center + EPSILON)
    return inverse, (values - center) * inverse


def norm_back(incoming, normed, inverse):
    return inverse * (incoming - row_mean(incoming) - normed * row_mean(incoming * normed))


def gelu_both(upper):
    c0 = math.sqrt(2.0 / math.pi)
    square = upper * upper
    tanh = jnp.tanh(upper * (c0 + (c0 * 0.044715) * square))
    half = 0.5 + 0.5 * tanh
    bend = (half * (1.0 - half)) * (2.0 * c0 + (2.0 * c0 * 0.134145) * square)
    return upper * half, half + upper * bend


def params(limit=56):
    return pltpu.CompilerParams(vmem_limit_bytes=limit * MIB)


def cost():
    return pl.CostEstimate(flops=1000000000, bytes_accessed=1, transcendentals=0)


def whole(array):
    return pl.BlockSpec(array.shape, lambda i, *_: (0,) * array.ndim)


def along(array):
    return pl.BlockSpec((1,) + array.shape[1:], lambda i, *_: (i,) + (0,) * (array.ndim - 1))


def shape_of(shape, dtype):
    return jax.ShapeDtypeStruct(shape, dtype)


def attend_kernel(heads, qkv_ref, out_ref):
    part = heads * HEAD
    scale = HEAD ** (-0.5)
    results = []
    for n in range(qkv_ref.shape[0]):
        for h in range(heads):
            at = h * HEAD
            q = qkv_ref[n, :, at : at + HEAD]
            k = qkv_ref[n, :, part + at : part + at + HEAD]
            v = qkv_ref[n, :, 2 * part + at : 2 * part + at + HEAD]
            s = dot(k, q, 1, 1)
            p = jnp.exp((s - jnp.max(s, axis=0, keepdims=True)) * scale)
            total = jnp.sum(p, axis=0, keepdims=True)
            results.append(dot(v, p.astype(BF16), 0, 0) / total)
    out_ref[...] = jnp.concatenate(results, axis=0).T.astype(BF16)


def attend(qkv, heads):
    groups, rows, cols = qkv.shape
    width = groups * heads * HEAD
    out = shape_of((rows, width), BF16)
    return pl.pallas_call(
        functools.partial(attend_kernel, heads),
        grid=(rows // PATCHES,),
        in_specs=[pl.BlockSpec((groups, PATCHES, cols), lambda f: (0, f, 0))],
        out_specs=pl.BlockSpec((PATCHES, width), lambda f: (f, 0)),
        out_shape=out,
        compiler_params=params(),
        cost_estimate=cost(),
        name="attend",
    )(qkv)


def attend_back_kernel(heads, qkv_ref, grad_ref, out_ref):
    part = heads * HEAD
    scale = HEAD ** (-0.5)
    for n in range(qkv_ref.shape[0]):
        dqs, dks, dvs = [], [], []
        for h in range(heads):
            at = h * HEAD
            q = qkv_ref[n, :, at : at + HEAD]
            k = qkv_ref[n, :, part + at : part + at + HEAD]
            v = qkv_ref[n, :, 2 * part + at : 2 * part + at + HEAD]
            g = grad_ref[:, n * part + at : n * part + at + HEAD]
            s = dot(k, q, 1, 1)
            p = jnp.exp((s - jnp.max(s, axis=0, keepdims=True)) * scale)
            p = p * (1.0 / jnp.sum(p, axis=0, keepdims=True))
            dvs.append(dot(p.astype(BF16), g, 1, 0))
            dp = dot(v, g, 1, 1)
            dp = dp - jnp.sum(p * dp, axis=0, keepdims=True)
            ds = (p * dp).astype(BF16)
            dks.append(dot(ds, q, 1, 0) * scale)
            dqs.append(dot(k, ds, 0, 0) * scale)
        dq = jnp.concatenate(dqs, axis=0).T
        pad = [jnp.zeros((PATCHES, out_ref.shape[2] - 3 * part), F32)]
        out_ref[n] = jnp.concatenate([dq] + dks + dvs + pad, axis=1).astype(BF16)


def attend_back(qkv, grad, heads, frame):
    groups, rows, cols = qkv.shape
    width = groups * heads * HEAD
    out = shape_of((groups, PATCHES, -(-cols // 128) * 128), BF16)
    return pl.pallas_call(
        functools.partial(attend_back_kernel, heads),
        grid=(1,),
        in_specs=[
            pl.BlockSpec((groups, PATCHES, cols), lambda i: (0, frame, 0)),
            pl.BlockSpec((PATCHES, width), lambda i: (frame, 0)),
        ],
        out_specs=pl.BlockSpec(out.shape, lambda i: (0, 0, 0)),
        out_shape=out,
        compiler_params=params(),
        cost_estimate=cost(),
        name="attend_back",
    )(qkv, grad)


class Sent:
    def __init__(self, *values):
        self.pending = list(values)

    def take(self, got):
        self.got = got
        self.pending = []


def land(sents, *ties):
    sents = [sent for sent in sents if sent.pending]
    pending = [value for sent in sents for value in sent.pending]
    values = list(tied(*pending, *ties))
    for sent in sents:
        count = len(sent.pending)
        sent.take(values[:count])
        values = values[count:]
    return values


class Gather:
    def __init__(self, shard, low, high):
        self.low = low
        self.depth = high - low
        self.cut = max(16, self.depth // 2 // 16 * 16)
        wide = [("wide", bit) for bit in reversed(bits_of(lax.axis_size("wide")))]
        narrow = [("narrow", bit) for bit in reversed(bits_of(lax.axis_size("narrow")))]
        self.core = wide[-1]
        self.front = wide[:-1]
        self.orders = [narrow, narrow[::-1]]
        self.parts = [shard[low:high][None]]
        self.stage = 0
        self.stages = len(self.front) + len(narrow)
        self.pending = []
        self.cored = []

    def start(self):
        if self.stage < len(self.front):
            keys = [self.front[self.stage]]
        else:
            keys = [order[self.stage - len(self.front)] for order in self.orders]
        self.pending = [swap(part, *key) for part, key in zip(self.parts, keys)]
        return self

    def take(self, got):
        self.pending = []
        self.stage += 1
        if self.stage == self.stages:
            self.near, self.far = self.parts, list(got)
        else:
            blocks = [jnp.concatenate([part, new], axis=0) for part, new in zip(self.parts, got)]
            if self.stage == len(self.front):
                block = blocks[0]
                blocks = [block[:, : self.cut], block[:, self.cut :]]
            self.parts = blocks

    def across(self):
        blocks = self.parts if self.stage < self.stages else self.far
        sent = Sent(*[swap(block, *self.core) for block in blocks])
        self.cored.append(sent)
        return sent

    def finish(self):
        near_core, far_core = self.cored[0].got, self.cored[1].got
        self.arrays = []
        for part in range(2):
            self.arrays += [self.near[part], self.far[part], near_core[part], far_core[part]]

    def ranges(self):
        return [(0, self.cut), (self.cut, self.depth - self.cut)]

    def entries(self, n, shift):
        found = []
        for w in range(lax.axis_size("wide")):
            for part, (offset, size) in enumerate(self.ranges()):
                keys = self.front + self.orders[part]
                flips = [(n if axis == "narrow" else w) & bit for axis, bit in keys]
                index = sum(1 << j for j, flip in enumerate(flips[:-1]) if flip)
                which = 4 * part + 2 * bool(w & self.core[1]) + bool(flips[-1])
                found.append((shift + which, index, w, self.low + offset, size))
        return found

    def assembled(self):
        pieces = []
        for part in range(2):
            near, far, near_core, far_core = self.arrays[4 * part : 4 * part + 4]
            block = jnp.stack([jnp.stack([near, far]), jnp.stack([near_core, far_core])])
            keys = [self.core] + (self.front + self.orders[part])[::-1]
            block = block.reshape([2] * len(keys) + list(block.shape[-2:]))
            wanted = [("narrow", bit) for bit in reversed(bits_of(lax.axis_size("narrow")))]
            wanted += self.front + [self.core]
            block = block.transpose([keys.index(key) for key in wanted] + [len(keys), len(keys) + 1])
            for dim, key in enumerate(wanted):
                if key[0] == "wide":
                    block = jnp.where(my_bit(*key) == 1, jnp.flip(block, dim), block)
            pieces.append(block)
        block = jnp.concatenate(pieces, axis=-2)
        return block.reshape(
            lax.axis_size("narrow"), lax.axis_size("wide"), self.depth, block.shape[-1]
        )


class Weight:
    def __init__(self, *gathers):
        groups, blocks = lax.axis_size("narrow"), lax.axis_size("wide")
        self.depth = sum(g.depth for g in gathers)
        self.cols = gathers[0].arrays[0].shape[-1]
        sizes = [size for g in gathers for pair in g.ranges() for size in pair]
        if any(size % 16 for size in sizes):
            block = jnp.concatenate([g.assembled() for g in gathers], axis=2)
            self.arrays = [block.reshape(groups, blocks * self.depth, self.cols)]
            self.plan = [[(0, n, None, 0, 0)] for n in range(groups)]
        else:
            self.arrays, self.plan = [], [[] for n in range(groups)]
            for g in gathers:
                for n in range(groups):
                    self.plan[n] += g.entries(n, len(self.arrays))
                self.arrays += g.arrays


def stream(step, weight, me, refs, buffer, sems):
    plan = weight.plan

    def issue(n):
        for which, index, w, offset, size in plan[n]:
            if w is None:
                target = buffer.at[n % 2]
            else:
                row = pl.multiple_of((me ^ w) * weight.depth + offset, 16)
                target = buffer.at[n % 2, pl.ds(row, size)]
            pltpu.make_async_copy(refs[which].at[index], target, sems.at[n % 2]).start()

    for n in range(len(plan)):

        @pl.when(step == n)
        def _():
            if n == 0:
                issue(0)
            if n + 1 < len(plan):
                issue(n + 1)

    slot = step % 2
    pltpu.make_async_copy(buffer.at[slot], buffer.at[slot], sems.at[slot]).wait()
    return buffer.at[slot]


def weight_call(body, weight, ins, in_specs, outs, out_specs, scratch, name):
    count, groups = len(weight.arrays), len(weight.plan)
    width = lax.axis_size("wide") * weight.depth

    def kernel(me_ref, *refs):
        step = pl.program_id(0)
        in_refs = refs[: len(ins)]
        weight_refs = refs[len(ins) : len(ins) + count]
        out_refs = refs[len(ins) + count : len(ins) + count + len(outs)]
        buffer, sems = refs[len(ins) + count + len(outs) :][:2]
        scratch_refs = refs[len(ins) + count + len(outs) + 2 :]
        w = stream(step, weight, me_ref[0], weight_refs, buffer, sems)
        body(step, in_refs, w, out_refs, scratch_refs)

    me = lax.axis_index("wide").astype(jnp.int32)[None]
    return pl.pallas_call(
        kernel,
        grid_spec=pltpu.PrefetchScalarGridSpec(
            num_scalar_prefetch=1,
            grid=(groups,),
            in_specs=list(in_specs) + [pl.BlockSpec(memory_space=pl.ANY)] * count,
            out_specs=list(out_specs),
            scratch_shapes=[
                pltpu.VMEM((2, width, weight.cols), BF16),
                pltpu.SemaphoreType.DMA((2,)),
            ]
            + list(scratch),
        ),
        out_shape=list(outs),
        compiler_params=params(),
        cost_estimate=cost(),
        name=name,
    )(me, *ins, *weight.arrays)


def project_call(weight, tokens, modes, bias, part):
    rows, width = tokens.shape
    spans, span = modes.shape[0], rows // modes.shape[0]
    groups = len(weight.plan)
    outs = [
        shape_of((rows, width), BF16),
        shape_of((groups, rows, 3 * part), BF16),
        shape_of((width, groups * part), BF16),
    ]

    def body(step, ins, w, out, scratch):
        tokens_ref, modes_ref, bias_ref = ins
        hidden_ref, qkv_ref, merge_ref = out

        @pl.when(step == 0)
        def _():
            for s in range(spans):
                at = slice(s * span, (s + 1) * span)
                unused, normed = normalize(tokens_ref[at, :].astype(F32))
                hidden = normed * (1.0 + modes_ref[s, 1:2]) + modes_ref[s, 0:1]
                hidden_ref[at, :] = hidden.astype(BF16)

        qkv_ref[0] = (dot(hidden_ref[...], w[:, : 3 * part], 1, 0) + bias_ref[0]).astype(BF16)
        for n in range(groups):

            @pl.when(step == n)
            def _():
                merge_ref[:, n * part : (n + 1) * part] = w[:, 3 * part :]

    return weight_call(
        body,
        weight,
        [tokens, modes, bias],
        [whole(tokens), whole(modes), along(bias)],
        outs,
        [whole(outs[0]), along(outs[1]), whole(outs[2])],
        [],
        "project",
    )


def merge_kernel(attended_ref, weight_ref, tokens_ref, modes_ref, bias_ref, branch_ref, hidden_ref):
    branch = dot(attended_ref[...], weight_ref[...], 1, 1) + bias_ref[...]
    branch_ref[...] = branch
    middle = tokens_ref[...].astype(F32) + modes_ref[0, 2:3] * branch
    unused, normed = normalize(middle)
    hidden_ref[...] = (normed * (1.0 + modes_ref[0, 4:5]) + modes_ref[0, 3:4]).astype(BF16)


def merge_call(attended, weight, tokens, modes, bias):
    rows, width = tokens.shape
    spans, span = modes.shape[0], rows // modes.shape[0]
    block = pl.BlockSpec((span, width), lambda i: (i, 0))
    outs = [shape_of((rows, width), F32), shape_of((rows, width), BF16)]
    return pl.pallas_call(
        merge_kernel,
        grid=(spans,),
        in_specs=[block, whole(weight), block, along(modes), whole(bias)],
        out_specs=[block, block],
        out_shape=outs,
        compiler_params=params(),
        cost_estimate=cost(),
        name="merge",
    )(attended, weight, tokens, modes, bias)


def up_call(weight, hidden, bias):
    rows, width = hidden.shape
    groups, units = len(weight.plan), weight.cols
    outs = [shape_of((groups, rows, units), BF16)] * 2

    def body(step, ins, w, out, scratch):
        hidden_ref, bias_ref = ins
        gelu, slope = gelu_both(dot(hidden_ref[...], w[...], 1, 0) + bias_ref[0])
        out[0][0] = gelu.astype(BF16)
        out[1][0] = slope.astype(BF16)

    return weight_call(
        body,
        weight,
        [hidden, bias],
        [whole(hidden), along(bias)],
        outs,
        [along(outs[0]), along(outs[1])],
        [],
        "up",
    )


def down_call(weight, gelu, tokens, branch, modes, bias, grad):
    rows, width = tokens.shape
    spans, span = modes.shape[0], rows // modes.shape[0]
    groups, units = len(weight.plan), weight.cols
    outs = [shape_of((rows, width), BF16), shape_of((spans, 1, width), F32)]

    def body(step, ins, w, out, scratch):
        gelu_ref, tokens_ref, branch_ref, modes_ref, bias_ref, grad_ref = ins
        total = scratch[0]
        @pl.when(step == 0)
        def _():
            total[...] = dot(gelu_ref[0], w[...], 1, 1)

        @pl.when((step > 0) & (step < groups - 1))
        def _():
            total[...] += dot(gelu_ref[0], w[...], 1, 1)

        @pl.when(step == groups - 1)
        def _():
            for s in range(spans):
                at = slice(s * span, (s + 1) * span)
                summed = total[at, :] + dot(gelu_ref[0, at, :], w[...], 1, 1)
                other = summed + bias_ref[...]
                middle = tokens_ref[at, :].astype(F32) + modes_ref[s, 2:3] * branch_ref[at, :]
                out[0][at, :] = (middle + modes_ref[s, 5:6] * other).astype(BF16)
                out[1][s] = jnp.sum(grad_ref[at, :].astype(F32) * other, axis=0, keepdims=True)

    return weight_call(
        body,
        weight,
        [gelu, tokens, branch, modes, bias, grad],
        [along(gelu)] + [whole(a) for a in (tokens, branch, modes, bias, grad)],
        outs,
        [whole(outs[0]), whole(outs[1])],
        [pltpu.VMEM((rows, width), F32)],
        "down",
    )


def gelu_back_call(weight, grad, slope):
    rows, width = grad.shape
    groups, units = len(weight.plan), weight.cols
    outs = [shape_of((groups, rows, units), BF16), shape_of((groups, 1, units), F32)]

    def body(step, ins, w, out, scratch):
        grad_ref, slope_ref = ins
        upper = (dot(grad_ref[...], w[...], 1, 0) * slope_ref[0].astype(F32)).astype(BF16)
        out[0][0] = upper
        out[1][0] = jnp.sum(upper.astype(F32), axis=0, keepdims=True)

    return weight_call(
        body,
        weight,
        [grad, slope],
        [whole(grad), along(slope)],
        outs,
        [along(outs[0]), along(outs[1])],
        [],
        "gelu_back",
    )


def up_back_call(weight, upper, tokens, branch, modes, grad):
    rows, width = tokens.shape
    spans, span = modes.shape[0], rows // modes.shape[0]
    groups, units = len(weight.plan), weight.cols
    outs = [
        shape_of((rows, width), F32),
        shape_of((rows, width), BF16),
        shape_of((spans, 3, width), F32),
        shape_of((1, width), F32),
    ]

    def body(step, ins, w, out, scratch):
        upper_ref, tokens_ref, branch_ref, modes_ref, grad_ref = ins
        middle_ref, merged_ref, sums_ref, bias_ref = out
        total = scratch[0]
        @pl.when(step == 0)
        def _():
            total[...] = dot(upper_ref[0], w[...], 1, 1)

        @pl.when((step > 0) & (step < groups - 1))
        def _():
            total[...] += dot(upper_ref[0], w[...], 1, 1)

        @pl.when(step == groups - 1)
        def _():
            for s in range(spans):
                at = slice(s * span, (s + 1) * span)
                summed = total[at, :] + dot(upper_ref[0, at, :], w[...], 1, 1)
                branch = branch_ref[at, :]
                gate = modes_ref[s, 2:3]
                inverse, normed = normalize(tokens_ref[at, :].astype(F32) + gate * branch)
                hidden = summed
                back = norm_back(hidden * (1.0 + modes_ref[s, 4:5]), normed, inverse)
                middle = grad_ref[at, :].astype(F32) + back
                gated = gate * middle
                middle_ref[at, :] = middle
                merged_ref[at, :] = gated.astype(BF16)
                sums_ref[s, 0:1] = jnp.sum(middle * branch, axis=0, keepdims=True)
                sums_ref[s, 1:2] = jnp.sum(hidden, axis=0, keepdims=True)
                sums_ref[s, 2:3] = jnp.sum(hidden * normed, axis=0, keepdims=True)
                here = jnp.sum(gated, axis=0, keepdims=True)
                bias_ref[...] = here if s == 0 else bias_ref[...] + here

    return weight_call(
        body,
        weight,
        [upper, tokens, branch, modes, grad],
        [along(upper)] + [whole(a) for a in (tokens, branch, modes, grad)],
        outs,
        [whole(a) for a in outs],
        [pltpu.VMEM((rows, width), F32)],
        "up_back",
    )


def project_back_call(weight, qkv_grads, tokens, middle, modes, cols):
    rows, width = tokens.shape
    spans, span = modes.shape[0], rows // modes.shape[0]
    groups, pieces = len(weight.plan), len(qkv_grads)
    outs = [
        shape_of((rows, width), F32),
        shape_of((spans, 2, width), F32),
        shape_of((groups, 1, cols), F32),
    ]

    def body(step, ins, w, out, scratch):
        tokens_ref, middle_ref, modes_ref = ins[pieces:]
        tokens_grad_ref, sums_ref, bias_ref = out
        total = scratch[0]
        grad = jnp.concatenate([ref[0, :, :cols] for ref in ins[:pieces]], axis=0)
        bias_ref[0] = jnp.sum(grad.astype(F32), axis=0, keepdims=True)

        @pl.when(step == 0)
        def _():
            total[...] = dot(grad, w[:, :cols], 1, 1)

        @pl.when((step > 0) & (step < groups - 1))
        def _():
            total[...] += dot(grad, w[:, :cols], 1, 1)

        @pl.when(step == groups - 1)
        def _():
            for s in range(spans):
                at = slice(s * span, (s + 1) * span)
                inverse, normed = normalize(tokens_ref[at, :].astype(F32))
                hidden = total[at, :] + dot(grad[at], w[:, :cols], 1, 1)
                back = norm_back(hidden * (1.0 + modes_ref[s, 1:2]), normed, inverse)
                tokens_grad_ref[at, :] = middle_ref[at, :] + back
                sums_ref[s, 0:1] = jnp.sum(hidden, axis=0, keepdims=True)
                sums_ref[s, 1:2] = jnp.sum(hidden * normed, axis=0, keepdims=True)

    return weight_call(
        body,
        weight,
        [*qkv_grads, tokens, middle, modes],
        [along(a) for a in qkv_grads] + [whole(a) for a in (tokens, middle, modes)],
        outs,
        [whole(outs[0]), whole(outs[1]), along(outs[2])],
        [pltpu.VMEM((rows, width), F32)],
        "project_back",
    )


def put_turned(depth, side, block, own_ref, other_ref):
    turned_block = block.T
    for z in range(own_ref.shape[0]):
        even = turned_block[2 * z * depth : (2 * z + 1) * depth]
        odd = turned_block[(2 * z + 1) * depth : (2 * z + 2) * depth]
        own_ref[z] = jnp.where(side == 1, odd, even)
        other_ref[z] = jnp.where(side == 1, even, odd)


def turn_kernel(depth, me_ref, block_ref, own_ref, other_ref):
    put_turned(depth, me_ref[0] & 1, block_ref[...], own_ref, other_ref)


def turn(block):
    rows, width = block.shape
    blocks = lax.axis_size("wide")
    out = shape_of((blocks // 2, width // blocks, rows), BF16)
    me = lax.axis_index("wide").astype(jnp.int32)[None]
    own, other = pl.pallas_call(
        functools.partial(turn_kernel, width // blocks),
        grid_spec=pltpu.PrefetchScalarGridSpec(
            num_scalar_prefetch=1, grid=(1,), in_specs=[whole(block)], out_specs=[whole(out)] * 2
        ),
        out_shape=[out, out],
        compiler_params=params(24),
        cost_estimate=cost(),
        name="turn",
    )(me, block)
    return own, other


def weight_grad_call(lefts, grads, merged, attended, cols, low, high):
    zs, depth, rows = lefts[0].shape
    groups, size = grads[0].shape[0], high - low
    width = 2 * zs * depth
    cut = max(16, size // 2 // 16 * 16)
    part = width // groups if merged else 0
    half = groups // 2
    outs = []
    for height in (cut, cut, size - cut, size - cut):
        outs.append(shape_of((half, zs, height, cols + part), BF16))
    ins = [*lefts, *merged, *grads, *attended]
    count = len(lefts)

    def kernel(*refs):
        step = pl.program_id(0)
        in_refs, out_refs, scratch = refs[: len(ins)], refs[len(ins) : len(ins) + 4], refs[len(ins) + 4 :]
        grad_refs = in_refs[count + len(merged) : count + len(merged) + len(grads)]
        attended_refs = in_refs[count + len(merged) + len(grads) :]

        @pl.when(step == 0)
        def _():
            for i in range(count + len(merged)):
                target, at = scratch[i // count], (i % count) * rows
                for z in range(zs):
                    target[z * size : (z + 1) * size, at : at + rows] = in_refs[i][z, low:high]
            if merged:
                both = jnp.concatenate([ref[...] for ref in attended_refs], axis=0)
                scratch[2][...] = dot(scratch[1][...], both, 1, 0).astype(BF16)

        both = jnp.concatenate([ref[0, :, :cols] for ref in grad_refs], axis=0)
        result = dot(scratch[0][...], both, 1, 0).astype(BF16)
        for n in range(groups):

            @pl.when(step == n)
            def _():
                value = result
                if merged:
                    value = jnp.concatenate([value, scratch[2][:, n * part : (n + 1) * part]], axis=1)
                first = out_refs[0] if n < half else out_refs[1]
                second = out_refs[2] if n % 2 == 0 else out_refs[3]
                for z in range(zs):
                    first[0, z] = value[z * size : z * size + cut]
                    second[0, z] = value[z * size + cut : (z + 1) * size]

    scratch = [pltpu.VMEM((zs * size, count * rows), BF16)]
    if merged:
        scratch += [pltpu.VMEM((zs * size, count * rows), BF16), pltpu.VMEM((zs * size, width), BF16)]
    rest = (0, 0, 0)
    out_specs = [
        pl.BlockSpec((1,) + outs[0].shape[1:], lambda i: (jnp.minimum(i, half - 1),) + rest),
        pl.BlockSpec((1,) + outs[1].shape[1:], lambda i: (jnp.maximum(i - half, 0),) + rest),
        pl.BlockSpec((1,) + outs[2].shape[1:], lambda i: (i // 2,) + rest),
        pl.BlockSpec((1,) + outs[3].shape[1:], lambda i: (i // 2,) + rest),
    ]
    return pl.pallas_call(
        kernel,
        grid=(groups,),
        in_specs=[whole(a) for a in (*lefts, *merged)]
        + [along(a) for a in grads]
        + [whole(a) for a in attended],
        out_specs=out_specs,
        scratch_shapes=scratch,
        out_shape=outs,
        compiler_params=params(),
        cost_estimate=cost(),
        name="weight_grad",
    )(*ins)


def plus(a, b):
    return (a.astype(F32) + b.astype(F32)).astype(BF16)


class Scatter:
    def __init__(self, first_kept, first_sent, second_kept, second_sent):
        narrow = list(reversed(bits_of(lax.axis_size("narrow"))))
        self.orders = [narrow, narrow[::-1]]
        self.left = [list(narrow), list(narrow)]
        self.front = list(bits_of(lax.axis_size("wide")))[1:]
        self.stage = 0
        self.stages = len(narrow) + len(self.front)
        self.kept, self.pending = [], []
        sides = ((first_kept, first_sent), (second_kept, second_sent))
        for part, (kept, sent) in enumerate(sides):
            bit = self.orders[part][0]
            self.left[part].remove(bit)
            self.kept.append(kept.reshape([2] * (len(narrow) - 1) + list(kept.shape[1:])))
            self.pending.append(swap(sent.reshape(self.kept[-1].shape), "narrow", bit))

    def take(self, got):
        kept, narrow = self.kept, len(self.orders[0])
        self.stage += 1
        if self.stage < narrow:
            self.kept, self.pending = [], []
            for part, order in enumerate(self.orders):
                bit = order[self.stage]
                dim = self.left[part].index(bit)
                self.left[part].remove(bit)
                stay, go = [
                    plus(
                        lax.index_in_dim(kept[part], side, dim, False),
                        lax.index_in_dim(got[part], side, dim, False),
                    )
                    for side in (0, 1)
                ]
                self.kept.append(stay)
                self.pending.append(swap(go, "narrow", bit))
        elif self.stage < self.stages:
            bit = self.front[self.stage - narrow]
            mine = my_bit("wide", bit)
            dim = len(self.front) - 1 - (self.stage - narrow)
            sides = []
            for side in (mine, 1 - mine):
                blocks = []
                for a, b in zip(kept, got):
                    if self.stage == narrow:
                        shape = [2] * len(self.front) + list(a.shape[1:])
                        a, b = a.reshape(shape), b.reshape(shape)
                    blocks.append(
                        plus(
                            lax.dynamic_index_in_dim(a, side, dim, False),
                            lax.dynamic_index_in_dim(b, side, dim, False),
                        )
                    )
                sides.append(jnp.concatenate(blocks, axis=-2) if len(blocks) > 1 else blocks[0])
            self.kept = [sides[0]]
            self.pending = [swap(sides[1], "wide", bit)]
        else:
            self.result = kept[0].astype(F32) + got[0].astype(F32)
            self.pending = []


def spread(block, axis, bits):
    blocks = [block]
    for index in range(1, 1 << len(bits)):
        mask = sum(bit for j, bit in enumerate(bits) if index >> j & 1)
        blocks.append(swap(block, axis, mask))
    return blocks


def tree_sum(blocks):
    while len(blocks) > 1:
        blocks = [blocks[i] + blocks[i + 1] for i in range(0, len(blocks), 2)]
    return blocks[0]


def unpack_call(span_clip, narrow_me, clips, blocks, grad):
    spans = span_clip.shape[0]
    rows, width = grad.shape
    span = rows // spans
    groups = sum(block.shape[0] for block in blocks)
    height, part = blocks[0].shape[1:]
    at = 6 * clips
    units = (height - at - 4) * part
    wide = lax.axis_size("wide")
    outs = [
        shape_of((spans, 6, width), F32),
        shape_of((2, 1, width), F32),
        shape_of((groups, 1, 3 * part), F32),
        shape_of((groups, 1, units), F32),
        shape_of((rows, width), BF16),
        shape_of((1, width), F32),
        shape_of((wide // 2, width // wide, rows), BF16),
        shape_of((wide // 2, width // wide, rows), BF16),
    ]

    def kernel(clip_ref, me_ref, *refs):
        block_refs, grad_ref = refs[: len(blocks)], refs[len(blocks)]
        modes_ref, bias_ref, qkv_ref, up_ref, core_ref, sum_ref, own_ref, other_ref = refs[len(blocks) + 1 :]
        places = [(ref, i) for ref, block in zip(block_refs, blocks) for i in range(block.shape[0])]
        for rel, (ref, i) in enumerate(places):
            owner = me_ref[0] ^ rel
            found = []
            for s in range(spans):
                for k in range(6):
                    found.append(ref[i, pl.ds(k * clips + clip_ref[s], 1), :])
            for n in range(groups):

                @pl.when(owner == n)
                def _():
                    lanes = slice(n * part, (n + 1) * part)
                    for s in range(spans):
                        for k in range(6):
                            modes_ref[s, k : k + 1, lanes] = found[6 * s + k]
                    for k in range(2):
                        bias_ref[k, :, lanes] = ref[i, at + 2 + k : at + 3 + k, :]

            qkv_ref[rel] = jnp.concatenate(
                [ref[i, at : at + 1, :], jnp.zeros((1, part), F32), ref[i, at + 1 : at + 2, :]], axis=1
            )
            for j in range(units // part):
                up_ref[rel, :, j * part : (j + 1) * part] = ref[i, at + 4 + j : at + 5 + j, :]
        for s in range(spans):
            lines = slice(s * span, (s + 1) * span)
            gated = modes_ref[s, 5:6] * grad_ref[lines, :].astype(F32)
            core_ref[lines, :] = gated.astype(BF16)
            here = jnp.sum(gated, axis=0, keepdims=True)
            sum_ref[...] = here if s == 0 else sum_ref[...] + here
        put_turned(width // wide, me_ref[1] & 1, core_ref[...], own_ref, other_ref)

    me = jnp.stack([narrow_me, lax.axis_index("wide")]).astype(jnp.int32)
    return pl.pallas_call(
        kernel,
        grid_spec=pltpu.PrefetchScalarGridSpec(
            num_scalar_prefetch=2,
            grid=(1,),
            in_specs=[whole(a) for a in (*blocks, grad)],
            out_specs=[whole(a) for a in outs],
        ),
        out_shape=outs,
        compiler_params=params(32),
        cost_estimate=cost(),
        name="unpack",
    )(span_clip, me, *blocks, grad)


def pack_call(span_clip, narrow_me, clips, sums_a, sums_b, sums_g, merge_bias, down_bias, qkv_sums, up_bias):
    spans, unused, width = sums_a.shape
    groups = qkv_sums.shape[0]
    part, units = width // groups, up_bias.shape[2]
    at = 6 * clips
    height = at + 4 + units // part
    outs = [shape_of((groups // 2, height, part), F32)] * 2
    ins = [sums_a, sums_b, sums_g, merge_bias, down_bias, qkv_sums, up_bias]

    def kernel(clip_ref, me_ref, a_ref, b_ref, g_ref, merge_ref, down_ref, qkv_ref, up_ref, *refs):
        total = refs[2]
        out_refs = [refs[rel // (groups // 2)].at[rel % (groups // 2)] for rel in range(groups)]
        total[...] = jnp.zeros_like(total)
        for s in range(spans):
            rows = [a_ref[s, 0:1], a_ref[s, 1:2]] + [b_ref[s, i : i + 1] for i in range(3)]
            rows.append(g_ref[s, 0:1])
            for k in range(6):
                row = pl.ds(k * clips + clip_ref[s], 1)
                total[row, :] += rows[k]
        total[at : at + 1, :] = merge_ref[...]
        total[at + 1 : at + 2, :] = down_ref[...]
        for rel in range(groups):
            owner = me_ref[0] ^ rel
            for n in range(groups):

                @pl.when(owner == n)
                def _():
                    own = total[:, n * part : (n + 1) * part]
                    out_refs[rel][:at, :] = own[:at]
                    out_refs[rel][at + 2 : at + 4, :] = own[at : at + 2]

            out_refs[rel][at : at + 1, :] = qkv_ref[rel, :, :part]
            out_refs[rel][at + 1 : at + 2, :] = qkv_ref[rel, :, 2 * part :]
            for j in range(units // part):
                out_refs[rel][at + 4 + j : at + 5 + j, :] = up_ref[rel, :, j * part : (j + 1) * part]

    return pl.pallas_call(
        kernel,
        grid_spec=pltpu.PrefetchScalarGridSpec(
            num_scalar_prefetch=2,
            grid=(1,),
            in_specs=[whole(a) for a in ins],
            out_specs=[whole(a) for a in outs],
            scratch_shapes=[pltpu.VMEM((at + 8, width), F32)],
        ),
        out_shape=outs,
        compiler_params=params(16),
        name="pack",
    )(span_clip, narrow_me.astype(jnp.int32)[None], *ins)


def sum_over(block, axis):
    for bit in bits_of(lax.axis_size(axis)):
        block = block + swap(block, axis, bit)
    return block


def collect(block, axis):
    block = block[None]
    for bit in bits_of(lax.axis_size(axis)):
        block = jnp.concatenate([block, swap(block, axis, bit)], axis=0)
    return block


def turned(block, axis):
    count = lax.axis_size(axis)
    bits = bits_of(count)
    rest = block.shape[1:]
    block = block.reshape([2] * len(bits) + list(rest))
    for dim, bit in enumerate(reversed(bits)):
        block = jnp.where(my_bit(axis, bit) == 1, jnp.flip(block, dim), block)
    return block.reshape((count,) + rest)


def share(block, count):
    for bit in bits_of(count):
        groups, rows, cols = block.shape
        pair = block.reshape(groups // 2, 2, rows, cols)
        kept, got = pair[:, 0], swap(pair[:, 1], "narrow", bit)
        mine = my_bit("narrow", bit) == 1
        block = jnp.concatenate([jnp.where(mine, got, kept), jnp.where(mine, kept, got)], axis=1)
    return block


def unshare(block, count):
    for bit in reversed(bits_of(count)):
        groups, rows, cols = block.shape
        pair = block.reshape(groups, 2, rows // 2, cols)
        mine = my_bit("narrow", bit)
        kept = lax.dynamic_index_in_dim(pair, mine, 1, True)
        got = swap(lax.dynamic_index_in_dim(pair, 1 - mine, 1, True), "narrow", bit)
        block = jnp.concatenate([kept, got], axis=1).reshape(2 * groups, rows // 2, cols)
    return block


def shards(
    tokens,
    condition,
    frame_clip,
    mod_weight,
    mod_bias,
    project_weight,
    project_bias,
    merge_weight,
    merge_bias,
    up_weight,
    up_bias,
    down_weight,
    down_bias,
    out_cotangent,
):
    rows, width = tokens.shape
    wide_count, narrow_count = lax.axis_size("wide"), lax.axis_size("narrow")
    wide_me, narrow_me = lax.axis_index("wide"), lax.axis_index("narrow")
    depth = width // wide_count
    part = width // narrow_count
    units = up_weight.shape[1]
    heads = part // HEAD
    clips = condition.shape[0]
    span = math.gcd(rows, PATCHES)
    spans = rows // span
    sharing = PATCHES // span

    def twin(*blocks):
        return Sent(*[swap(block, "wide", 1) for block in blocks])

    def hop(block, axis, bit):
        return Sent(swap(block, axis, bit))

    attn = Gather(
        jnp.concatenate([project_weight.reshape(depth, 3 * part), merge_weight.T], axis=1), 0, depth
    )
    up, down = Gather(up_weight, 0, depth), Gather(down_weight.T, 0, depth)
    attn.start()
    z_bits = bits_of(wide_count)[1:]
    narrow_bits = bits_of(narrow_count)
    active = jax.nn.silu(condition).astype(BF16)
    active_mine = lax.dynamic_slice_in_dim(active, wide_me * depth, depth, 1)
    mode_part = jnp.einsum("cd,dki->kci", active_mine, mod_weight, preferred_element_type=F32)
    mode_part = mode_part + swap(mode_part, "wide", 1)
    for bit in z_bits:
        sent = hop(mode_part, "wide", bit)
        if bit == z_bits[0]:
            (mode_part,) = land([sent, attn], mode_part)
        else:
            mode_part, *attn.parts = land([sent], mode_part, *attn.parts)
        mode_part = mode_part + sent.got[0]
    unit_rows = units // part
    at = 6 * clips
    small = jnp.concatenate(
        [
            (mode_part + mod_bias.astype(F32)[:, None]).reshape(at, part),
            project_bias.astype(F32),
            merge_bias.astype(F32)[None],
            down_bias.astype(F32)[None],
            up_bias.astype(F32).reshape(unit_rows, part),
        ],
        axis=0,
    )
    span_frame = (narrow_me * rows + jnp.arange(spans, dtype=jnp.int32) * span) // PATCHES
    span_clip = jnp.sum(
        jnp.where(
            span_frame[:, None] == jnp.arange(frame_clip.shape[0], dtype=jnp.int32)[None],
            frame_clip[None],
            0,
        ),
        axis=1,
    )
    attn.start()
    sent = Sent(*spread(small, "narrow", narrow_bits)[1:])
    small, span_clip, *up.parts = land([sent, attn], small, span_clip, *up.parts)
    while attn.stage < len(attn.front):
        attn.start()
        land([attn])
    attn.start()
    up.start()
    modes, out_bias, qkv_bias, up_bias_all, core_grad, down_bias_grad, core_own, core_other = unpack_call(
        span_clip, narrow_me, clips, [block[None] for block in (small, *sent.got)], out_cotangent
    )
    (modes,) = land([attn, up], modes)
    while attn.stage < attn.stages - 1:
        attn.start()
        up.start()
        land([attn, up])
    attn.start()
    if up.stage < len(up.front):
        up.start()
    attn_near = attn.across()
    modes, *down.parts = land([attn, up, attn_near], modes, *down.parts)
    while up.stage < len(up.front):
        up.start()
        land([up])
    attn_far = attn.across()
    up.start()
    down.start()
    (modes,) = land([attn_far], modes)
    attn.finish()

    attn_w = Weight(attn)
    hidden_a, qkv, merge_w = project_call(attn_w, tokens, modes, qkv_bias, part)
    qkv, hidden_a = land([up, down], qkv, hidden_a)
    while up.stage < up.stages - 1:
        up.start()
        (qkv,) = land([up], qkv)
    up.start()
    down.start()
    up_near = up.across()
    qkv_frames = share(qkv, sharing)
    attended = attend(qkv_frames, heads)
    if sharing > 1:
        attended = attended.reshape(rows * sharing, narrow_count // sharing, part)
        attended = unshare(attended.transpose(1, 0, 2), sharing)
        attended = attended.transpose(1, 0, 2).reshape(rows, width)
    attended, hidden_a = land([down, up_near], attended, hidden_a)
    while down.stage < len(down.front):
        down.start()
        (attended,) = land([down], attended)
    down.start()
    hidden_own, hidden_other = turn(hidden_a)
    hidden_twin = twin(hidden_other)
    branch_a, hidden_b = merge_call(attended, merge_w, tokens, modes, out_bias[0])
    hidden_b, attended = land([up, down, hidden_twin], hidden_b, attended)
    while down.stage < down.stages - 1:
        down.start()
        (hidden_b,) = land([down], hidden_b)
    up_far = up.across()
    down.start()
    (hidden_b,) = land([up_far], hidden_b)
    up.finish()
    down_near = down.across()
    up_w = Weight(up)
    gelu, slope = up_call(up_w, hidden_b, up_bias_all)

    gelu, slope, hidden_b = land([down, down_near], gelu, slope, hidden_b)
    down_far = down.across()
    sent_parts = weight_grad_call([core_other], [gelu], [], [], units, 0, depth)
    slope, core_own, *sent_parts = land([down_far], slope, core_own, *sent_parts)
    down.finish()
    down_cross = twin(*sent_parts)
    kept_parts = weight_grad_call([core_own], [gelu], [], [], units, 0, depth)
    slope, hidden_b, *kept_parts = land([], slope, hidden_b, *kept_parts)
    hidden_b_own, hidden_b_other = turn(hidden_b)
    hidden_b_twin = twin(hidden_b_other)
    down_w = Weight(down)
    upper_grad, up_bias_grad = gelu_back_call(down_w, core_grad, slope)
    upper_grad, attended, *kept_parts = land(
        [down_cross, hidden_b_twin], upper_grad, attended, *kept_parts
    )
    upper_twin = twin(upper_grad)
    attended_twin = twin(attended)
    down_scatter = Scatter(*[plus(a, b) for a, b in zip(kept_parts, down_cross.got)])
    middle_grad, merged_grad, sums_b, merge_bias_grad = up_back_call(
        up_w, upper_grad, tokens, branch_a, modes, out_cotangent
    )
    merged_grad, upper_grad = land([upper_twin, attended_twin], merged_grad, upper_grad)
    merged_own, merged_other = turn(merged_grad)
    merged_twin = twin(merged_other)
    up_parts = weight_grad_call(
        [hidden_b_own, hidden_b_twin.got[0]], [upper_grad, upper_twin.got[0]], [], [], units, 0, depth
    )
    merged_grad, *up_parts = land([down_scatter, merged_twin], merged_grad, *up_parts)
    up_scatter = Scatter(*up_parts)

    attended_grad = jnp.dot(merged_grad, merge_w, preferred_element_type=F32).astype(BF16)
    if sharing > 1:
        attended_grad = attended_grad.reshape(rows, narrow_count, part).transpose(1, 0, 2)
        attended_grad = share(attended_grad, sharing).transpose(1, 0, 2)
        attended_grad = attended_grad.reshape(rows * sharing, width // sharing)
    qkv_grads, qkv_twins = [], []
    frames = rows * sharing // PATCHES
    for frame in range(frames):
        qkv_grad = attend_back(qkv_frames, attended_grad, heads, frame)
        scatters = [down_scatter] if frame == frames - 1 else []
        qkv_grad, attended_grad = land(scatters, qkv_grad, attended_grad)
        qkv_grads.append(qkv_grad)
        if sharing == 1:
            qkv_twins.append(twin(qkv_grad))
    if sharing > 1:
        qkv_grads = [unshare(jnp.concatenate(qkv_grads, axis=1), sharing)]
        qkv_twins = [twin(qkv_grads[0])]
    tokens_grad, sums_a, qkv_sums = project_back_call(
        attn_w, qkv_grads, tokens, middle_grad, modes, 3 * part
    )
    sums_a, *qkv_grads = land([up_scatter, down_scatter, *qkv_twins], sums_a, *qkv_grads)
    attn_parts = weight_grad_call(
        [hidden_own, hidden_twin.got[0]],
        qkv_grads + [sent.got[0] for sent in qkv_twins],
        [merged_own, merged_twin.got[0]],
        [attended, attended_twin.got[0]],
        3 * part,
        0,
        depth,
    )
    gelu, *attn_parts = land([up_scatter, down_scatter], gelu, *attn_parts)
    attn_scatter = Scatter(*attn_parts)
    output, sums_g = down_call(
        down_w, gelu, tokens, branch_a, modes, out_bias[1], out_cotangent
    )
    (sums_g,) = land([up_scatter], sums_g)

    lower, upper = pack_call(
        span_clip, narrow_me, clips, sums_a, sums_b, sums_g, merge_bias_grad, down_bias_grad,
        qkv_sums, up_bias_grad,
    )
    sent = hop(upper, "narrow", narrow_bits[-1])
    (lower,) = land([sent, up_scatter], lower)
    packed = lower + sent.got[0]
    for bit in reversed(narrow_bits[:-1]):
        packed = packed[:bit] + swap(packed[bit:], "narrow", bit)
    packed = packed[0]
    sent = hop(packed, "wide", 1)
    (packed,) = land([sent, attn_scatter], packed)
    packed = packed + sent.got[0]
    for bit in z_bits:
        sent = hop(packed, "wide", bit)
        (packed,) = land([sent], packed)
        packed = packed + sent.got[0]
    clip_slice = packed[:at].reshape(6, clips, part)
    active_grad = jnp.einsum(
        "kci,dki->cd", clip_slice, mod_weight.astype(F32), precision=lax.Precision.HIGHEST
    )
    for bit in narrow_bits:
        sent = hop(active_grad, "narrow", bit)
        (active_grad,) = land([sent] + ([attn_scatter] if bit == narrow_bits[-1] else []), active_grad)
        active_grad = active_grad + sent.got[0]
    active_grad = active_grad[None]
    for bit in bits_of(wide_count):
        sent = hop(active_grad, "wide", bit)
        (active_grad,) = land([sent], active_grad)
        active_grad = jnp.concatenate([active_grad, sent.got[0]], axis=0)
    active_grad = turned(active_grad, "wide").transpose(1, 0, 2).reshape(clips, width)
    unused, silu_pullback = jax.vjp(jax.nn.silu, condition)
    condition_grad = silu_pullback(active_grad)[0]
    mod_bias_grad = jnp.sum(clip_slice, axis=1)
    mod_weight_grad = jnp.einsum(
        "cd,kci->dki", active_mine.astype(F32), clip_slice, precision=lax.Precision.HIGHEST
    )

    for scatter in (down_scatter, up_scatter, attn_scatter):
        while scatter.stage < scatter.stages:
            land([scatter])
    attn_grad = attn_scatter.result
    return (
        output,
        tokens_grad,
        condition_grad,
        mod_weight_grad,
        mod_bias_grad,
        attn_grad[:, : 3 * part].reshape(depth, 3, part),
        packed[at : at + 2],
        attn_grad[:, 3 * part :].T,
        packed[at + 2],
        up_scatter.result,
        packed[at + 4 :].reshape(units),
        down_scatter.result.T,
        packed[at + 3],
    )


def solution(mesh):
    both = P(("wide", "narrow"), None)
    ins = (
        both,
        P(),
        P("wide"),
        P("wide", None, "narrow"),
        P(None, "narrow"),
        P("wide", None, "narrow"),
        P(None, "narrow"),
        P("narrow", "wide"),
        P("narrow"),
        P("wide", "narrow"),
        P("narrow"),
        P("narrow", "wide"),
        P("narrow"),
        both,
    )
    outs = (
        both,
        both,
        P(),
        P("wide", None, "narrow"),
        P(None, "narrow"),
        P("wide", None, "narrow"),
        P(None, "narrow"),
        P("narrow", "wide"),
        P("narrow"),
        P("wide", "narrow"),
        P("narrow"),
        P("narrow", "wide"),
        P("narrow"),
    )
    return jax.shard_map(shards, mesh=mesh, in_specs=ins, out_specs=outs, check_vma=False)
```

time: 852 us -> 538 us (0.63)
  waiting for transfers between devices: 354 us -> 172 us
  Pallas kernels: 56.1 us -> 226 us
  matrix products: 150 us -> 6.53 us
  other arithmetic: 132 us -> 39 us
  local copies, waits for them, and re-layouts: 77.4 us -> 23.7 us
    ppermute x60 -> x76, waiting for transfers between devices: 354 us -> 172 us  [swap(): return lax.ppermute(block, axis, [(i, i ^ bit) for i in range(count)])]
    pallas_call x2 -> x20, Pallas kernels: 56.1 us -> 226 us  [the longest x6 112 us: weight_call(): pl.pallas_call(kernel, grid_spec=pltpu.PrefetchScalarGridSpec(num_scalar_...]
    dot_general x15 -> x4, matrix products: 150 us -> 6.53 us  [the longest x1 3.96 us: shards(): jnp.dot(merged_grad, merge_w, preferred_element_type=F32).astype(BF16)]
    reduce_sum x9 -> x1, other arithmetic: 37.3 us -> 0.63 us  [shards(): mod_bias_grad = jnp.sum(clip_slice, axis=1)]
    select_n x27 -> x3, other arithmetic: 25.5 us -> 0.04 us  [turned(): block = jnp.where(my_bit(axis, bit) == 1, jnp.flip(block, dim), block)]
    concatenate x32 -> x13, other arithmetic: 26.8 us -> 4.28 us  [the longest x9 4.11 us: take(): jnp.concatenate([part, new], axis=0)]
    concatenate x10 -> x6, local copies, waits for them, and re-layouts: 18.1 us -> 0.28 us  [the longest x3 0.24 us: take(): jnp.concatenate([part, new], axis=0)]
    dynamic_slice x21 -> x0, local copies, waits for them, and re-layouts: 16.2 us -> none  [the longest x20 16.2 us: halve(): sent = lax.dynamic_slice_in_dim(block, 1 - mine, 1, dim)]
  transfers between devices with their start and end apart: 60 -> 76, of which waited for: 34 -> 28; matrix products, arithmetic and copies ran while one was open for 25% -> 8% of each run, Pallas kernels for 2% -> 42%
where the time goes in v2:
time: 538 us; the launch traced here: 533 us
  Pallas kernels  226 us (42%)
  waiting for transfers between devices  172 us (32%)
  starting transfers between devices  64.3 us (12%)
  other arithmetic  39 us (7%)
  local copies, waits for them, and re-layouts  23.7 us (4%)
  matrix products  6.53 us (1%)
    ppermute x76, waiting for transfers between devices, swap(): return lax.ppermute(block, axis, [(i, i ^ bit) for i in range(count)])  172 us
    pallas_call x6, Pallas kernels, weight_call(): pl.pallas_call(kernel, grid_spec=pltpu.PrefetchScalarGridSpec(num_scalar_...  112 us
    ppermute x76, starting transfers between devices, swap(): return lax.ppermute(block, axis, [(i, i ^ bit) for i in range(count)])  64.3 us
    pallas_call x4, Pallas kernels, weight_grad_call(): pl.pallas_call(kernel, grid=(groups,), in_specs=[whole(a) for a in (*left...  52.3 us
    pallas_call x3, Pallas kernels, attend_back(): pl.pallas_call(functools.partial(attend_back_kernel, heads), grid=(1,), i...  31.2 us
    convert_element_type x19, other arithmetic, plus(): return (a.astype(F32) + b.astype(F32)).astype(BF16)  28.6 us
    pallas_call x1, Pallas kernels, attend(): pl.pallas_call(functools.partial(attend_kernel, heads), grid=(rows // PAT...  17.7 us
    unnamed x171, local copies, waits for them, and re-layouts  17.3 us
  transfers between devices with their start and end apart: 76, of which 28 were waited for; matrix products, arithmetic and copies ran while one was open for 8% of the time, Pallas kernels for 42%

profile of v2, /device:TPU:0, one launch (start us, length us, event | category | flops | bytes accessed | tf_op | source)
XLA Modules:
  0.0 533.0 jit_solution(1469517272944660179)
XLA Ops:
  10.0 6.7 %collective-permute-done.1 = f32[6,12,288]{2,1,0:T(8,128)S(1)} collective-permute-done((f32[6,12,288]{2,1,0:T(8,128)S(1)}, f32[6,12,288]{2,1,0:T(8,128)S(1)}, u32[]{:S(2)}, u32[]{:S(2)}) %collective-permute-start.1) | collective-permute-done | bytes 82976 | tf_op jit(solution)/shard_map/ppermute | solution.py:25
  21.5 9.1 %collective-permute-done.3 = f32[6,12,288]{2,1,0:T(8,128)S(1)} collective-permute-done((f32[6,12,288]{2,1,0:T(8,128)S(1)}, f32[6,12,288]{2,1,0:T(8,128)S(1)}, u32[]{:S(2)}, u32[]{:S(2)}) %collective-permute-start.3) | collective-permute-done | bytes 82976 | tf_op jit(solution)/shard_map/ppermute | solution.py:25
  38.8 6.0 %collective-permute-done.7 = bf16[2,144,1152]{2,1,0:T(8,128)(2,1)S(1)} collective-permute-done((bf16[2,144,1152]{2,1,0:T(8,128)(2,1)S(1)}, bf16[2,144,1152]{2,1,0:T(8,128)(2,1)S(1)}, u32[]{:S(2)}, u32[]{:S(2)}) %collective-permute-start.7) | collective-permute-done | bytes 663584 | tf_op jit(solution)/shard_map/ppermute | solution.py:25
  52.6 10.2 %collective-permute-done.10 = bf16[1,144,1152]{2,1,0:T(8,128)(2,1)S(1)} collective-permute-done((bf16[1,144,1152]{2,1,0:T(8,128)(2,1)S(1)}, bf16[1,144,1152]{2,1,0:T(8,128)(2,1)S(1)}, u32[]{:S(2)}, u32[]{:S(2)}) %collective-permute-start.10) | collective-permute-done | bytes 331808 | tf_op jit(solution)/shard_map/ppermute | solution.py:25
  65.9 15.9 %collective-permute-done.13 = bf16[2,144,1152]{2,1,0:T(8,128)(2,1)S(1)} collective-permute-done((bf16[2,144,1152]{2,1,0:T(8,128)(2,1)S(1)}, bf16[2,144,1152]{2,1,0:T(8,128)(2,1)S(1)}, u32[]{:S(2)}, u32[]{:S(2)}) %collective-permute-start.13) | collective-permute-done | bytes 663584 | tf_op jit(solution)/shard_map/ppermute | solution.py:25
  81.9 10.4 %collective-permute-done.11.refs_4_.refs_7_ = bf16[8,64,1152]{2,1,0:T(8,128)(2,1)S(1)} collective-permute-done((bf16[8,64,1152]{2,1,0:T(8,128)(2,1)S(1)}, bf16[8,64,1152]{2,1,0:T(8,128)(2,1)S(1)}, u32[]{:S(2)}, u32[]{:S(2)}) %collective-permute-start.11) | collective-permute-done | bytes 1179680 | tf_op jit(solution)/shard_map/ppermute | solution.py:25
  92.3 5.5 %collective-permute-done.12.refs_8_.refs_11_ = bf16[8,80,1152]{2,1,0:T(8,128)(2,1)S(1)} collective-permute-done((bf16[8,80,1152]{2,1,0:T(8,128)(2,1)S(1)}, bf16[8,80,1152]{2,1,0:T(8,128)(2,1)S(1)}, u32[]{:S(2)}, u32[]{:S(2)}) %collective-permute-start.12) | collective-permute-done | bytes 1474592 | tf_op jit(solution)/shard_map/ppermute | solution.py:25
  105.6 17.3 %project.1 = (bf16[768,1152]{1,0:T(8,128)(2,1)}, bf16[4,768,864]{2,1,0:T(8,128)(2,1)}, bf16[1152,1152]{1,0:T(8,128)(2,1)}) custom-call(s32[1]{0:T(128)} %bitcast.me_ref, bf16[768,1152]{1,0:T(8,128)(2,1)} %refs_1_.3, f32[3,6,1152]{2,1,0:T(8,128)} %copy-done.2, f32[4,1,864]{2,1,0:T(1,128)} %copy-done.14, bf16[8,64,1152]{2,1,0:T(8,128)(2,1)} %copy-done.26, ...), custom_call_target="tpu_custom_call" | custom-call | flops 1000000000 | bytes 1 | tf_op jit(solution)/shard_map/project/pallas_call | solution.py:321
  130.5 17.7 %attend.1.attended_ref.refs_10_ = bf16[768,1152]{1,0:T(8,128)(2,1)} custom-call(bf16[4,768,864]{2,1,0:T(8,128)(2,1)} %get-tuple-element.238.qkv_ref), custom_call_target="tpu_custom_call" | custom-call | flops 1000000000 | bytes 1 | tf_op jit(solution)/shard_map/attend/pallas_call | solution.py:104
  151.0 7.5 %merge.1 = (f32[768,1152]{1,0:T(8,128)}, bf16[768,1152]{1,0:T(8,128)(2,1)}) custom-call(bf16[768,1152]{1,0:T(8,128)(2,1)} %attend.1.attended_ref.refs_10_, bf16[1152,1152]{1,0:T(8,128)(2,1)} %get-tuple-element.244.weight_ref, bf16[768,1152]{1,0:T(8,128)(2,1)} %refs_1_.3, f32[3,6,1152]{2,1,0:T(8,128)} %copy-done.2, f32[1,1152]{1,0:T(1,128)} %get-tuple-element.448.bias_ref), custom_call_target="tpu_custom_call" | custom-call | flops 1000000000 | bytes 1 | tf_op jit(solution)/shard_map/merge/pallas_call | solution.py:395
  162.8 11.4 %collective-permute-done.26 = bf16[4,64,1152]{2,1,0:T(8,128)(2,1)S(1)} collective-permute-done((bf16[4,64,1152]{2,1,0:T(8,128)(2,1)S(1)}, bf16[4,64,1152]{2,1,0:T(8,128)(2,1)S(1)}, u32[]{:S(2)}, u32[]{:S(2)}) %collective-permute-start.26) | collective-permute-done | bytes 589856 | tf_op jit(solution)/shard_map/ppermute | solution.py:25
  181.7 19.8 %up.1 = (bf16[4,768,1152]{2,1,0:T(8,128)(2,1)}, bf16[4,768,1152]{2,1,0:T(8,128)(2,1)}) custom-call(s32[1]{0:T(128)} %bitcast.me_ref, bf16[768,1152]{1,0:T(8,128)(2,1)} %get-tuple-element.281.refs_0_.block_ref, f32[4,1,1152]{2,1,0:T(1,128)} %copy-done.13, bf16[8,64,1152]{2,1,0:T(8,128)(2,1)} %copy-done.28, ...), custom_call_target="tpu_custom_call" | custom-call | flops 1000000000 | bytes 1 | tf_op jit(solution)/shard_map/up/pallas_call | solution.py:321
  201.5 5.8 %collective-permute-done.29.refs_3_.refs_7_ = bf16[8,64,1152]{2,1,0:T(8,128)(2,1)} collective-permute-done((bf16[8,64,1152]{2,1,0:T(8,128)(2,1)S(1)}, bf16[8,64,1152]{2,1,0:T(8,128)(2,1)}, u32[]{:S(2)}, u32[]{:S(2)}) %collective-permute-start.29) | collective-permute-done | bytes 1179680 | tf_op jit(solution)/shard_map/ppermute | solution.py:25
  207.3 4.7 collective-permute-done.30.refs_7_.refs_11_
  212.6 9.8 %weight_grad.4 = (bf16[2,4,64,1152]{3,2,1,0:T(8,128)(2,1)}, bf16[2,4,64,1152]{3,2,1,0:T(8,128)(2,1)}, bf16[2,4,80,1152]{3,2,1,0:T(8,128)(2,1)}, bf16[2,4,80,1152]{3,2,1,0:T(8,128)(2,1)}) custom-call(bf16[4,144,768]{2,1,0:T(8,128)(2,1)} %copy-done.8, bf16[4,768,1152]{2,1,0:T(8,128)(2,1)} %get-tuple-element.351.refs_1_.refs_0_), custom_call_target="tpu_custom_call" | custom-call | flops 1000000000 | bytes 1 | tf_op jit(solution)/shard_map/weight_grad/pallas_call | solution.py:680
  223.6 10.1 %weight_grad.5 = (bf16[2,4,64,1152]{3,2,1,0:T(8,128)(2,1)}, bf16[2,4,64,1152]{3,2,1,0:T(8,128)(2,1)}, bf16[2,4,80,1152]{3,2,1,0:T(8,128)(2,1)}, bf16[2,4,80,1152]{3,2,1,0:T(8,128)(2,1)}) custom-call(bf16[4,144,768]{2,1,0:T(8,128)(2,1)} %copy-done.6, bf16[4,768,1152]{2,1,0:T(8,128)(2,1)} %get-tuple-element.351.refs_1_.refs_0_), custom_call_target="tpu_custom_call" | custom-call | flops 1000000000 | bytes 1 | tf_op jit(solution)/shard_map/weight_grad/pallas_call | solution.py:680
  235.2 16.6 %gelu_back.1 = (bf16[4,768,1152]{2,1,0:T(8,128)(2,1)}, f32[4,1,1152]{2,1,0:T(1,128)}) custom-call(s32[1]{0:T(128)} %bitcast.me_ref, bf16[768,1152]{1,0:T(8,128)(2,1)} %copy-done.3, bf16[4,768,1152]{2,1,0:T(8,128)(2,1)} %get-tuple-element.284.refs_1_, bf16[8,64,1152]{2,1,0:T(8,128)(2,1)} %copy-done.27, ...), custom_call_target="tpu_custom_call" | custom-call | flops 1000000000 | bytes 1 | tf_op jit(solution)/shard_map/gelu_back/pallas_call | solution.py:321
  259.0 21.6 %up_back.1 = (f32[768,1152]{1,0:T(8,128)}, bf16[768,1152]{1,0:T(8,128)(2,1)}, f32[3,3,1152]{2,1,0:T(4,128)}, f32[1,1152]{1,0:T(1,128)}) custom-call(s32[1]{0:T(128)} %bitcast.me_ref, bf16[4,768,1152]{2,1,0:T(8,128)(2,1)} %get-tuple-element.307.refs_0_.refs_2_, bf16[768,1152]{1,0:T(8,128)(2,1)} %refs_1_.3, f32[768,1152]{1,0:T(8,128)} %get-tuple-element.301.refs_2_, ...), custom_call_target="tpu_custom_call" | custom-call | flops 1000000000 | bytes 1 | tf_op jit(solution)/shard_map/up_back/pallas_call | solution.py:321
  289.6 14.8 %weight_grad.6 = (bf16[2,4,64,1152]{3,2,1,0:T(8,128)(2,1)}, bf16[2,4,64,1152]{3,2,1,0:T(8,128)(2,1)}, bf16[2,4,80,1152]{3,2,1,0:T(8,128)(2,1)}, bf16[2,4,80,1152]{3,2,1,0:T(8,128)(2,1)}) custom-call(bf16[4,144,768]{2,1,0:T(8,128)(2,1)} %copy-done.9, bf16[4,144,768]{2,1,0:T(8,128)(2,1)} %copy-done.58, ...), custom_call_target="tpu_custom_call" | custom-call | flops 1000000000 | bytes 1 | tf_op jit(solution)/shard_map/weight_grad/pallas_call | solution.py:680
  304.3 4.7 collective-permute-done.42
  319.9 10.2 %attend_back.3.refs_0_.refs_4_ = bf16[4,256,896]{2,1,0:T(8,128)(2,1)} custom-call(bf16[4,768,864]{2,1,0:T(8,128)(2,1)} %get-tuple-element.238.qkv_ref, bf16[768,1152]{1,0:T(8,128)(2,1)} %convolution_convert_fusion.grad_ref), custom_call_target="tpu_custom_call" | custom-call | flops 1000000000 | bytes 1 | tf_op jit(solution)/shard_map/attend_back/pallas_call | solution.py:145
  330.1 10.7 %attend_back.4.refs_1_.refs_5_ = bf16[4,256,896]{2,1,0:T(8,128)(2,1)} custom-call(bf16[4,768,864]{2,1,0:T(8,128)(2,1)} %get-tuple-element.238.qkv_ref, bf16[768,1152]{1,0:T(8,128)(2,1)} %convolution_convert_fusion.grad_ref), custom_call_target="tpu_custom_call" | custom-call | flops 1000000000 | bytes 1 | tf_op jit(solution)/shard_map/attend_back/pallas_call | solution.py:145
  340.8 10.3 %attend_back.5.refs_2_.refs_6_ = bf16[4,256,896]{2,1,0:T(8,128)(2,1)} custom-call(bf16[4,768,864]{2,1,0:T(8,128)(2,1)} %get-tuple-element.238.qkv_ref, bf16[768,1152]{1,0:T(8,128)(2,1)} %convolution_convert_fusion.grad_ref), custom_call_target="tpu_custom_call" | custom-call | flops 1000000000 | bytes 1 | tf_op jit(solution)/shard_map/attend_back/pallas_call | solution.py:145
  357.1 18.4 %project_back.1 = (f32[768,1152]{1,0:T(8,128)}, f32[3,2,1152]{2,1,0:T(2,128)}, f32[4,1,864]{2,1,0:T(1,128)}) custom-call(s32[1]{0:T(128)} %bitcast.me_ref, bf16[4,256,896]{2,1,0:T(8,128)(2,1)} %attend_back.3.refs_0_.refs_4_, bf16[4,256,896]{2,1,0:T(8,128)(2,1)} %attend_back.4.refs_1_.refs_5_, bf16[4,256,896]{2,1,0:T(8,128)(2,1)} %attend_back.5.refs_2_.refs_6_, ...), custom_call_target="tpu_custom_call" | custom-call | flops 1000000000 | bytes 1 | tf_op jit(solution)/shard_map/project_back/pallas_call | solution.py:321
  375.6 11.9 %collective-permute-done.48 = bf16[2,4,80,1152]{3,2,1,0:T(8,128)(2,1)} collective-permute-done((bf16[2,4,80,1152]{3,2,1,0:T(8,128)(2,1)}, bf16[2,4,80,1152]{3,2,1,0:T(8,128)(2,1)}, u32[]{:S(2)}, u32[]{:S(2)}) %collective-permute-start.48) | collective-permute-done | bytes 1474592 | tf_op jit(solution)/shard_map/ppermute | solution.py:25
  396.0 17.6 %weight_grad.7 = (bf16[2,4,64,1152]{3,2,1,0:T(8,128)(2,1)}, bf16[2,4,64,1152]{3,2,1,0:T(8,128)(2,1)}, bf16[2,4,80,1152]{3,2,1,0:T(8,128)(2,1)}, bf16[2,4,80,1152]{3,2,1,0:T(8,128)(2,1)}) custom-call(bf16[4,144,768]{2,1,0:T(8,128)(2,1)} %copy-done.5, bf16[4,144,768]{2,1,0:T(8,128)(2,1)} %copy-done.56, bf16[4,144,768]{2,1,0:T(8,128)(2,1)} %copy-done.7, ...), custom_call_target="tpu_custom_call" | custom-call | flops 1000000000 | bytes 1 | tf_op jit(solution)/shard_map/weight_grad/pallas_call | solution.py:680
  420.1 18.3 %down.1 = (bf16[768,1152]{1,0:T(8,128)(2,1)}, f32[3,1,1152]{2,1,0:T(1,128)}) custom-call(s32[1]{0:T(128)} %bitcast.me_ref, bf16[4,768,1152]{2,1,0:T(8,128)(2,1)} %get-tuple-element.351.refs_1_.refs_0_, bf16[768,1152]{1,0:T(8,128)(2,1)} %refs_1_.3, f32[768,1152]{1,0:T(8,128)} %get-tuple-element.301.refs_2_, f32[3,6,1152]{2,1,0:T(8,128)} %copy-done.2, ...), custom_call_target="tpu_custom_call" | custom-call | flops 1000000000 | bytes 1 | tf_op jit(solution)/shard_map/down/pallas_call | solution.py:321
  443.2 6.1 %collective-permute-done.59 = f32[2,80,288]{2,1,0:T(8,128)S(1)} collective-permute-done((f32[2,80,288]{2,1,0:T(8,128)S(1)}, f32[2,80,288]{2,1,0:T(8,128)S(1)}, u32[]{:S(2)}, u32[]{:S(2)}) %collective-permute-start.59) | collective-permute-done | bytes 184352 | tf_op jit(solution)/shard_map/ppermute | solution.py:25
  449.3 4.9 collective-permute-done.60
  475.5 4.7 collective-permute-done.66
  500.2 13.7 %collective-permute-done.74 = bf16[2,144,1152]{2,1,0:T(8,128)(2,1)S(1)} collective-permute-done((bf16[2,144,1152]{2,1,0:T(8,128)(2,1)S(1)}, bf16[2,144,1152]{2,1,0:T(8,128)(2,1)S(1)}, u32[]{:S(2)}, u32[]{:S(2)}) %collective-permute-start.74) | collective-permute-done | bytes 663584 | tf_op jit(solution)/shard_map/ppermute | solution.py:25
  515.2 15.2 %collective-permute-done.75 = bf16[144,1152]{1,0:T(8,128)(2,1)S(1)} collective-permute-done((bf16[144,1152]{1,0:T(8,128)(2,1)S(1)}, bf16[144,1152]{1,0:T(8,128)(2,1)S(1)}, u32[]{:S(2)}, u32[]{:S(2)}) %collective-permute-start.75) | collective-permute-done | bytes 331808 | tf_op jit(solution)/shard_map/ppermute | solution.py:25
  (402 shorter events, 162.9 us)
Async XLA Ops:
  63.1 29.2 %collective-permute-start.15 = (bf16[8,80,1152]{2,1,0:T(8,128)(2,1)S(1)}, bf16[8,80,1152]{2,1,0:T(8,128)(2,1)S(1)}, u32[]{:S(2)}, u32[]{:S(2)}) collective-permute-start(bf16[8,80,1152]{2,1,0:T(8,128)(2,1)S(1)} %pad_maximum_fusion.refs_7_.refs_10_), channel_id=1, source_target_pairs={{0,4},{4,0},{8,12},{12,8},{16,20},{20,16},{24,28},{28,24},{1,5},{5... | collective-permute-start | bytes 4423688 | tf_op jit(solution)/shard_map/ppermute | solution.py:25
  63.2 34.7 %collective-permute-start.12 = (bf16[8,80,1152]{2,1,0:T(8,128)(2,1)S(1)}, bf16[8,80,1152]{2,1,0:T(8,128)(2,1)S(1)}, u32[]{:S(2)}, u32[]{:S(2)}) collective-permute-start(bf16[8,80,1152]{2,1,0:T(8,128)(2,1)S(1)} %pad_maximum_fusion.refs_7_.refs_10_), channel_id=1, source_target_pairs={{0,2},{1,3},{2,0},{3,1},{4,6},{5,7},{6,4},{7,5},{8,10},{9,11},{10,... | collective-permute-start | bytes 4423688 | tf_op jit(solution)/shard_map/ppermute | solution.py:25
  64.1 28.2 %collective-permute-start.11 = (bf16[8,64,1152]{2,1,0:T(8,128)(2,1)S(1)}, bf16[8,64,1152]{2,1,0:T(8,128)(2,1)S(1)}, u32[]{:S(2)}, u32[]{:S(2)}) collective-permute-start(bf16[8,64,1152]{2,1,0:T(8,128)(2,1)S(1)} %pad_maximum_fusion.3.refs_3_.refs_6_), channel_id=1, source_target_pairs={{0,1},{1,0},{2,3},{3,2},{4,5},{5,4},{6,7},{7,6},{8,9},{9,8},{10,11... | collective-permute-start | bytes 3538952 | tf_op jit(solution)/shard_map/ppermute | solution.py:25
  99.6 23.4 %collective-permute-start.17 = (bf16[4,80,1152]{2,1,0:T(8,128)(2,1)}, bf16[4,80,1152]{2,1,0:T(8,128)(2,1)S(1)}, u32[]{:S(2)}, u32[]{:S(2)}) collective-permute-start(bf16[4,80,1152]{2,1,0:T(8,128)(2,1)} %slice.167), channel_id=1, source_target_pairs={{0,1},{1,0},{2,3},{3,2},{4,5},{5,4},{6,7},{7,6},{8,9},{9,8},{10,11... | collective-permute-start | bytes 2211848 | tf_op jit(solution)/shard_map/ppermute | solution.py:25
  124.2 23.9 %collective-permute-start.23 = (bf16[8,80,1152]{2,1,0:T(8,128)(2,1)S(1)}, bf16[8,80,1152]{2,1,0:T(8,128)(2,1)}, u32[]{:S(2)}, u32[]{:S(2)}) collective-permute-start(bf16[8,80,1152]{2,1,0:T(8,128)(2,1)S(1)} %pad_maximum_fusion.1.refs_6_.refs_9_), channel_id=1, source_target_pairs={{0,4},{4,0},{8,12},{12,8},{16,20},{20,16},{24,28},{28,24},{1,5},{5... | collective-permute-start | bytes 4423688 | tf_op jit(solution)/shard_map/ppermute | solution.py:25
  124.4 23.7 %collective-permute-start.22 = (bf16[8,64,1152]{2,1,0:T(8,128)(2,1)S(1)}, bf16[8,64,1152]{2,1,0:T(8,128)(2,1)}, u32[]{:S(2)}, u32[]{:S(2)}) collective-permute-start(bf16[8,64,1152]{2,1,0:T(8,128)(2,1)S(1)} %pad_maximum_fusion.4.refs_2_.refs_5_), channel_id=1, source_target_pairs={{0,4},{4,0},{8,12},{12,8},{16,20},{20,16},{24,28},{28,24},{1,5},{5... | collective-permute-start | bytes 3538952 | tf_op jit(solution)/shard_map/ppermute | solution.py:25
  127.5 35.3 %collective-permute-start.25 = (bf16[8,80,1152]{2,1,0:T(8,128)(2,1)S(1)}, bf16[8,80,1152]{2,1,0:T(8,128)(2,1)}, u32[]{:S(2)}, u32[]{:S(2)}) collective-permute-start(bf16[8,80,1152]{2,1,0:T(8,128)(2,1)S(1)} %pad_maximum_fusion.1.refs_6_.refs_9_), channel_id=1, source_target_pairs={{0,2},{1,3},{2,0},{3,1},{4,6},{5,7},{6,4},{7,5},{8,10},{9,11},{10,... | collective-permute-start | bytes 4423688 | tf_op jit(solution)/shard_map/ppermute | solution.py:25
  128.9 29.6 %collective-permute-start.24 = (bf16[8,64,1152]{2,1,0:T(8,128)(2,1)S(1)}, bf16[8,64,1152]{2,1,0:T(8,128)(2,1)}, u32[]{:S(2)}, u32[]{:S(2)}) collective-permute-start(bf16[8,64,1152]{2,1,0:T(8,128)(2,1)S(1)} %pad_maximum_fusion.4.refs_2_.refs_5_), channel_id=1, source_target_pairs={{0,1},{1,0},{2,3},{3,2},{4,5},{5,4},{6,7},{7,6},{8,9},{9,8},{10,11... | collective-permute-start | bytes 3538952 | tf_op jit(solution)/shard_map/ppermute | solution.py:25
  148.7 25.6 %collective-permute-start.28 = (bf16[4,144,768]{2,1,0:T(8,128)(2,1)S(1)}, bf16[4,144,768]{2,1,0:T(8,128)(2,1)S(1)}, u32[]{:S(2)}, u32[]{:S(2)}) collective-permute-start(bf16[4,144,768]{2,1,0:T(8,128)(2,1)S(1)} %get-tuple-element.242), channel_id=1, source_target_pairs={{0,4},{4,0},{8,12},{12,8},{16,20},{20,16},{24,28},{28,24},{1,5},{5... | collective-permute-start | bytes 2654216 | tf_op jit(solution)/shard_map/ppermute | solution.py:25
  148.9 25.4 %collective-permute-start.27 = (bf16[4,80,1152]{2,1,0:T(8,128)(2,1)S(1)}, bf16[4,80,1152]{2,1,0:T(8,128)(2,1)}, u32[]{:S(2)}, u32[]{:S(2)}) collective-permute-start(bf16[4,80,1152]{2,1,0:T(8,128)(2,1)S(1)} %slice.169), channel_id=1, source_target_pairs={{0,1},{1,0},{2,3},{3,2},{4,5},{5,4},{6,7},{7,6},{8,9},{9,8},{10,11... | collective-permute-start | bytes 2211848 | tf_op jit(solution)/shard_map/ppermute | solution.py:25
  149.6 24.7 %collective-permute-start.26 = (bf16[4,64,1152]{2,1,0:T(8,128)(2,1)S(1)}, bf16[4,64,1152]{2,1,0:T(8,128)(2,1)S(1)}, u32[]{:S(2)}, u32[]{:S(2)}) collective-permute-start(bf16[4,64,1152]{2,1,0:T(8,128)(2,1)S(1)} %slice.168), channel_id=1, source_target_pairs={{0,2},{1,3},{2,0},{3,1},{4,6},{5,7},{6,4},{7,5},{8,10},{9,11},{10,... | collective-permute-start | bytes 1769480 | tf_op jit(solution)/shard_map/ppermute | solution.py:25
  177.2 30.1 %collective-permute-start.32 = (bf16[8,80,1152]{2,1,0:T(8,128)(2,1)S(1)}, bf16[8,80,1152]{2,1,0:T(8,128)(2,1)S(1)}, u32[]{:S(2)}, u32[]{:S(2)}) collective-permute-start(bf16[8,80,1152]{2,1,0:T(8,128)(2,1)S(1)} %pad_maximum_fusion.2.refs_6_.refs_10_), channel_id=1, source_target_pairs={{0,4},{4,0},{8,12},{12,8},{16,20},{20,16},{24,28},{28,24},{1,5},{5... | collective-permute-start | bytes 4423688 | tf_op jit(solution)/shard_map/ppermute | solution.py:25
  177.3 34.8 %collective-permute-start.30 = (bf16[8,80,1152]{2,1,0:T(8,128)(2,1)S(1)}, bf16[8,80,1152]{2,1,0:T(8,128)(2,1)}, u32[]{:S(2)}, u32[]{:S(2)}) collective-permute-start(bf16[8,80,1152]{2,1,0:T(8,128)(2,1)S(1)} %pad_maximum_fusion.2.refs_6_.refs_10_), channel_id=1, source_target_pairs={{0,2},{1,3},{2,0},{3,1},{4,6},{5,7},{6,4},{7,5},{8,10},{9,11},{10,... | collective-permute-start | bytes 4423688 | tf_op jit(solution)/shard_map/ppermute | solution.py:25
  179.0 28.3 %collective-permute-start.29 = (bf16[8,64,1152]{2,1,0:T(8,128)(2,1)S(1)}, bf16[8,64,1152]{2,1,0:T(8,128)(2,1)}, u32[]{:S(2)}, u32[]{:S(2)}) collective-permute-start(bf16[8,64,1152]{2,1,0:T(8,128)(2,1)S(1)} %pad_maximum_fusion.5.refs_2_.refs_6_), channel_id=1, source_target_pairs={{0,1},{1,0},{2,3},{3,2},{4,5},{5,4},{6,7},{7,6},{8,9},{9,8},{10,11... | collective-permute-start | bytes 3538952 | tf_op jit(solution)/shard_map/ppermute | solution.py:25
  222.5 29.4 %collective-permute-start.39 = (bf16[2,4,80,1152]{3,2,1,0:T(8,128)(2,1)}, bf16[2,4,80,1152]{3,2,1,0:T(8,128)(2,1)}, u32[]{:S(2)}, u32[]{:S(2)}) collective-permute-start(bf16[2,4,80,1152]{3,2,1,0:T(8,128)(2,1)} %get-tuple-element.272), channel_id=1, source_target_pairs={{0,4},{4,0},{8,12},{12,8},{16,20},{20,16},{24,28},{28,24},{1,5},{5... | collective-permute-start | bytes 4423688 | tf_op jit(solution)/shard_map/ppermute | solution.py:25
  222.6 29.3 %collective-permute-start.40 = (bf16[2,4,80,1152]{3,2,1,0:T(8,128)(2,1)}, bf16[2,4,80,1152]{3,2,1,0:T(8,128)(2,1)}, u32[]{:S(2)}, u32[]{:S(2)}) collective-permute-start(bf16[2,4,80,1152]{3,2,1,0:T(8,128)(2,1)} %get-tuple-element.273), channel_id=1, source_target_pairs={{0,4},{4,0},{8,12},{12,8},{16,20},{20,16},{24,28},{28,24},{1,5},{5... | collective-permute-start | bytes 4423688 | tf_op jit(solution)/shard_map/ppermute | solution.py:25
  223.1 28.8 %collective-permute-start.37 = (bf16[2,4,64,1152]{3,2,1,0:T(8,128)(2,1)}, bf16[2,4,64,1152]{3,2,1,0:T(8,128)(2,1)}, u32[]{:S(2)}, u32[]{:S(2)}) collective-permute-start(bf16[2,4,64,1152]{3,2,1,0:T(8,128)(2,1)} %get-tuple-element.270), channel_id=1, source_target_pairs={{0,4},{4,0},{8,12},{12,8},{16,20},{20,16},{24,28},{28,24},{1,5},{5... | collective-permute-start | bytes 3538952 | tf_op jit(solution)/shard_map/ppermute | solution.py:25
  223.1 28.7 %collective-permute-start.38 = (bf16[2,4,64,1152]{3,2,1,0:T(8,128)(2,1)}, bf16[2,4,64,1152]{3,2,1,0:T(8,128)(2,1)}, u32[]{:S(2)}, u32[]{:S(2)}) collective-permute-start(bf16[2,4,64,1152]{3,2,1,0:T(8,128)(2,1)} %get-tuple-element.271), channel_id=1, source_target_pairs={{0,4},{4,0},{8,12},{12,8},{16,20},{20,16},{24,28},{28,24},{1,5},{5... | collective-permute-start | bytes 3538952 | tf_op jit(solution)/shard_map/ppermute | solution.py:25
  252.8 29.5 %collective-permute-start.44 = (bf16[4,768,1152]{2,1,0:T(8,128)(2,1)}, bf16[4,768,1152]{2,1,0:T(8,128)(2,1)}, u32[]{:S(2)}, u32[]{:S(2)}) collective-permute-start(bf16[4,768,1152]{2,1,0:T(8,128)(2,1)} %get-tuple-element.307.refs_0_.refs_2_), channel_id=1, source_target_pairs={{0,4},{4,0},{8,12},{12,8},{16,20},{20,16},{24,28},{28,24},{1,5},{5... | collective-permute-start | bytes 21233672 | tf_op jit(solution)/shard_map/ppermute | solution.py:25
  253.2 29.0 %collective-permute-start.45 = (bf16[768,1152]{1,0:T(8,128)(2,1)S(1)}, bf16[768,1152]{1,0:T(8,128)(2,1)S(1)}, u32[]{:S(2)}, u32[]{:S(2)}) collective-permute-start(bf16[768,1152]{1,0:T(8,128)(2,1)S(1)} %copy-done.22), channel_id=1, source_target_pairs={{0,4},{4,0},{8,12},{12,8},{16,20},{20,16},{24,28},{28,24},{1,5},{5... | collective-permute-start | bytes 5308424 | tf_op jit(solution)/shard_map/ppermute | solution.py:25
  255.0 54.0 %collective-permute-start.43 = (bf16[2,4,80,1152]{3,2,1,0:T(8,128)(2,1)S(1)}, bf16[2,4,80,1152]{3,2,1,0:T(8,128)(2,1)S(1)}, u32[]{:S(2)}, u32[]{:S(2)}) collective-permute-start(bf16[2,4,80,1152]{3,2,1,0:T(8,128)(2,1)S(1)} %add_convert_fusion.1), channel_id=1, source_target_pairs={{0,1},{1,0},{2,3},{3,2},{4,5},{5,4},{6,7},{7,6},{8,9},{9,8},{10,11... | collective-permute-start | bytes 4423688 | tf_op jit(solution)/shard_map/ppermute | solution.py:25
  280.6 28.4 %collective-permute-start.42 = (bf16[2,4,64,1152]{3,2,1,0:T(8,128)(2,1)}, bf16[2,4,64,1152]{3,2,1,0:T(8,128)(2,1)}, u32[]{:S(2)}, u32[]{:S(2)}) collective-permute-start(bf16[2,4,64,1152]{3,2,1,0:T(8,128)(2,1)} %add_convert_fusion.3), channel_id=1, source_target_pairs={{0,2},{1,3},{2,0},{3,1},{4,6},{5,7},{6,4},{7,5},{8,10},{9,11},{10,... | collective-permute-start | bytes 3538952 | tf_op jit(solution)/shard_map/ppermute | solution.py:25
  285.5 23.6 %collective-permute-start.46 = (bf16[4,144,768]{2,1,0:T(8,128)(2,1)S(1)}, bf16[4,144,768]{2,1,0:T(8,128)(2,1)S(1)}, u32[]{:S(2)}, u32[]{:S(2)}) collective-permute-start(bf16[4,144,768]{2,1,0:T(8,128)(2,1)S(1)} %get-tuple-element.304), channel_id=1, source_target_pairs={{0,4},{4,0},{8,12},{12,8},{16,20},{20,16},{24,28},{28,24},{1,5},{5... | collective-permute-start | bytes 2654216 | tf_op jit(solution)/shard_map/ppermute | solution.py:25
  311.8 39.8 %collective-permute-start.49 = (bf16[4,64,1152]{2,1,0:T(8,128)(2,1)S(1)}, bf16[4,64,1152]{2,1,0:T(8,128)(2,1)S(1)}, u32[]{:S(2)}, u32[]{:S(2)}) collective-permute-start(bf16[4,64,1152]{2,1,0:T(8,128)(2,1)S(1)} %get-tuple-element.434), channel_id=1, source_target_pairs={{0,1},{1,0},{2,3},{3,2},{4,5},{5,4},{6,7},{7,6},{8,9},{9,8},{10,11... | collective-permute-start | bytes 1769480 | tf_op jit(solution)/shard_map/ppermute | solution.py:25
  313.9 37.7 %collective-permute-start.50 = (bf16[4,80,1152]{2,1,0:T(8,128)(2,1)S(1)}, bf16[4,80,1152]{2,1,0:T(8,128)(2,1)S(1)}, u32[]{:S(2)}, u32[]{:S(2)}) collective-permute-start(bf16[4,80,1152]{2,1,0:T(8,128)(2,1)S(1)} %get-tuple-element.428), channel_id=1, source_target_pairs={{0,2},{1,3},{2,0},{3,1},{4,6},{5,7},{6,4},{7,5},{8,10},{9,11},{10,... | collective-permute-start | bytes 2211848 | tf_op jit(solution)/shard_map/ppermute | solution.py:25
  315.2 41.6 %collective-permute-start.47 = (bf16[2,4,64,1152]{3,2,1,0:T(8,128)(2,1)}, bf16[2,4,64,1152]{3,2,1,0:T(8,128)(2,1)}, u32[]{:S(2)}, u32[]{:S(2)}) collective-permute-start(bf16[2,4,64,1152]{3,2,1,0:T(8,128)(2,1)} %get-tuple-element.314), channel_id=1, source_target_pairs={{0,2},{1,3},{2,0},{3,1},{4,6},{5,7},{6,4},{7,5},{8,10},{9,11},{10,... | collective-permute-start | bytes 3538952 | tf_op jit(solution)/shard_map/ppermute | solution.py:25
  351.1 36.4 %collective-permute-start.53 = (bf16[4,256,896]{2,1,0:T(8,128)(2,1)}, bf16[4,256,896]{2,1,0:T(8,128)(2,1)}, u32[]{:S(2)}, u32[]{:S(2)}) collective-permute-start(bf16[4,256,896]{2,1,0:T(8,128)(2,1)} %attend_back.4.refs_1_.refs_5_), channel_id=1, source_target_pairs={{0,4},{4,0},{8,12},{12,8},{16,20},{20,16},{24,28},{28,24},{1,5},{5... | collective-permute-start | bytes 5505032 | tf_op jit(solution)/shard_map/ppermute | solution.py:25
  351.1 36.4 %collective-permute-start.52 = (bf16[4,256,896]{2,1,0:T(8,128)(2,1)S(1)}, bf16[4,256,896]{2,1,0:T(8,128)(2,1)}, u32[]{:S(2)}, u32[]{:S(2)}) collective-permute-start(bf16[4,256,896]{2,1,0:T(8,128)(2,1)S(1)} %copy-done.21), channel_id=1, source_target_pairs={{0,4},{4,0},{8,12},{12,8},{16,20},{20,16},{24,28},{28,24},{1,5},{5... | collective-permute-start | bytes 5505032 | tf_op jit(solution)/shard_map/ppermute | solution.py:25
  352.5 35.0 %collective-permute-start.54 = (bf16[4,256,896]{2,1,0:T(8,128)(2,1)}, bf16[4,256,896]{2,1,0:T(8,128)(2,1)}, u32[]{:S(2)}, u32[]{:S(2)}) collective-permute-start(bf16[4,256,896]{2,1,0:T(8,128)(2,1)} %attend_back.5.refs_2_.refs_6_), channel_id=1, source_target_pairs={{0,4},{4,0},{8,12},{12,8},{16,20},{20,16},{24,28},{28,24},{1,5},{5... | collective-permute-start | bytes 5505032 | tf_op jit(solution)/shard_map/ppermute | solution.py:25
  352.7 34.9 %collective-permute-start.48 = (bf16[2,4,80,1152]{3,2,1,0:T(8,128)(2,1)}, bf16[2,4,80,1152]{3,2,1,0:T(8,128)(2,1)}, u32[]{:S(2)}, u32[]{:S(2)}) collective-permute-start(bf16[2,4,80,1152]{3,2,1,0:T(8,128)(2,1)} %get-tuple-element.315), channel_id=1, source_target_pairs={{0,1},{1,0},{2,3},{3,2},{4,5},{5,4},{6,7},{7,6},{8,9},{9,8},{10,11... | collective-permute-start | bytes 4423688 | tf_op jit(solution)/shard_map/ppermute | solution.py:25
  417.5 46.5 %collective-permute-start.63 = (bf16[2,4,64,1152]{3,2,1,0:T(8,128)(2,1)}, bf16[2,4,64,1152]{3,2,1,0:T(8,128)(2,1)}, u32[]{:S(2)}, u32[]{:S(2)}) collective-permute-start(bf16[2,4,64,1152]{3,2,1,0:T(8,128)(2,1)} %get-tuple-element.369), channel_id=1, source_target_pairs={{0,2},{1,3},{2,0},{3,1},{4,6},{5,7},{6,4},{7,5},{8,10},{9,11},{10,... | collective-permute-start | bytes 3538952 | tf_op jit(solution)/shard_map/ppermute | solution.py:25
  418.5 45.4 %collective-permute-start.64 = (bf16[2,4,80,1152]{3,2,1,0:T(8,128)(2,1)}, bf16[2,4,80,1152]{3,2,1,0:T(8,128)(2,1)S(1)}, u32[]{:S(2)}, u32[]{:S(2)}) collective-permute-start(bf16[2,4,80,1152]{3,2,1,0:T(8,128)(2,1)} %get-tuple-element.370), channel_id=1, source_target_pairs={{0,1},{1,0},{2,3},{3,2},{4,5},{5,4},{6,7},{7,6},{8,9},{9,8},{10,11... | collective-permute-start | bytes 4423688 | tf_op jit(solution)/shard_map/ppermute | solution.py:25
  (125 other events, 1228.7 us)

commit v3 on v2

v3 whole, which is shorter than its diff:
```python
import functools
import math

import jax
import jax.numpy as jnp
from jax import lax
from jax.experimental import pallas as pl
from jax.experimental.pallas import tpu as pltpu
from jax.sharding import PartitionSpec as P

HEAD = 72
PATCHES = 256
EPSILON = 1e-06
MIB = 1 << 20
F32 = jnp.float32
BF16 = jnp.bfloat16


def bits_of(size):
    return [1 << k for k in range(size.bit_length() - 1)]


def swap(block, axis, bit):
    count = lax.axis_size(axis)
    return lax.ppermute(block, axis, [(i, i ^ bit) for i in range(count)])


def my_bit(axis, bit):
    return (lax.axis_index(axis) // bit) % 2


def tied(*values):
    return lax.optimization_barrier(values)


def dot(a, b, ca, cb):
    return lax.dot_general(a, b, (((ca,), (cb,)), ((), ())), preferred_element_type=F32)


def row_mean(values):
    return jnp.mean(values, axis=1, keepdims=True)


def normalize(values):
    center = row_mean(values)
    inverse = lax.rsqrt(row_mean(values * values) - center * center + EPSILON)
    return inverse, (values - center) * inverse


def norm_back(incoming, normed, inverse):
    return inverse * (incoming - row_mean(incoming) - normed * row_mean(incoming * normed))


def gelu_both(upper):
    c0 = math.sqrt(2.0 / math.pi)
    square = upper * upper
    tanh = jnp.tanh(upper * (c0 + (c0 * 0.044715) * square))
    half = 0.5 + 0.5 * tanh
    bend = (half * (1.0 - half)) * (2.0 * c0 + (2.0 * c0 * 0.134145) * square)
    return upper * half, half + upper * bend


def params(limit=56):
    return pltpu.CompilerParams(vmem_limit_bytes=limit * MIB)


def cost():
    return pl.CostEstimate(flops=1000000000, bytes_accessed=1, transcendentals=0)


def whole(array):
    return pl.BlockSpec(array.shape, lambda i, *_: (0,) * array.ndim)


def along(array):
    return pl.BlockSpec((1,) + array.shape[1:], lambda i, *_: (i,) + (0,) * (array.ndim - 1))


def shape_of(shape, dtype):
    return jax.ShapeDtypeStruct(shape, dtype)


def attend_kernel(heads, qkv_ref, out_ref):
    part = heads * HEAD
    scale = HEAD ** (-0.5)
    results = []
    for n in range(qkv_ref.shape[0]):
        qs, ks, vs = [
            [qkv_ref[n, :, i * part + h * HEAD : i * part + (h + 1) * HEAD] for h in range(heads)]
            for i in range(3)
        ]
        scores = [dot(k, q, 1, 1) for k, q in zip(ks, qs)]
        probs = []
        for s in scores:
            p = jnp.exp((s - jnp.max(s, axis=0, keepdims=True)) * scale)
            probs.append((p.astype(BF16), 1.0 / jnp.sum(p, axis=0, keepdims=True)))
        for (p, weight), v in zip(probs, vs):
            results.append(dot(v, p, 0, 0) * weight)
    out_ref[...] = jnp.concatenate(results, axis=0).T.astype(BF16)


def attend(qkv, heads):
    groups, rows, cols = qkv.shape
    width = groups * heads * HEAD
    out = shape_of((rows, width), BF16)
    return pl.pallas_call(
        functools.partial(attend_kernel, heads),
        grid=(rows // PATCHES,),
        in_specs=[pl.BlockSpec((groups, PATCHES, cols), lambda f: (0, f, 0))],
        out_specs=pl.BlockSpec((PATCHES, width), lambda f: (f, 0)),
        out_shape=out,
        compiler_params=params(),
        cost_estimate=cost(),
        name="attend",
    )(qkv)


def attend_back_kernel(heads, qkv_ref, grad_ref, *refs):
    out_ref = refs[-1]
    part = heads * HEAD
    scale = HEAD ** (-0.5)
    pad = out_ref.shape[2] - 3 * part
    grad = grad_ref[...]
    if len(refs) > 1:
        grad = dot(grad, refs[0][...], 1, 0).astype(BF16)
    for n in range(qkv_ref.shape[0]):
        qs, ks, vs = [
            [qkv_ref[n, :, i * part + h * HEAD : i * part + (h + 1) * HEAD] for h in range(heads)]
            for i in range(3)
        ]
        gs = [grad[:, n * part + h * HEAD : n * part + (h + 1) * HEAD] for h in range(heads)]
        scores = [dot(k, q, 1, 1) for k, q in zip(ks, qs)]
        slopes = [dot(v, g, 1, 1) for v, g in zip(vs, gs)]
        probs, score_grads = [], []
        for s, dp in zip(scores, slopes):
            p = jnp.exp((s - jnp.max(s, axis=0, keepdims=True)) * scale)
            p = p * (1.0 / jnp.sum(p, axis=0, keepdims=True))
            probs.append(p.astype(BF16))
            score_grads.append((p * (dp - jnp.sum(p * dp, axis=0, keepdims=True))).astype(BF16))
        dvs = [dot(p, g, 1, 0) for p, g in zip(probs, gs)]
        dks = [dot(ds, q, 1, 0) * scale for ds, q in zip(score_grads, qs)]
        dqs = [dot(k, ds, 0, 0) * scale for ds, k in zip(score_grads, ks)]
        dq = jnp.concatenate(dqs, axis=0).T
        zeros = [jnp.zeros((PATCHES, pad), F32)] if pad else []
        out_ref[n] = jnp.concatenate([dq] + dks + dvs + zeros, axis=1).astype(BF16)


def attend_back(qkv, grad, heads, weight=None):
    groups, rows, cols = qkv.shape
    width = groups * heads * HEAD
    out = shape_of((groups, rows, -(-cols // 128) * 128), BF16)
    more = [] if weight is None else [weight]
    return pl.pallas_call(
        functools.partial(attend_back_kernel, heads),
        grid=(rows // PATCHES,),
        in_specs=[
            pl.BlockSpec((groups, PATCHES, cols), lambda f: (0, f, 0)),
            pl.BlockSpec((PATCHES, width), lambda f: (f, 0)),
        ]
        + [whole(a) for a in more],
        out_specs=pl.BlockSpec((groups, PATCHES, out.shape[2]), lambda f: (0, f, 0)),
        out_shape=out,
        compiler_params=params(),
        cost_estimate=cost(),
        name="attend_back",
    )(qkv, grad, *more)


class Sent:
    def __init__(self, *values):
        self.pending = list(values)

    def take(self, got):
        self.got = got
        self.pending = []


def land(sents, *ties):
    sents = [sent for sent in sents if sent.pending]
    pending = [value for sent in sents for value in sent.pending]
    values = list(tied(*pending, *ties))
    for sent in sents:
        count = len(sent.pending)
        sent.take(values[:count])
        values = values[count:]
    return values


class Gather:
    def __init__(self, shard):
        self.depth, self.cols = shard.shape
        self.cut = max(16, self.depth // 2 // 16 * 16)
        wide = [("wide", bit) for bit in reversed(bits_of(lax.axis_size("wide")))]
        narrow = [("narrow", bit) for bit in reversed(bits_of(lax.axis_size("narrow")))]
        self.core = wide[-1]
        self.front = wide[:-1] + narrow[:-2]
        self.last = narrow[-2:]
        self.own = shard[None]
        self.stage = 0
        self.pending = []
        self.crossed = {}

    def in_front(self):
        return self.stage < len(self.front)

    def start(self):
        if self.in_front():
            self.pending = [swap(self.own, *self.front[self.stage])]
        elif self.stage == len(self.front):
            self.pending = [swap(self.own, *key) for key in self.last]
        else:
            self.pending = [
                swap(self.first[:, : self.cut], *self.last[1]),
                swap(self.second[:, self.cut :], *self.last[0]),
            ]
        return self

    def take(self, got):
        self.pending = []
        if self.in_front():
            self.own = jnp.concatenate([self.own, got[0]], axis=0)
        elif self.stage == len(self.front):
            self.first, self.second = got
        else:
            self.third, self.fourth = got
        self.stage += 1

    def cross(self, *names):
        sent = Sent(*[swap(getattr(self, name), *self.core) for name in names])
        for i, name in enumerate(names):
            self.crossed[name] = (sent, i)
        return sent

    def finish(self):
        names = ["own", "first", "second", "third", "fourth"]
        self.arrays = [getattr(self, name) for name in names]
        for name in names:
            sent, i = self.crossed[name]
            self.arrays.append(sent.got[i])
        return self

    def entries(self, n):
        found = []
        (unused, high), (unused, low) = self.last
        whole_rows, cut = (0, self.depth), self.cut
        for w in range(lax.axis_size("wide")):
            index = 0
            for j, (axis, bit) in enumerate(self.front):
                index += bool((n if axis == "narrow" else w) & bit) << j
            side = 5 * bool(w & self.core[1])
            if n & high and n & low:
                parts = [(3, 0, cut), (4, cut, self.depth - cut)]
            else:
                parts = [(1 if n & high else 2 if n & low else 0, 0, self.depth)]
            found += [(side + which, index, w, offset, size) for which, offset, size in parts]
        return found

    def assembled(self):
        sides = []
        for side in (0, 5):
            own, first, second, third, fourth = self.arrays[side : side + 5]
            across = jnp.concatenate([third, fourth], axis=1)
            sides.append(jnp.stack([jnp.stack([own, second]), jnp.stack([first, across])]))
        block = jnp.stack(sides)
        keys = [self.core, *self.last, *self.front[::-1]]
        block = block.reshape([2] * len(keys) + [self.depth, self.cols])
        narrow = [("narrow", bit) for bit in reversed(bits_of(lax.axis_size("narrow")))]
        wide = [("wide", bit) for bit in reversed(bits_of(lax.axis_size("wide")))]
        order = [keys.index(key) for key in narrow + wide]
        block = block.transpose(order + [len(keys), len(keys) + 1])
        for dim, key in enumerate(wide):
            dim += len(narrow)
            block = jnp.where(my_bit(*key) == 1, jnp.flip(block, dim), block)
        return block.reshape(lax.axis_size("narrow"), -1, self.cols)


class Weight:
    def __init__(self, gather):
        groups = lax.axis_size("narrow")
        self.depth, self.cols = gather.depth, gather.cols
        if gather.cut % 16 or gather.depth % 16:
            self.arrays = [gather.assembled()]
            self.plan = [[(0, n, None, 0, 0)] for n in range(groups)]
        else:
            self.arrays = gather.arrays
            self.plan = [gather.entries(n) for n in range(groups)]


class Whole:
    def __init__(self, shard):
        self.depth, self.cols = shard.shape
        groups = lax.axis_size("narrow")
        blocks = lax.all_gather(shard, ("narrow", "wide"), axis=0)
        self.blocks = blocks.reshape(groups, lax.axis_size("wide") * self.depth, self.cols)

    def finish(self):
        self.arrays = [self.blocks]
        self.plan = [[(0, n, None, 0, 0)] for n in range(lax.axis_size("narrow"))]
        return self


def stream(step, weight, me, refs, buffer, sems, before):
    plan = weight.plan

    def issue(n):
        for which, index, w, offset, size in plan[n]:
            if w is None:
                target = buffer.at[n % 2]
                if isinstance(weight, Whole):
                    index = me[1] ^ index
            else:
                row = pl.multiple_of((me[0] ^ w) * weight.depth + offset, 16)
                target = buffer.at[n % 2, pl.ds(row, size)]
            pltpu.make_async_copy(refs[which].at[index], target, sems.at[n % 2]).start()

    @pl.when(step == -before)
    def _():
        issue(0)
        pltpu.make_async_copy(buffer.at[0], buffer.at[0], sems.at[0]).wait()
        issue(1)

    for n in range(1, len(plan)):

        @pl.when(step == n)
        def _():
            pltpu.make_async_copy(buffer.at[n % 2], buffer.at[n % 2], sems.at[n % 2]).wait()
            if n + 1 < len(plan):
                issue(n + 1)

    return buffer.at[jnp.clip(step, 0, len(plan) - 1) % 2]


def group_at(array, before, groups):
    def index(i, *_):
        return (jnp.clip(i - before, 0, groups - 1),) + (0,) * (array.ndim - 1)

    return pl.BlockSpec((1,) + array.shape[1:], index)


def rows_at(array, first, spans):
    def index(i, *_):
        return (jnp.clip(i - first, 0, spans - 1),) + (0,) * (array.ndim - 1)

    return pl.BlockSpec((array.shape[0] // spans,) + array.shape[1:], index)


def weight_call(body, weight, ins, in_specs, outs, out_specs, scratch, name, before=0, after=0):
    count, groups = len(weight.arrays), len(weight.plan)
    width = lax.axis_size("wide") * weight.depth

    def kernel(me_ref, *refs):
        step = pl.program_id(0) - before
        in_refs = refs[: len(ins)]
        weight_refs = refs[len(ins) : len(ins) + count]
        out_refs = refs[len(ins) + count : len(ins) + count + len(outs)]
        buffer, sems = refs[len(ins) + count + len(outs) :][:2]
        scratch_refs = refs[len(ins) + count + len(outs) + 2 :]
        w = stream(step, weight, me_ref, weight_refs, buffer, sems, before)
        body(step, in_refs, w, out_refs, scratch_refs)

    me = jnp.stack([lax.axis_index("wide"), lax.axis_index("narrow")]).astype(jnp.int32)
    return pl.pallas_call(
        kernel,
        grid_spec=pltpu.PrefetchScalarGridSpec(
            num_scalar_prefetch=1,
            grid=(before + groups + after,),
            in_specs=list(in_specs) + [pl.BlockSpec(memory_space=pl.ANY)] * count,
            out_specs=list(out_specs),
            scratch_shapes=[
                pltpu.VMEM((2, width, weight.cols), BF16),
                pltpu.SemaphoreType.DMA((2,)),
            ]
            + list(scratch),
        ),
        out_shape=list(outs),
        compiler_params=params(),
        cost_estimate=cost(),
        name=name,
    )(me, *ins, *weight.arrays)


def project_call(weight, tokens, modes, bias, part):
    rows, width = tokens.shape
    spans, span = modes.shape[0], rows // modes.shape[0]
    groups = len(weight.plan)
    outs = [
        shape_of((rows, width), BF16),
        shape_of((groups, rows, 3 * part), BF16),
        shape_of((width, groups * part), BF16),
    ]

    before = spans - 1

    def body(step, ins, w, out, scratch):
        tokens_ref, modes_ref, bias_ref = ins
        hidden_ref, qkv_ref, merge_ref = out
        held = scratch[0]

        @pl.when(step <= 0)
        def _():
            at = pl.ds(pl.multiple_of((step + before) * span, span), span)
            unused, normed = normalize(tokens_ref[...].astype(F32))
            hidden = (normed * (1.0 + modes_ref[0, 1:2]) + modes_ref[0, 0:1]).astype(BF16)
            hidden_ref[...] = hidden
            held[at, :] = hidden
            qkv_ref[0, at, :] = (dot(hidden, w[:, : 3 * part], 1, 0) + bias_ref[0]).astype(BF16)

        @pl.when(step > 0)
        def _():
            qkv_ref[0] = (dot(held[...], w[:, : 3 * part], 1, 0) + bias_ref[0]).astype(BF16)

        for n in range(groups):

            @pl.when(step == n)
            def _():
                merge_ref[:, n * part : (n + 1) * part] = w[:, 3 * part :]

    return weight_call(
        body,
        weight,
        [tokens, modes, bias],
        [rows_at(tokens, 0, spans), rows_at(modes, 0, spans), group_at(bias, before, groups)],
        outs,
        [rows_at(outs[0], 0, spans), group_at(outs[1], before, groups), whole(outs[2])],
        [pltpu.VMEM((rows, width), BF16)],
        "project",
        before=before,
    )


def merge_kernel(attended_ref, weight_ref, tokens_ref, modes_ref, bias_ref, branch_ref, hidden_ref):
    branch = dot(attended_ref[...], weight_ref[...], 1, 1) + bias_ref[...]
    branch_ref[...] = branch
    middle = tokens_ref[...].astype(F32) + modes_ref[0, 2:3] * branch
    unused, normed = normalize(middle)
    hidden_ref[...] = (normed * (1.0 + modes_ref[0, 4:5]) + modes_ref[0, 3:4]).astype(BF16)


def merge_call(attended, weight, tokens, modes, bias):
    rows, width = tokens.shape
    spans, span = modes.shape[0], rows // modes.shape[0]
    block = pl.BlockSpec((span, width), lambda i: (i, 0))
    outs = [shape_of((rows, width), F32), shape_of((rows, width), BF16)]
    return pl.pallas_call(
        merge_kernel,
        grid=(spans,),
        in_specs=[block, whole(weight), block, along(modes), whole(bias)],
        out_specs=[block, block],
        out_shape=outs,
        compiler_params=params(),
        cost_estimate=cost(),
        name="merge",
    )(attended, weight, tokens, modes, bias)


def up_call(weight, hidden, bias, left):
    rows, width = hidden.shape
    groups, units = len(weight.plan), weight.cols
    zs, depth = left.shape[:2]
    outs = [shape_of((groups, rows, units), BF16)] * 2 + [shape_of((groups, zs, depth, units), BF16)]

    def body(step, ins, w, out, scratch):
        hidden_ref, bias_ref, left_ref = ins
        gelu, slope = gelu_both(dot(hidden_ref[...], w[...], 1, 0) + bias_ref[0])
        gelu = gelu.astype(BF16)
        out[0][0] = gelu
        out[1][0] = slope.astype(BF16)
        part = dot(left_ref[...].reshape(zs * depth, rows), gelu, 1, 0)
        out[2][0] = part.astype(BF16).reshape(zs, depth, units)

    return weight_call(
        body,
        weight,
        [hidden, bias, left],
        [whole(hidden), along(bias), whole(left)],
        outs,
        [along(out) for out in outs],
        [],
        "up",
    )


def down_call(weight, gelu, tokens, branch, modes, bias, grad):
    rows, width = tokens.shape
    spans, span = modes.shape[0], rows // modes.shape[0]
    groups, units = len(weight.plan), weight.cols
    outs = [shape_of((rows, width), BF16), shape_of((spans, 1, width), F32)]

    def body(step, ins, w, out, scratch):
        gelu_ref, tokens_ref, branch_ref, modes_ref, bias_ref, grad_ref = ins
        total = scratch[0]

        @pl.when(step == 0)
        def _():
            total[...] = dot(gelu_ref[0], w[...], 1, 1)

        @pl.when((step > 0) & (step < groups - 1))
        def _():
            total[...] += dot(gelu_ref[0], w[...], 1, 1)

        @pl.when(step >= groups - 1)
        def _():
            at = pl.ds(pl.multiple_of((step - groups + 1) * span, span), span)
            other = total[at, :] + dot(gelu_ref[0, at, :], w[...], 1, 1) + bias_ref[...]
            middle = tokens_ref[...].astype(F32) + modes_ref[0, 2:3] * branch_ref[...]
            out[0][...] = (middle + modes_ref[0, 5:6] * other).astype(BF16)
            out[1][0] = jnp.sum(grad_ref[...].astype(F32) * other, axis=0, keepdims=True)

    def by_span(array):
        return rows_at(array, groups - 1, spans)

    return weight_call(
        body,
        weight,
        [gelu, tokens, branch, modes, bias, grad],
        [group_at(gelu, 0, groups), by_span(tokens), by_span(branch), by_span(modes), whole(bias), by_span(grad)],
        outs,
        [by_span(outs[0]), by_span(outs[1])],
        [pltpu.VMEM((rows, width), F32)],
        "down",
        after=spans - 1,
    )


def gelu_back_call(weight, grad, slope, left):
    rows, width = grad.shape
    groups, units = len(weight.plan), weight.cols
    zs, depth = left.shape[:2]
    outs = [
        shape_of((groups, rows, units), BF16),
        shape_of((groups, 1, units), F32),
        shape_of((groups, zs, depth, units), BF16),
    ]

    def body(step, ins, w, out, scratch):
        grad_ref, slope_ref, left_ref = ins
        upper = (dot(grad_ref[...], w[...], 1, 0) * slope_ref[0].astype(F32)).astype(BF16)
        out[0][0] = upper
        out[1][0] = jnp.sum(upper.astype(F32), axis=0, keepdims=True)
        part = dot(left_ref[...].reshape(zs * depth, rows), upper, 1, 0)
        out[2][0] = part.astype(BF16).reshape(zs, depth, units)

    return weight_call(
        body,
        weight,
        [grad, slope, left],
        [whole(grad), along(slope), whole(left)],
        outs,
        [along(out) for out in outs],
        [],
        "gelu_back",
    )


def up_back_call(weight, upper, tokens, branch, modes, grad):
    rows, width = tokens.shape
    spans, span = modes.shape[0], rows // modes.shape[0]
    groups, units = len(weight.plan), weight.cols
    outs = [
        shape_of((rows, width), F32),
        shape_of((rows, width), BF16),
        shape_of((spans, 3, width), F32),
        shape_of((1, width), F32),
    ]

    def body(step, ins, w, out, scratch):
        upper_ref, tokens_ref, branch_ref, modes_ref, grad_ref = ins
        middle_ref, merged_ref, sums_ref, bias_ref = out
        total = scratch[0]

        @pl.when(step == 0)
        def _():
            total[...] = dot(upper_ref[0], w[...], 1, 1)
            bias_ref[...] = jnp.zeros_like(bias_ref)

        @pl.when((step > 0) & (step < groups - 1))
        def _():
            total[...] += dot(upper_ref[0], w[...], 1, 1)

        @pl.when(step >= groups - 1)
        def _():
            at = pl.ds(pl.multiple_of((step - groups + 1) * span, span), span)
            hidden = total[at, :] + dot(upper_ref[0, at, :], w[...], 1, 1)
            branch = branch_ref[...]
            gate = modes_ref[0, 2:3]
            inverse, normed = normalize(tokens_ref[...].astype(F32) + gate * branch)
            back = norm_back(hidden * (1.0 + modes_ref[0, 4:5]), normed, inverse)
            middle = grad_ref[...].astype(F32) + back
            gated = gate * middle
            middle_ref[...] = middle
            merged_ref[...] = gated.astype(BF16)
            sums_ref[0, 0:1] = jnp.sum(middle * branch, axis=0, keepdims=True)
            sums_ref[0, 1:2] = jnp.sum(hidden, axis=0, keepdims=True)
            sums_ref[0, 2:3] = jnp.sum(hidden * normed, axis=0, keepdims=True)
            bias_ref[...] += jnp.sum(gated, axis=0, keepdims=True)

    def by_span(array):
        return rows_at(array, groups - 1, spans)

    return weight_call(
        body,
        weight,
        [upper, tokens, branch, modes, grad],
        [group_at(upper, 0, groups)] + [by_span(a) for a in (tokens, branch, modes, grad)],
        outs,
        [by_span(a) for a in outs[:3]] + [whole(outs[3])],
        [pltpu.VMEM((rows, width), F32)],
        "up_back",
        after=spans - 1,
    )


def project_back_call(weight, qkv_grad, tokens, middle, modes, cols):
    rows, width = tokens.shape
    spans, span = modes.shape[0], rows // modes.shape[0]
    groups = len(weight.plan)
    outs = [
        shape_of((rows, width), F32),
        shape_of((spans, 2, width), F32),
        shape_of((groups, 1, cols), F32),
    ]

    def body(step, ins, w, out, scratch):
        grad_ref, tokens_ref, middle_ref, modes_ref = ins
        tokens_grad_ref, sums_ref, bias_ref = out
        total = scratch[0]

        @pl.when(step < groups)
        def _():
            bias_ref[0] = jnp.sum(grad_ref[0, :, :cols].astype(F32), axis=0, keepdims=True)

        @pl.when(step == 0)
        def _():
            total[...] = dot(grad_ref[0, :, :cols], w[:, :cols], 1, 1)

        @pl.when((step > 0) & (step < groups - 1))
        def _():
            total[...] += dot(grad_ref[0, :, :cols], w[:, :cols], 1, 1)

        @pl.when(step >= groups - 1)
        def _():
            at = pl.ds(pl.multiple_of((step - groups + 1) * span, span), span)
            inverse, normed = normalize(tokens_ref[...].astype(F32))
            hidden = total[at, :] + dot(grad_ref[0, at, :cols], w[:, :cols], 1, 1)
            back = norm_back(hidden * (1.0 + modes_ref[0, 1:2]), normed, inverse)
            tokens_grad_ref[...] = middle_ref[...] + back
            sums_ref[0, 0:1] = jnp.sum(hidden, axis=0, keepdims=True)
            sums_ref[0, 1:2] = jnp.sum(hidden * normed, axis=0, keepdims=True)

    def by_span(array):
        return rows_at(array, groups - 1, spans)

    return weight_call(
        body,
        weight,
        [qkv_grad, tokens, middle, modes],
        [group_at(qkv_grad, 0, groups)] + [by_span(a) for a in (tokens, middle, modes)],
        outs,
        [by_span(outs[0]), by_span(outs[1]), group_at(outs[2], 0, groups)],
        [pltpu.VMEM((rows, width), F32)],
        "project_back",
        after=spans - 1,
    )


def put_turned(depth, side, block, own_ref, other_ref):
    turned_block = block.T
    for z in range(own_ref.shape[0]):
        even = turned_block[2 * z * depth : (2 * z + 1) * depth]
        odd = turned_block[(2 * z + 1) * depth : (2 * z + 2) * depth]
        own_ref[z] = jnp.where(side == 1, odd, even)
        other_ref[z] = jnp.where(side == 1, even, odd)


def turn_kernel(depth, me_ref, block_ref, own_ref, other_ref):
    put_turned(depth, me_ref[0] & 1, block_ref[...], own_ref, other_ref)


def turn(block):
    rows, width = block.shape
    blocks = lax.axis_size("wide")
    out = shape_of((blocks // 2, width // blocks, rows), BF16)
    me = lax.axis_index("wide").astype(jnp.int32)[None]
    own, other = pl.pallas_call(
        functools.partial(turn_kernel, width // blocks),
        grid_spec=pltpu.PrefetchScalarGridSpec(
            num_scalar_prefetch=1, grid=(1,), in_specs=[whole(block)], out_specs=[whole(out)] * 2
        ),
        out_shape=[out, out],
        compiler_params=params(24),
        cost_estimate=cost(),
        name="turn",
    )(me, block)
    return own, other


def weight_grad_call(lefts, grads, merged, attended, cols, added=None):
    zs, size, rows = lefts[0].shape
    groups = grads[0].shape[0]
    width = 2 * zs * size
    cut = max(16, size // 2 // 16 * 16)
    part = width // groups if merged else 0
    half = groups // 2
    outs = []
    for height in (cut, cut, size - cut, size - cut):
        outs.append(shape_of((half, zs, height, cols + part), BF16))
    more = [] if added is None else [added]
    ins = [*lefts, *grads, *more, *merged, *attended]
    count = len(lefts)

    def product(left_refs, right_refs):
        terms = [
            dot(left[...].reshape(zs * size, rows), right, 1, 0)
            for left, right in zip(left_refs, right_refs)
        ]
        return sum(terms[1:], terms[0])

    def kernel(*refs):
        step = pl.program_id(0)
        left_refs, grad_refs, rest = refs[:count], refs[count : 2 * count], refs[2 * count : len(ins)]
        out_refs, scratch = refs[len(ins) : len(ins) + 4], refs[len(ins) + 4 :]
        result = product(left_refs, [ref[0, :, :cols] for ref in grad_refs])
        if more:
            result = result + rest[0][0].reshape(zs * size, cols).astype(F32)
        result = result.astype(BF16)
        if merged:

            @pl.when(step == 0)
            def _():
                pairs = rest[len(more) :]
                values = [ref[...] for ref in pairs[len(merged) :]]
                scratch[0][...] = product(pairs[: len(merged)], values).astype(BF16)

        for n in range(groups):

            @pl.when(step == n)
            def _():
                value = result
                if merged:
                    value = jnp.concatenate([value, scratch[0][:, n * part : (n + 1) * part]], axis=1)
                first = out_refs[0] if n < half else out_refs[1]
                second = out_refs[2] if n % 2 == 0 else out_refs[3]
                for z in range(zs):
                    first[0, z] = value[z * size : z * size + cut]
                    second[0, z] = value[z * size + cut : (z + 1) * size]

    rest = (0, 0, 0)
    out_specs = [
        pl.BlockSpec((1,) + out.shape[1:], index)
        for out, index in zip(
            outs,
            [
                lambda i: (jnp.minimum(i, half - 1),) + rest,
                lambda i: (jnp.maximum(i - half, 0),) + rest,
                lambda i: (i // 2,) + rest,
                lambda i: (i // 2,) + rest,
            ],
        )
    ]
    return pl.pallas_call(
        kernel,
        grid=(groups,),
        in_specs=[whole(a) for a in lefts]
        + [along(a) for a in (*grads, *more)]
        + [whole(a) for a in (*merged, *attended)],
        out_specs=out_specs,
        scratch_shapes=[pltpu.VMEM((zs * size, width), BF16)] if merged else [],
        out_shape=outs,
        compiler_params=params(),
        cost_estimate=cost(),
        name="weight_grad",
    )(*ins)


def plus(a, b):
    return (a.astype(F32) + b.astype(F32)).astype(BF16)


class Scatter:
    def __init__(self, first_kept, first_sent, second_kept, second_sent):
        narrow = list(reversed(bits_of(lax.axis_size("narrow"))))
        self.orders = [narrow, narrow[::-1]]
        self.left = [list(narrow), list(narrow)]
        self.front = list(bits_of(lax.axis_size("wide")))[1:]
        self.stage = 0
        self.stages = len(narrow) + len(self.front)
        self.kept, self.pending = [], []
        sides = ((first_kept, first_sent), (second_kept, second_sent))
        for part, (kept, sent) in enumerate(sides):
            bit = self.orders[part][0]
            self.left[part].remove(bit)
            self.kept.append(kept.reshape([2] * (len(narrow) - 1) + list(kept.shape[1:])))
            self.pending.append(swap(sent.reshape(self.kept[-1].shape), "narrow", bit))

    def take(self, got):
        self.got = list(got)
        self.go()

    def wait(self):
        sent = Sent(*self.pending)
        sent.take = lambda got: setattr(self, "got", list(got))
        self.pending = []
        return sent

    def go(self):
        kept, got, narrow = self.kept, self.got, len(self.orders[0])
        self.stage += 1
        if self.stage < narrow:
            self.kept, self.pending = [], []
            for part, order in enumerate(self.orders):
                bit = order[self.stage]
                dim = self.left[part].index(bit)
                self.left[part].remove(bit)
                stay, go = [
                    plus(
                        lax.index_in_dim(kept[part], side, dim, False),
                        lax.index_in_dim(got[part], side, dim, False),
                    )
                    for side in (0, 1)
                ]
                self.kept.append(stay)
                self.pending.append(swap(go, "narrow", bit))
        elif self.stage < self.stages:
            bit = self.front[self.stage - narrow]
            mine = my_bit("wide", bit)
            dim = len(self.front) - 1 - (self.stage - narrow)
            sides = []
            for side in (mine, 1 - mine):
                blocks = []
                for a, b in zip(kept, got):
                    if self.stage == narrow:
                        shape = [2] * len(self.front) + list(a.shape[1:])
                        a, b = a.reshape(shape), b.reshape(shape)
                    blocks.append(
                        plus(
                            lax.dynamic_index_in_dim(a, side, dim, False),
                            lax.dynamic_index_in_dim(b, side, dim, False),
                        )
                    )
                sides.append(jnp.concatenate(blocks, axis=-2) if len(blocks) > 1 else blocks[0])
            self.kept = [sides[0]]
            self.pending = [swap(sides[1], "wide", bit)]
        else:
            self.result = kept[0].astype(F32) + got[0].astype(F32)
            self.pending = []


def spread(block, axis, bits):
    blocks = [block]
    for index in range(1, 1 << len(bits)):
        mask = sum(bit for j, bit in enumerate(bits) if index >> j & 1)
        blocks.append(swap(block, axis, mask))
    return blocks


def tree_sum(blocks):
    while len(blocks) > 1:
        blocks = [blocks[i] + blocks[i + 1] for i in range(0, len(blocks), 2)]
    return blocks[0]


def unpack_call(span_clip, narrow_me, clips, blocks, grad):
    spans = span_clip.shape[0]
    rows, width = grad.shape
    span = rows // spans
    groups = len(blocks)
    height, part = blocks[0].shape
    at = 6 * clips
    units = (height - at - 4) * part
    wide = lax.axis_size("wide")
    outs = [
        shape_of((spans, 6, width), F32),
        shape_of((2, 1, width), F32),
        shape_of((groups, 1, 3 * part), F32),
        shape_of((groups, 1, units), F32),
        shape_of((rows, width), BF16),
        shape_of((1, width), F32),
        shape_of((wide // 2, width // wide, rows), BF16),
        shape_of((wide // 2, width // wide, rows), BF16),
    ]

    def kernel(clip_ref, me_ref, *refs):
        block_refs, grad_ref = refs[: len(blocks)], refs[len(blocks)]
        modes_ref, bias_ref, qkv_ref, up_ref, core_ref, sum_ref, own_ref, other_ref = refs[len(blocks) + 1 :]
        for rel, ref in enumerate(block_refs):
            owner = me_ref[0] ^ rel
            found = []
            for s in range(spans):
                for k in range(6):
                    found.append(ref[pl.ds(k * clips + clip_ref[s], 1), :])
            for n in range(groups):

                @pl.when(owner == n)
                def _():
                    lanes = slice(n * part, (n + 1) * part)
                    for s in range(spans):
                        for k in range(6):
                            modes_ref[s, k : k + 1, lanes] = found[6 * s + k]
                    for k in range(2):
                        bias_ref[k, :, lanes] = ref[at + 2 + k : at + 3 + k, :]

            qkv_ref[rel] = jnp.concatenate(
                [ref[at : at + 1, :], jnp.zeros((1, part), F32), ref[at + 1 : at + 2, :]], axis=1
            )
            for j in range(units // part):
                up_ref[rel, :, j * part : (j + 1) * part] = ref[at + 4 + j : at + 5 + j, :]
        for s in range(spans):
            lines = slice(s * span, (s + 1) * span)
            gated = modes_ref[s, 5:6] * grad_ref[lines, :].astype(F32)
            core_ref[lines, :] = gated.astype(BF16)
            here = jnp.sum(gated, axis=0, keepdims=True)
            sum_ref[...] = here if s == 0 else sum_ref[...] + here
        put_turned(width // wide, me_ref[1] & 1, core_ref[...], own_ref, other_ref)

    me = jnp.stack([narrow_me, lax.axis_index("wide")]).astype(jnp.int32)
    return pl.pallas_call(
        kernel,
        grid_spec=pltpu.PrefetchScalarGridSpec(
            num_scalar_prefetch=2,
            grid=(1,),
            in_specs=[whole(a) for a in (*blocks, grad)],
            out_specs=[whole(a) for a in outs],
        ),
        out_shape=outs,
        compiler_params=params(32),
        cost_estimate=cost(),
        name="unpack",
    )(span_clip, me, *blocks, grad)


def pack_call(span_clip, narrow_me, clips, sums_a, sums_b, sums_g, merge_bias, down_bias, qkv_sums, up_bias):
    spans, unused, width = sums_a.shape
    groups = qkv_sums.shape[0]
    part, units = width // groups, up_bias.shape[2]
    at = 6 * clips
    height = at + 4 + units // part
    outs = [shape_of((groups // 2, height, part), F32)] * 2
    ins = [sums_a, sums_b, sums_g, merge_bias, down_bias, qkv_sums, up_bias]

    def kernel(clip_ref, me_ref, a_ref, b_ref, g_ref, merge_ref, down_ref, qkv_ref, up_ref, *refs):
        total = refs[2]
        out_refs = [refs[rel // (groups // 2)].at[rel % (groups // 2)] for rel in range(groups)]
        total[...] = jnp.zeros_like(total)
        for s in range(spans):
            rows = [a_ref[s, 0:1], a_ref[s, 1:2]] + [b_ref[s, i : i + 1] for i in range(3)]
            rows.append(g_ref[s, 0:1])
            for k in range(6):
                row = pl.ds(k * clips + clip_ref[s], 1)
                total[row, :] += rows[k]
        total[at : at + 1, :] = merge_ref[...]
        total[at + 1 : at + 2, :] = down_ref[...]
        for rel in range(groups):
            owner = me_ref[0] ^ rel
            for n in range(groups):

                @pl.when(owner == n)
                def _():
                    own = total[:, n * part : (n + 1) * part]
                    out_refs[rel][:at, :] = own[:at]
                    out_refs[rel][at + 2 : at + 4, :] = own[at : at + 2]

            out_refs[rel][at : at + 1, :] = qkv_ref[rel, :, :part]
            out_refs[rel][at + 1 : at + 2, :] = qkv_ref[rel, :, 2 * part :]
            for j in range(units // part):
                out_refs[rel][at + 4 + j : at + 5 + j, :] = up_ref[rel, :, j * part : (j + 1) * part]

    return pl.pallas_call(
        kernel,
        grid_spec=pltpu.PrefetchScalarGridSpec(
            num_scalar_prefetch=2,
            grid=(1,),
            in_specs=[whole(a) for a in ins],
            out_specs=[whole(a) for a in outs],
            scratch_shapes=[pltpu.VMEM((at + 8, width), F32)],
        ),
        out_shape=outs,
        compiler_params=params(16),
        name="pack",
    )(span_clip, narrow_me.astype(jnp.int32)[None], *ins)


def sum_over(block, axis):
    for bit in bits_of(lax.axis_size(axis)):
        block = block + swap(block, axis, bit)
    return block


def collect(block, axis):
    block = block[None]
    for bit in bits_of(lax.axis_size(axis)):
        block = jnp.concatenate([block, swap(block, axis, bit)], axis=0)
    return block


def turned(block, axis):
    count = lax.axis_size(axis)
    bits = bits_of(count)
    rest = block.shape[1:]
    block = block.reshape([2] * len(bits) + list(rest))
    for dim, bit in enumerate(reversed(bits)):
        block = jnp.where(my_bit(axis, bit) == 1, jnp.flip(block, dim), block)
    return block.reshape((count,) + rest)


def share(block, count):
    for bit in bits_of(count):
        groups, rows, cols = block.shape
        pair = block.reshape(groups // 2, 2, rows, cols)
        kept, got = pair[:, 0], swap(pair[:, 1], "narrow", bit)
        mine = my_bit("narrow", bit) == 1
        block = jnp.concatenate([jnp.where(mine, got, kept), jnp.where(mine, kept, got)], axis=1)
    return block


def unshare(block, count):
    for bit in reversed(bits_of(count)):
        groups, rows, cols = block.shape
        pair = block.reshape(groups, 2, rows // 2, cols)
        mine = my_bit("narrow", bit)
        kept = lax.dynamic_index_in_dim(pair, mine, 1, True)
        got = swap(lax.dynamic_index_in_dim(pair, 1 - mine, 1, True), "narrow", bit)
        block = jnp.concatenate([kept, got], axis=1).reshape(2 * groups, rows // 2, cols)
    return block


def shards(
    tokens,
    condition,
    frame_clip,
    mod_weight,
    mod_bias,
    project_weight,
    project_bias,
    merge_weight,
    merge_bias,
    up_weight,
    up_bias,
    down_weight,
    down_bias,
    out_cotangent,
):
    rows, width = tokens.shape
    wide_count, narrow_count = lax.axis_size("wide"), lax.axis_size("narrow")
    wide_me, narrow_me = lax.axis_index("wide"), lax.axis_index("narrow")
    depth = width // wide_count
    part = width // narrow_count
    units = up_weight.shape[1]
    heads = part // HEAD
    clips = condition.shape[0]
    span = math.gcd(rows, PATCHES)
    spans = rows // span
    sharing = PATCHES // span

    def twin(*blocks):
        return Sent(*[swap(block, "wide", 1) for block in blocks])

    def hop(block, axis, bit):
        return Sent(swap(block, axis, bit))

    attn = Gather(
        jnp.concatenate([project_weight.reshape(depth, 3 * part), merge_weight.T], axis=1)
    )
    up, down_shard = Gather(up_weight), down_weight.T
    attn.start()
    z_bits = bits_of(wide_count)[1:]
    narrow_bits = bits_of(narrow_count)
    active = jax.nn.silu(condition).astype(BF16)
    active_mine = lax.dynamic_slice_in_dim(active, wide_me * depth, depth, 1)
    mode_part = jnp.einsum("cd,dki->kci", active_mine, mod_weight, preferred_element_type=F32)
    unit_rows = units // part
    at = 6 * clips
    mode_part = mode_part + swap(mode_part, "wide", 1)
    for bit in z_bits:
        sent = hop(mode_part, "wide", bit)
        if bit == z_bits[0]:
            (mode_part,) = land([sent, attn], mode_part)
        else:
            mode_part, attn.own = land([sent], mode_part, attn.own)
        mode_part = mode_part + sent.got[0]
    small = jnp.concatenate(
        [
            (mode_part + mod_bias.astype(F32)[:, None]).reshape(at, part),
            project_bias.astype(F32),
            merge_bias.astype(F32)[None],
            down_bias.astype(F32)[None],
            up_bias.astype(F32).reshape(unit_rows, part),
        ],
        axis=0,
    )
    span_frame = (narrow_me * rows + jnp.arange(spans, dtype=jnp.int32) * span) // PATCHES
    span_clip = jnp.sum(
        jnp.where(
            span_frame[:, None] == jnp.arange(frame_clip.shape[0], dtype=jnp.int32)[None],
            frame_clip[None],
            0,
        ),
        axis=1,
    )
    attn.start()
    sent = Sent(*spread(small, "narrow", narrow_bits)[1:])
    small, span_clip, up.own = land([sent, attn], small, span_clip, up.own)
    while attn.in_front():
        attn.start()
        land([attn])
    attn.start()
    up.start()
    modes, out_bias, qkv_bias, up_bias_all, core_grad, down_bias_grad, core_own, core_other = unpack_call(
        span_clip, narrow_me, clips, [small, *sent.got], out_cotangent
    )
    (modes,) = land([attn, up, attn.cross("own")], modes)
    while len(up.front) - up.stage > 1:
        up.start()
        land([up])
    attn.start()
    up.start()
    modes, down_shard = land([attn, up, attn.cross("first")], modes, down_shard)
    down = Whole(down_shard)
    attn_far = attn.cross("second", "third", "fourth")
    up.start()
    modes, up.own = land([attn_far], modes, up.own)
    attn.finish()

    attn_w = Weight(attn)
    up_own = up.cross("own")
    hidden_a, qkv, merge_w = project_call(attn_w, tokens, modes, qkv_bias, part)
    qkv, hidden_a = land([up, up_own], qkv, hidden_a)
    up.start()
    up_near = up.cross("first")
    qkv_frames = share(qkv, sharing)
    attended = attend(qkv_frames, heads)
    if sharing > 1:
        attended = attended.reshape(rows * sharing, narrow_count // sharing, part)
        attended = unshare(attended.transpose(1, 0, 2), sharing)
        attended = attended.transpose(1, 0, 2).reshape(rows, width)
    attended, hidden_a = land([up, up_near], attended, hidden_a)
    up_far = up.cross("second", "third", "fourth")
    branch_a, hidden_b = merge_call(attended, merge_w, tokens, modes, out_bias[0])
    hidden_b, attended, hidden_a = land([up_far], hidden_b, attended, hidden_a)
    up.finish()
    hidden_own, hidden_other = turn(hidden_a)
    hidden_twin = twin(hidden_other)
    up_w = Weight(up)
    gelu, slope, sent_part = up_call(up_w, hidden_b, up_bias_all, core_other)

    gelu, slope, hidden_b, sent_part = land([hidden_twin], gelu, slope, hidden_b, sent_part)
    down_cross = twin(sent_part)
    hidden_b_own, hidden_b_other = turn(hidden_b)
    down_w = down.finish()
    upper_grad, up_bias_grad, sent_part = gelu_back_call(down_w, core_grad, slope, hidden_b_other)
    upper_grad, sent_part, attended, gelu, core_own = land(
        [down_cross], upper_grad, sent_part, attended, gelu, core_own
    )
    up_cross = twin(sent_part)
    down_parts = weight_grad_call([core_own], [gelu], [], [], units, down_cross.got[0])
    upper_grad, attended, *down_parts = land([up_cross], upper_grad, attended, *down_parts)
    down_scatter = Scatter(*down_parts)
    attended_twin = twin(attended)
    middle_grad, merged_grad, sums_b, merge_bias_grad = up_back_call(
        up_w, upper_grad, tokens, branch_a, modes, out_cotangent
    )
    merged_grad, upper_grad = land([attended_twin], merged_grad, upper_grad)
    merged_own, merged_other = turn(merged_grad)
    merged_twin = twin(merged_other)
    (merged_grad,) = land([], merged_grad)

    if sharing > 1:
        attended_grad = jnp.dot(merged_grad, merge_w, preferred_element_type=F32).astype(BF16)
        attended_grad = attended_grad.reshape(rows, narrow_count, part).transpose(1, 0, 2)
        attended_grad = share(attended_grad, sharing).transpose(1, 0, 2)
        attended_grad = attended_grad.reshape(rows * sharing, width // sharing)
        qkv_grad = unshare(attend_back(qkv_frames, attended_grad, heads), sharing)
    else:
        qkv_grad = attend_back(qkv_frames, merged_grad, heads, merge_w)
    qkv_grad, upper_grad = land([down_scatter, merged_twin], qkv_grad, upper_grad)
    qkv_twin = twin(qkv_grad)
    up_parts = weight_grad_call(
        [hidden_b_own],
        [upper_grad],
        [merged_own, merged_twin.got[0]],
        [attended, attended_twin.got[0]],
        units,
        up_cross.got[0],
    )
    qkv_grad, *up_parts = land([down_scatter, qkv_twin], qkv_grad, *up_parts)
    up_scatter = Scatter(*up_parts)
    tokens_grad, sums_a, qkv_sums = project_back_call(
        attn_w, qkv_grad, tokens, middle_grad, modes, 3 * part
    )
    sums_a, qkv_grad = land([down_scatter], sums_a, qkv_grad)
    attn_parts = weight_grad_call(
        [hidden_own, hidden_twin.got[0]],
        [qkv_grad, qkv_twin.got[0]],
        [],
        [],
        3 * part,
    )
    gelu, *attn_parts = land([down_scatter], gelu, *attn_parts)
    attn_scatter = Scatter(*attn_parts)
    output, sums_g = down_call(
        down_w, gelu, tokens, branch_a, modes, out_bias[1], out_cotangent
    )
    sums_g, *up_scatter.kept = land([up_scatter.wait()], sums_g, *up_scatter.kept)

    lower, upper = pack_call(
        span_clip, narrow_me, clips, sums_a, sums_b, sums_g, merge_bias_grad, down_bias_grad,
        qkv_sums, up_bias_grad,
    )
    sent = hop(upper, "narrow", narrow_bits[-1])
    up_scatter.go()
    lower, *attn_scatter.kept = land([sent, attn_scatter.wait()], lower, *attn_scatter.kept)
    packed = lower + sent.got[0]
    for bit in reversed(narrow_bits[:-1]):
        sent = hop(packed[bit:], "narrow", bit)
        packed, *attn_scatter.kept = land([sent], packed, *attn_scatter.kept)
        packed = packed[:bit] + sent.got[0]
    packed = packed[0]
    attn_scatter.go()
    sent = hop(packed, "wide", 1)
    (packed,) = land([sent], packed)
    packed = packed + sent.got[0]
    for bit in z_bits:
        sent = hop(packed, "wide", bit)
        (packed,) = land([sent], packed)
        packed = packed + sent.got[0]
    clip_slice = packed[:at].reshape(6, clips, part)
    active_grad = jnp.einsum(
        "kci,dki->cd", clip_slice, mod_weight.astype(F32), precision=lax.Precision.HIGHEST
    )
    (active_grad,) = land([up_scatter], active_grad)
    for bit in narrow_bits:
        sent = hop(active_grad, "narrow", bit)
        (active_grad,) = land(
            [sent, attn_scatter] if bit == narrow_bits[0] else [sent], active_grad
        )
        active_grad = active_grad + sent.got[0]
    active_grad = active_grad[None]
    for bit in bits_of(wide_count):
        sent = hop(active_grad, "wide", bit)
        scatters = {1: [up_scatter], z_bits[0]: [attn_scatter]}
        (active_grad,) = land([sent, *scatters.get(bit, [])], active_grad)
        active_grad = jnp.concatenate([active_grad, sent.got[0]], axis=0)
    active_grad = turned(active_grad, "wide").transpose(1, 0, 2).reshape(clips, width)
    unused, silu_pullback = jax.vjp(jax.nn.silu, condition)
    condition_grad = silu_pullback(active_grad)[0]
    mod_bias_grad = jnp.sum(clip_slice, axis=1)
    mod_weight_grad = jnp.einsum(
        "cd,kci->dki", active_mine.astype(F32), clip_slice, precision=lax.Precision.HIGHEST
    )

    for scatter in (down_scatter, up_scatter, attn_scatter):
        while scatter.stage < scatter.stages:
            land([scatter])
    return (
        output,
        tokens_grad,
        condition_grad,
        mod_weight_grad,
        mod_bias_grad,
        attn_scatter.result.reshape(depth, 3, part),
        packed[at : at + 2],
        up_scatter.result[:, units:].T,
        packed[at + 2],
        up_scatter.result[:, :units],
        packed[at + 4 :].reshape(units),
        down_scatter.result.T,
        packed[at + 3],
    )


def solution(mesh):
    both = P(("wide", "narrow"), None)
    ins = (
        both,
        P(),
        P("wide"),
        P("wide", None, "narrow"),
        P(None, "narrow"),
        P("wide", None, "narrow"),
        P(None, "narrow"),
        P("narrow", "wide"),
        P("narrow"),
        P("wide", "narrow"),
        P("narrow"),
        P("narrow", "wide"),
        P("narrow"),
        both,
    )
    outs = (
        both,
        both,
        P(),
        P("wide", None, "narrow"),
        P(None, "narrow"),
        P("wide", None, "narrow"),
        P(None, "narrow"),
        P("narrow", "wide"),
        P("narrow"),
        P("wide", "narrow"),
        P("narrow"),
        P("narrow", "wide"),
        P("narrow"),
    )
    return jax.shard_map(shards, mesh=mesh, in_specs=ins, out_specs=outs, check_vma=False)
```

time: 538 us -> 479 us (0.89)
  Pallas kernels: 226 us -> 200 us
  waiting for transfers between devices: 172 us -> 153 us
  between operations: 2.23 us -> 15.4 us
  starting transfers between devices: 64.3 us -> 53.4 us
  other arithmetic: 39 us -> 31.5 us
    pallas_call x7 -> x4, Pallas kernels: 83.5 us -> 57.7 us  [the longest x3 38.4 us: weight_grad_call(): pl.pallas_call(kernel, grid=(groups,), in_specs=[whole(a) for a in lefts]...]
    ppermute x76 -> x62, waiting for transfers between devices: 172 us -> 153 us  [swap(): return lax.ppermute(block, axis, [(i, i ^ bit) for i in range(count)])]
    ppermute x76 -> x62, starting transfers between devices: 64.3 us -> 53.4 us  [swap(): return lax.ppermute(block, axis, [(i, i ^ bit) for i in range(count)])]
    pallas_call x6, Pallas kernels: 112 us -> 119 us  [weight_call(): pl.pallas_call(kernel, grid_spec=pltpu.PrefetchScalarGridSpec(num_scalar_...]
    pallas_call x1, Pallas kernels: 17.7 us -> 11.7 us  [attend(): pl.pallas_call(functools.partial(attend_kernel, heads), grid=(rows // PAT...]
    unnamed x171 -> x141, local copies, waits for them, and re-layouts: 17.3 us -> 11.8 us
    convert_element_type x19 -> x15, other arithmetic: 28.6 us -> 24.2 us  [plus(): return (a.astype(F32) + b.astype(F32)).astype(BF16)]
  transfers between devices with their start and end apart: 76 -> 63, of which waited for: 28 -> 35; matrix products, arithmetic and copies ran while one was open for 8% -> 8% of each run, Pallas kernels for 42% -> 42%
where the time goes in v3:
time: 479 us; the launch traced here: 475 us
  Pallas kernels  200 us (42%)
  waiting for transfers between devices  153 us (32%)
  starting transfers between devices  53.4 us (11%)
  other arithmetic  31.5 us (7%)
  local copies, waits for them, and re-layouts  18.5 us (4%)
  between operations  15.4 us (3%)
    ppermute x62, waiting for transfers between devices, swap(): return lax.ppermute(block, axis, [(i, i ^ bit) for i in range(count)])  153 us
    pallas_call x6, Pallas kernels, weight_call(): pl.pallas_call(kernel, grid_spec=pltpu.PrefetchScalarGridSpec(num_scalar_...  119 us
    ppermute x62, starting transfers between devices, swap(): return lax.ppermute(block, axis, [(i, i ^ bit) for i in range(count)])  53.4 us
    pallas_call x3, Pallas kernels, weight_grad_call(): pl.pallas_call(kernel, grid=(groups,), in_specs=[whole(a) for a in lefts]...  38.4 us
    convert_element_type x15, other arithmetic, plus(): return (a.astype(F32) + b.astype(F32)).astype(BF16)  24.2 us
    pallas_call x1, Pallas kernels, attend_back(): pl.pallas_call(functools.partial(attend_back_kernel, heads), grid=(rows /...  19.3 us
    unnamed x141, local copies, waits for them, and re-layouts  11.8 us
    pallas_call x1, Pallas kernels, attend(): pl.pallas_call(functools.partial(attend_kernel, heads), grid=(rows // PAT...  11.7 us
  transfers between devices with their start and end apart: 63, of which 35 were waited for; matrix products, arithmetic and copies ran while one was open for 8% of the time, Pallas kernels for 42%

profile of v3, /device:TPU:0, one launch (start us, length us, event | category | flops | bytes accessed | tf_op | source)
XLA Modules:
  0.0 474.7 jit_solution(2240655709295808366)
XLA Ops:
  8.9 4.1 collective-permute-start.2
  16.6 6.7 %collective-permute-done.1 = f32[6,12,288]{2,1,0:T(8,128)S(1)} collective-permute-done((f32[6,12,288]{2,1,0:T(8,128)S(1)}, f32[6,12,288]{2,1,0:T(8,128)S(1)}, u32[]{:S(2)}, u32[]{:S(2)}) %collective-permute-start.1) | collective-permute-done | bytes 82976 | tf_op jit(solution)/shard_map/ppermute | solution.py:25
  23.3 4.6 collective-permute-done.2
  28.1 9.1 %collective-permute-done.3 = f32[6,12,288]{2,1,0:T(8,128)S(1)} collective-permute-done((f32[6,12,288]{2,1,0:T(8,128)S(1)}, f32[6,12,288]{2,1,0:T(8,128)S(1)}, u32[]{:S(2)}, u32[]{:S(2)}) %collective-permute-start.3) | collective-permute-done | bytes 82976 | tf_op jit(solution)/shard_map/ppermute | solution.py:25
  46.4 5.1 %collective-permute-done.7 = bf16[2,144,1152]{2,1,0:T(8,128)(2,1)} collective-permute-done((bf16[2,144,1152]{2,1,0:T(8,128)(2,1)S(1)}, bf16[2,144,1152]{2,1,0:T(8,128)(2,1)}, u32[]{:S(2)}, u32[]{:S(2)}) %collective-permute-start.7) | collective-permute-done | bytes 663584 | tf_op jit(solution)/shard_map/ppermute | solution.py:25
  59.6 13.8 %collective-permute-done.10 = bf16[1,144,1152]{2,1,0:T(8,128)(2,1)S(1)} collective-permute-done((bf16[1,144,1152]{2,1,0:T(8,128)(2,1)S(1)}, bf16[1,144,1152]{2,1,0:T(8,128)(2,1)S(1)}, u32[]{:S(2)}, u32[]{:S(2)}) %collective-permute-start.10) | collective-permute-done | bytes 331808 | tf_op jit(solution)/shard_map/ppermute | solution.py:25
  73.4 10.9 %collective-permute-done.8.refs_4_.refs_5_ = bf16[4,144,1152]{2,1,0:T(8,128)(2,1)S(1)} collective-permute-done((bf16[4,144,1152]{2,1,0:T(8,128)(2,1)S(1)}, bf16[4,144,1152]{2,1,0:T(8,128)(2,1)S(1)}, u32[]{:S(2)}, u32[]{:S(2)}) %collective-permute-start.8) | collective-permute-done | bytes 1327136 | tf_op jit(solution)/shard_map/ppermute | solution.py:25
  89.1 13.8 %collective-permute-done.12.refs_6_.refs_7_ = bf16[4,64,1152]{2,1,0:T(8,128)(2,1)} collective-permute-done((bf16[4,64,1152]{2,1,0:T(8,128)(2,1)S(1)}, bf16[4,64,1152]{2,1,0:T(8,128)(2,1)}, u32[]{:S(2)}, u32[]{:S(2)}) %collective-permute-start.12) | collective-permute-done | bytes 589856 | tf_op jit(solution)/shard_map/ppermute | solution.py:25
  112.7 17.3 %project.1 = (bf16[768,1152]{1,0:T(8,128)(2,1)}, bf16[4,768,864]{2,1,0:T(8,128)(2,1)}, bf16[1152,1152]{1,0:T(8,128)(2,1)}) custom-call(s32[2]{0:T(128)} %pad_add_fusion.me_ref, bf16[768,1152]{1,0:T(8,128)(2,1)} %refs_1_.5, f32[3,6,1152]{2,1,0:T(8,128)} %copy-done.2, f32[4,1,864]{2,1,0:T(1,128)} %copy-done.16, bf16[4,144,1152]{2,1,0:T(8,128)(2,1)} %copy-done.24, ...), custom_call_target="tpu_custom_call" | custom-call | flops 1000000000 | bytes 1 | tf_op jit(solution)/shard_map/project/pallas_call | solution.py:362
  130.0 14.7 %collective-permute-done.16.refs_4_.refs_6_ = bf16[4,144,1152]{2,1,0:T(8,128)(2,1)S(1)} collective-permute-done((bf16[4,144,1152]{2,1,0:T(8,128)(2,1)S(1)}, bf16[4,144,1152]{2,1,0:T(8,128)(2,1)S(1)}, u32[]{:S(2)}, u32[]{:S(2)}) %collective-permute-start.16) | collective-permute-done | bytes 1327136 | tf_op jit(solution)/shard_map/ppermute | solution.py:25
  149.8 11.7 %attend.1.attended_ref.refs_5_ = bf16[768,1152]{1,0:T(8,128)(2,1)} custom-call(bf16[4,768,864]{2,1,0:T(8,128)(2,1)} %get-tuple-element.221.qkv_ref), custom_call_target="tpu_custom_call" | custom-call | flops 1000000000 | bytes 1 | tf_op jit(solution)/shard_map/attend/pallas_call | solution.py:106
  166.0 7.7 %merge.1 = (f32[768,1152]{1,0:T(8,128)}, bf16[768,1152]{1,0:T(8,128)(2,1)}) custom-call(bf16[768,1152]{1,0:T(8,128)(2,1)} %attend.1.attended_ref.refs_5_, bf16[1152,1152]{1,0:T(8,128)(2,1)} %get-tuple-element.226.weight_ref.refs_0_, bf16[768,1152]{1,0:T(8,128)(2,1)} %refs_1_.5, f32[3,6,1152]{2,1,0:T(8,128)} %copy-done.2, f32[1,1152]{1,0:T(1,128)} %get-tuple-element.414.bias_ref), custom_call_target="tpu_custom_call" | custom-call | flops 1000000000 | bytes 1 | tf_op jit(solution)/shard_map/merge/pallas_call | solution.py:444
  175.7 22.5 %up.1 = (bf16[4,768,1152]{2,1,0:T(8,128)(2,1)}, bf16[4,768,1152]{2,1,0:T(8,128)(2,1)}, bf16[4,4,144,1152]{3,2,1,0:T(8,128)(2,1)}) custom-call(s32[2]{0:T(128)} %pad_add_fusion.me_ref, bf16[768,1152]{1,0:T(8,128)(2,1)} %get-tuple-element.246.refs_0_.block_ref, f32[4,1,1152]{2,1,0:T(1,128)} %copy-done.15, bf16[4,144,768]{2,1,0:T(8,128)(2,1)} %copy-done.8, ...), custom_call_target="tpu_custom_call" | custom-call | flops 1000000000 | bytes 1 | tf_op jit(solution)/shard_map/up/pallas_call | solution.py:362
  202.0 21.2 %gelu_back.1 = (bf16[4,768,1152]{2,1,0:T(8,128)(2,1)}, f32[4,1,1152]{2,1,0:T(1,128)}, bf16[4,4,144,1152]{3,2,1,0:T(8,128)(2,1)}) custom-call(s32[2]{0:T(128)} %pad_add_fusion.me_ref, bf16[768,1152]{1,0:T(8,128)(2,1)} %copy-done.3, bf16[4,768,1152]{2,1,0:T(8,128)(2,1)} %get-tuple-element.245.refs_1_, bf16[4,144,768]{2,1,0:T(8,128)(2,1)} %copy-done.11, ...), custom_call_target="tpu_custom_call" | custom-call | flops 1000000000 | bytes 1 | tf_op jit(solution)/shard_map/gelu_back/pallas_call | solution.py:362
  223.4 10.8 %weight_grad.3 = (bf16[2,4,64,1152]{3,2,1,0:T(8,128)(2,1)}, bf16[2,4,64,1152]{3,2,1,0:T(8,128)(2,1)}, bf16[2,4,80,1152]{3,2,1,0:T(8,128)(2,1)}, bf16[2,4,80,1152]{3,2,1,0:T(8,128)(2,1)}) custom-call(bf16[4,144,768]{2,1,0:T(8,128)(2,1)} %copy-done.7, bf16[4,768,1152]{2,1,0:T(8,128)(2,1)} %get-tuple-element.302.refs_1_.refs_0_, ...), custom_call_target="tpu_custom_call" | custom-call | flops 1000000000 | bytes 1 | tf_op jit(solution)/shard_map/weight_grad/pallas_call | solution.py:760
  234.6 2.6 collective-permute-start.32
  239.4 20.8 %up_back.1 = (f32[768,1152]{1,0:T(8,128)}, bf16[768,1152]{1,0:T(8,128)(2,1)}, f32[3,3,1152]{2,1,0:T(4,128)}, f32[1,1152]{1,0:T(1,128)}) custom-call(s32[2]{0:T(128)} %pad_add_fusion.me_ref, bf16[4,768,1152]{2,1,0:T(8,128)(2,1)} %get-tuple-element.279.refs_0_.refs_1_, bf16[768,1152]{1,0:T(8,128)(2,1)} %refs_1_.5, f32[768,1152]{1,0:T(8,128)} %get-tuple-element.269.refs_2_, ...), custom_call_target="tpu_custom_call" | custom-call | flops 1000000000 | bytes 1 | tf_op jit(solution)/shard_map/up_back/pallas_call | solution.py:362
  263.2 19.3 %attend_back.1.refs_0_.refs_2_ = bf16[4,768,896]{2,1,0:T(8,128)(2,1)} custom-call(bf16[4,768,864]{2,1,0:T(8,128)(2,1)} %get-tuple-element.221.qkv_ref, bf16[768,1152]{1,0:T(8,128)(2,1)} %get-tuple-element.271.block_ref.grad_ref, bf16[1152,1152]{1,0:T(8,128)(2,1)} %get-tuple-element.226.weight_ref.refs_0_), custom_call_target="tpu_custom_call" | custom-call | flops 1000000000 | bytes 1 | tf_op jit(solution)/shard_map/attend_back/pallas_call | solution.py:153
  283.1 2.7 add_convert_fusion.4
  288.1 15.3 %weight_grad.4 = (bf16[2,4,64,1440]{3,2,1,0:T(8,128)(2,1)}, bf16[2,4,64,1440]{3,2,1,0:T(8,128)(2,1)}, bf16[2,4,80,1440]{3,2,1,0:T(8,128)(2,1)}, bf16[2,4,80,1440]{3,2,1,0:T(8,128)(2,1)}) custom-call(bf16[4,144,768]{2,1,0:T(8,128)(2,1)} %copy-done.9, bf16[4,768,1152]{2,1,0:T(8,128)(2,1)} %get-tuple-element.279.refs_0_.refs_1_, ...), custom_call_target="tpu_custom_call" | custom-call | flops 1000000000 | bytes 1 | tf_op jit(solution)/shard_map/weight_grad/pallas_call | solution.py:760
  309.7 18.1 %project_back.1 = (f32[768,1152]{1,0:T(8,128)}, f32[3,2,1152]{2,1,0:T(2,128)}, f32[4,1,864]{2,1,0:T(1,128)}) custom-call(s32[2]{0:T(128)} %pad_add_fusion.me_ref, bf16[4,768,896]{2,1,0:T(8,128)(2,1)} %attend_back.1.refs_0_.refs_2_, bf16[768,1152]{1,0:T(8,128)(2,1)} %refs_1_.5, f32[768,1152]{1,0:T(8,128)} %get-tuple-element.291.refs_2_, ...), custom_call_target="tpu_custom_call" | custom-call | flops 1000000000 | bytes 1 | tf_op jit(solution)/shard_map/project_back/pallas_call | solution.py:362
  329.9 12.3 %weight_grad.5 = (bf16[2,4,64,864]{3,2,1,0:T(8,128)(2,1)}, bf16[2,4,64,864]{3,2,1,0:T(8,128)(2,1)}, bf16[2,4,80,864]{3,2,1,0:T(8,128)(2,1)}, bf16[2,4,80,864]{3,2,1,0:T(8,128)(2,1)}) custom-call(bf16[4,144,768]{2,1,0:T(8,128)(2,1)} %copy-done.6, bf16[4,144,768]{2,1,0:T(8,128)(2,1)} %copy-done.51, bf16[4,768,896]{2,1,0:T(8,128)(2,1)} %attend_back.1.refs_0_.refs_2_, ...), custom_call_target="tpu_custom_call" | custom-call | flops 1000000000 | bytes 1 | tf_op jit(solution)/shard_map/weight_grad/pallas_call | solution.py:760
  342.2 2.8 collective-permute-done.39
  346.8 18.6 %down.1 = (bf16[768,1152]{1,0:T(8,128)(2,1)}, f32[3,1,1152]{2,1,0:T(1,128)}) custom-call(s32[2]{0:T(128)} %pad_add_fusion.me_ref, bf16[4,768,1152]{2,1,0:T(8,128)(2,1)} %get-tuple-element.302.refs_1_.refs_0_, bf16[768,1152]{1,0:T(8,128)(2,1)} %refs_1_.5, f32[768,1152]{1,0:T(8,128)} %get-tuple-element.269.refs_2_, f32[3,6,1152]{2,1,0:T(8,128)} %copy-done.2, ...), custom_call_target="tpu_custom_call" | custom-call | flops 1000000000 | bytes 1 | tf_op jit(solution)/shard_map/down/pallas_call | solution.py:362
  368.1 3.2 add_convert_fusion
  375.4 2.9 add_convert_fusion.2
  382.5 2.6 add_convert_fusion.8
  391.1 5.1 %collective-permute-done.50 = f32[80,288]{1,0:T(8,128)S(1)} collective-permute-done((f32[80,288]{1,0:T(8,128)S(1)}, f32[80,288]{1,0:T(8,128)S(1)}, u32[]{:S(2)}, u32[]{:S(2)}) %collective-permute-start.50) | collective-permute-done | bytes 92192 | tf_op jit(solution)/shard_map/ppermute | solution.py:25
  416.2 14.3 %collective-permute-done.56 = bf16[2,144,1440]{2,1,0:T(8,128)(2,1)} collective-permute-done((bf16[2,144,1440]{2,1,0:T(8,128)(2,1)}, bf16[2,144,1440]{2,1,0:T(8,128)(2,1)}, u32[]{:S(2)}, u32[]{:S(2)}) %collective-permute-start.56) | collective-permute-done | bytes 829472 | tf_op jit(solution)/shard_map/ppermute | solution.py:25
  432.5 6.2 %collective-permute-done.58 = bf16[2,144,864]{2,1,0:T(8,128)(2,1)S(1)} collective-permute-done((bf16[2,144,864]{2,1,0:T(8,128)(2,1)S(1)}, bf16[2,144,864]{2,1,0:T(8,128)(2,1)S(1)}, u32[]{:S(2)}, u32[]{:S(2)}) %collective-permute-start.58) | collective-permute-done | bytes 497696 | tf_op jit(solution)/shard_map/ppermute | solution.py:25
  439.2 3.0 collective-permute-start.60
  442.2 17.1 %collective-permute-done.59 = f32[4,12,144]{2,1,0:T(8,128)S(1)} collective-permute-done((f32[4,12,144]{2,1,0:T(8,128)S(1)}, f32[4,12,144]{2,1,0:T(8,128)S(1)}, u32[]{:S(2)}, u32[]{:S(2)}) %collective-permute-start.59) | collective-permute-done | bytes 27680 | tf_op jit(solution)/shard_map/ppermute | solution.py:25
  (330 shorter events, 118.3 us)
Async XLA Ops:
  7.2 194.8 %all-gather.3.cloned.1.call-start = ((), (), s32[]{:S(2)}) async-start(), calls=%async_computation | async-start | bytes 10948608 | tf_op jit(solution)/shard_map/all_gather | solution.py:293
  52.7 20.8 %collective-permute-start.11 = (bf16[4,144,1152]{2,1,0:T(8,128)(2,1)S(1)}, bf16[4,144,1152]{2,1,0:T(8,128)(2,1)S(1)}, u32[]{:S(2)}, u32[]{:S(2)}) collective-permute-start(bf16[4,144,1152]{2,1,0:T(8,128)(2,1)S(1)} %constant_dynamic-update-slice_fusion.refs_3_.refs_4_), channel_id=1, source_target_pairs={{0,4},{4,0},{8,12},{12,8},{16,20},{20,16},{24,28},{28,24},{1,5},{5... | collective-permute-start | bytes 3981320 | tf_op jit(solution)/shard_map/ppermute | solution.py:25
  52.7 31.5 %collective-permute-start.8 = (bf16[4,144,1152]{2,1,0:T(8,128)(2,1)S(1)}, bf16[4,144,1152]{2,1,0:T(8,128)(2,1)S(1)}, u32[]{:S(2)}, u32[]{:S(2)}) collective-permute-start(bf16[4,144,1152]{2,1,0:T(8,128)(2,1)S(1)} %constant_dynamic-update-slice_fusion.refs_3_.refs_4_), channel_id=1, source_target_pairs={{0,2},{1,3},{2,0},{3,1},{4,6},{5,7},{6,4},{7,5},{8,10},{9,11},{10,... | collective-permute-start | bytes 3981320 | tf_op jit(solution)/shard_map/ppermute | solution.py:25
  54.3 31.2 %collective-permute-start.9 = (bf16[4,144,1152]{2,1,0:T(8,128)(2,1)S(1)}, bf16[4,144,1152]{2,1,0:T(8,128)(2,1)S(1)}, u32[]{:S(2)}, u32[]{:S(2)}) collective-permute-start(bf16[4,144,1152]{2,1,0:T(8,128)(2,1)S(1)} %constant_dynamic-update-slice_fusion.refs_3_.refs_4_), channel_id=1, source_target_pairs={{0,1},{1,0},{2,3},{3,2},{4,5},{5,4},{6,7},{7,6},{8,9},{9,8},{10,11... | collective-permute-start | bytes 3981320 | tf_op jit(solution)/shard_map/ppermute | solution.py:25
  85.5 19.1 %collective-permute-start.15 = (bf16[4,144,1152]{2,1,0:T(8,128)(2,1)S(1)}, bf16[4,144,1152]{2,1,0:T(8,128)(2,1)S(1)}, u32[]{:S(2)}, u32[]{:S(2)}) collective-permute-start(bf16[4,144,1152]{2,1,0:T(8,128)(2,1)S(1)} %collective-permute-done.8.refs_4_.refs_5_), channel_id=1, source_target_pairs={{0,4},{4,0},{8,12},{12,8},{16,20},{20,16},{24,28},{28,24},{1,5},{5... | collective-permute-start | bytes 3981320 | tf_op jit(solution)/shard_map/ppermute | solution.py:25
  85.6 19.1 %collective-permute-start.13 = (bf16[4,80,1152]{2,1,0:T(8,128)(2,1)S(1)}, bf16[4,80,1152]{2,1,0:T(8,128)(2,1)}, u32[]{:S(2)}, u32[]{:S(2)}) collective-permute-start(bf16[4,80,1152]{2,1,0:T(8,128)(2,1)S(1)} %slice.118), channel_id=1, source_target_pairs={{0,2},{1,3},{2,0},{3,1},{4,6},{5,7},{6,4},{7,5},{8,10},{9,11},{10,... | collective-permute-start | bytes 2211848 | tf_op jit(solution)/shard_map/ppermute | solution.py:25
  106.6 38.1 %collective-permute-start.16 = (bf16[4,144,1152]{2,1,0:T(8,128)(2,1)S(1)}, bf16[4,144,1152]{2,1,0:T(8,128)(2,1)S(1)}, u32[]{:S(2)}, u32[]{:S(2)}) collective-permute-start(bf16[4,144,1152]{2,1,0:T(8,128)(2,1)S(1)} %constant_dynamic-update-slice_fusion.2.refs_3_.refs_5_), channel_id=1, source_target_pairs={{0,2},{1,3},{2,0},{3,1},{4,6},{5,7},{6,4},{7,5},{8,10},{9,11},{10,... | collective-permute-start | bytes 3981320 | tf_op jit(solution)/shard_map/ppermute | solution.py:25
  107.2 38.5 %collective-permute-start.17 = (bf16[4,144,1152]{2,1,0:T(8,128)(2,1)S(1)}, bf16[4,144,1152]{2,1,0:T(8,128)(2,1)S(1)}, u32[]{:S(2)}, u32[]{:S(2)}) collective-permute-start(bf16[4,144,1152]{2,1,0:T(8,128)(2,1)S(1)} %constant_dynamic-update-slice_fusion.2.refs_3_.refs_5_), channel_id=1, source_target_pairs={{0,1},{1,0},{2,3},{3,2},{4,5},{5,4},{6,7},{7,6},{8,9},{9,8},{10,11... | collective-permute-start | bytes 3981320 | tf_op jit(solution)/shard_map/ppermute | solution.py:25
  111.8 33.8 %collective-permute-start.21 = (bf16[4,144,1152]{2,1,0:T(8,128)(2,1)S(1)}, bf16[4,144,1152]{2,1,0:T(8,128)(2,1)S(1)}, u32[]{:S(2)}, u32[]{:S(2)}) collective-permute-start(bf16[4,144,1152]{2,1,0:T(8,128)(2,1)S(1)} %constant_dynamic-update-slice_fusion.2.refs_3_.refs_5_), channel_id=1, source_target_pairs={{0,4},{4,0},{8,12},{12,8},{16,20},{20,16},{24,28},{28,24},{1,5},{5... | collective-permute-start | bytes 3981320 | tf_op jit(solution)/shard_map/ppermute | solution.py:25
  145.6 19.0 %collective-permute-start.25 = (bf16[4,144,1152]{2,1,0:T(8,128)(2,1)S(1)}, bf16[4,144,1152]{2,1,0:T(8,128)(2,1)S(1)}, u32[]{:S(2)}, u32[]{:S(2)}) collective-permute-start(bf16[4,144,1152]{2,1,0:T(8,128)(2,1)S(1)} %collective-permute-done.16.refs_4_.refs_6_), channel_id=1, source_target_pairs={{0,4},{4,0},{8,12},{12,8},{16,20},{20,16},{24,28},{28,24},{1,5},{5... | collective-permute-start | bytes 3981320 | tf_op jit(solution)/shard_map/ppermute | solution.py:25
  149.8 23.9 %collective-permute-start.22 = (bf16[4,144,1152]{2,1,0:T(8,128)(2,1)S(1)}, bf16[4,144,1152]{2,1,0:T(8,128)(2,1)}, u32[]{:S(2)}, u32[]{:S(2)}) collective-permute-start(bf16[4,144,1152]{2,1,0:T(8,128)(2,1)S(1)} %collective-permute-done.17.refs_5_.refs_7_), channel_id=1, source_target_pairs={{0,4},{4,0},{8,12},{12,8},{16,20},{20,16},{24,28},{28,24},{1,5},{5... | collective-permute-start | bytes 3981320 | tf_op jit(solution)/shard_map/ppermute | solution.py:25
  175.7 22.5 %collective-permute-start.28 = (bf16[4,144,768]{2,1,0:T(8,128)(2,1)S(1)}, bf16[4,144,768]{2,1,0:T(8,128)(2,1)S(1)}, u32[]{:S(2)}, u32[]{:S(2)}) collective-permute-start(bf16[4,144,768]{2,1,0:T(8,128)(2,1)S(1)} %get-tuple-element.231), channel_id=1, source_target_pairs={{0,4},{4,0},{8,12},{12,8},{16,20},{20,16},{24,28},{28,24},{1,5},{5... | collective-permute-start | bytes 2654216 | tf_op jit(solution)/shard_map/ppermute | solution.py:25
  199.1 24.1 %collective-permute-start.29 = (bf16[4,4,144,1152]{3,2,1,0:T(8,128)(2,1)}, bf16[4,4,144,1152]{3,2,1,0:T(8,128)(2,1)}, u32[]{:S(2)}, u32[]{:S(2)}) collective-permute-start(bf16[4,4,144,1152]{3,2,1,0:T(8,128)(2,1)} %get-tuple-element.243), channel_id=1, source_target_pairs={{0,4},{4,0},{8,12},{12,8},{16,20},{20,16},{24,28},{28,24},{1,5},{5... | collective-permute-start | bytes 15925256 | tf_op jit(solution)/shard_map/ppermute | solution.py:25
  234.2 26.0 %collective-permute-start.33 = (bf16[768,1152]{1,0:T(8,128)(2,1)S(1)}, bf16[768,1152]{1,0:T(8,128)(2,1)}, u32[]{:S(2)}, u32[]{:S(2)}) collective-permute-start(bf16[768,1152]{1,0:T(8,128)(2,1)S(1)} %copy-done.21), channel_id=1, source_target_pairs={{0,4},{4,0},{8,12},{12,8},{16,20},{20,16},{24,28},{28,24},{1,5},{5... | collective-permute-start | bytes 5308424 | tf_op jit(solution)/shard_map/ppermute | solution.py:25
  234.6 47.9 %collective-permute-start.32 = (bf16[2,4,80,1152]{3,2,1,0:T(8,128)(2,1)}, bf16[2,4,80,1152]{3,2,1,0:T(8,128)(2,1)}, u32[]{:S(2)}, u32[]{:S(2)}) collective-permute-start(bf16[2,4,80,1152]{3,2,1,0:T(8,128)(2,1)} %get-tuple-element.266), channel_id=1, source_target_pairs={{0,1},{1,0},{2,3},{3,2},{4,5},{5,4},{6,7},{7,6},{8,9},{9,8},{10,11... | collective-permute-start | bytes 4423688 | tf_op jit(solution)/shard_map/ppermute | solution.py:25
  237.2 45.4 %collective-permute-start.31 = (bf16[2,4,64,1152]{3,2,1,0:T(8,128)(2,1)}, bf16[2,4,64,1152]{3,2,1,0:T(8,128)(2,1)}, u32[]{:S(2)}, u32[]{:S(2)}) collective-permute-start(bf16[2,4,64,1152]{3,2,1,0:T(8,128)(2,1)} %get-tuple-element.265), channel_id=1, source_target_pairs={{0,2},{1,3},{2,0},{3,1},{4,6},{5,7},{6,4},{7,5},{8,10},{9,11},{10,... | collective-permute-start | bytes 3538952 | tf_op jit(solution)/shard_map/ppermute | solution.py:25
  263.2 19.4 %collective-permute-start.34 = (bf16[4,144,768]{2,1,0:T(8,128)(2,1)S(1)}, bf16[4,144,768]{2,1,0:T(8,128)(2,1)S(1)}, u32[]{:S(2)}, u32[]{:S(2)}) collective-permute-start(bf16[4,144,768]{2,1,0:T(8,128)(2,1)S(1)} %get-tuple-element.272), channel_id=1, source_target_pairs={{0,4},{4,0},{8,12},{12,8},{16,20},{20,16},{24,28},{28,24},{1,5},{5... | collective-permute-start | bytes 2654216 | tf_op jit(solution)/shard_map/ppermute | solution.py:25
  282.6 22.3 %collective-permute-start.37 = (bf16[4,768,896]{2,1,0:T(8,128)(2,1)}, bf16[4,768,896]{2,1,0:T(8,128)(2,1)}, u32[]{:S(2)}, u32[]{:S(2)}) collective-permute-start(bf16[4,768,896]{2,1,0:T(8,128)(2,1)} %attend_back.1.refs_0_.refs_2_), channel_id=1, source_target_pairs={{0,4},{4,0},{8,12},{12,8},{16,20},{20,16},{24,28},{28,24},{1,5},{5... | collective-permute-start | bytes 16515080 | tf_op jit(solution)/shard_map/ppermute | solution.py:25
  285.8 19.1 %collective-permute-start.36 = (bf16[4,80,1152]{2,1,0:T(8,128)(2,1)}, bf16[4,80,1152]{2,1,0:T(8,128)(2,1)}, u32[]{:S(2)}, u32[]{:S(2)}) collective-permute-start(bf16[4,80,1152]{2,1,0:T(8,128)(2,1)} %get-tuple-element.394), channel_id=1, source_target_pairs={{0,2},{1,3},{2,0},{3,1},{4,6},{5,7},{6,4},{7,5},{8,10},{9,11},{10,... | collective-permute-start | bytes 2211848 | tf_op jit(solution)/shard_map/ppermute | solution.py:25
  304.9 60.5 %collective-permute-start.41 = (bf16[2,4,80,1440]{3,2,1,0:T(8,128)(2,1)}, bf16[2,4,80,1440]{3,2,1,0:T(8,128)(2,1)}, u32[]{:S(2)}, u32[]{:S(2)}) collective-permute-start(bf16[2,4,80,1440]{3,2,1,0:T(8,128)(2,1)} %get-tuple-element.306), channel_id=1, source_target_pairs={{0,1},{1,0},{2,3},{3,2},{4,5},{5,4},{6,7},{7,6},{8,9},{9,8},{10,11... | collective-permute-start | bytes 5529608 | tf_op jit(solution)/shard_map/ppermute | solution.py:25
  307.6 20.3 %collective-permute-start.38 = (bf16[2,144,1152]{2,1,0:T(8,128)(2,1)S(1)}, bf16[2,144,1152]{2,1,0:T(8,128)(2,1)S(1)}, u32[]{:S(2)}, u32[]{:S(2)}) collective-permute-start(bf16[2,144,1152]{2,1,0:T(8,128)(2,1)S(1)} %pad_maximum_fusion.3), channel_id=1, source_target_pairs={{0,8},{4,12},{8,0},{12,4},{16,24},{20,28},{24,16},{28,20},{1,9},{5... | collective-permute-start | bytes 1990664 | tf_op jit(solution)/shard_map/ppermute | solution.py:25
  307.9 57.5 %collective-permute-start.40 = (bf16[2,4,64,1440]{3,2,1,0:T(8,128)(2,1)}, bf16[2,4,64,1440]{3,2,1,0:T(8,128)(2,1)}, u32[]{:S(2)}, u32[]{:S(2)}) collective-permute-start(bf16[2,4,64,1440]{3,2,1,0:T(8,128)(2,1)} %get-tuple-element.305), channel_id=1, source_target_pairs={{0,2},{1,3},{2,0},{3,1},{4,6},{5,7},{6,4},{7,5},{8,10},{9,11},{10,... | collective-permute-start | bytes 4423688 | tf_op jit(solution)/shard_map/ppermute | solution.py:25
  345.0 30.1 %collective-permute-start.46 = (bf16[2,4,80,864]{3,2,1,0:T(8,128)(2,1)}, bf16[2,4,80,864]{3,2,1,0:T(8,128)(2,1)}, u32[]{:S(2)}, u32[]{:S(2)}) collective-permute-start(bf16[2,4,80,864]{3,2,1,0:T(8,128)(2,1)} %get-tuple-element.323), channel_id=1, source_target_pairs={{0,1},{1,0},{2,3},{3,2},{4,5},{5,4},{6,7},{7,6},{8,9},{9,8},{10,11... | collective-permute-start | bytes 3317768 | tf_op jit(solution)/shard_map/ppermute | solution.py:25
  345.4 27.3 %collective-permute-start.45 = (bf16[2,4,64,864]{3,2,1,0:T(8,128)(2,1)}, bf16[2,4,64,864]{3,2,1,0:T(8,128)(2,1)S(1)}, u32[]{:S(2)}, u32[]{:S(2)}) collective-permute-start(bf16[2,4,64,864]{3,2,1,0:T(8,128)(2,1)} %get-tuple-element.322), channel_id=1, source_target_pairs={{0,2},{1,3},{2,0},{3,1},{4,6},{5,7},{6,4},{7,5},{8,10},{9,11},{10,... | collective-permute-start | bytes 2654216 | tf_op jit(solution)/shard_map/ppermute | solution.py:25
  371.3 27.8 %collective-permute-start.43 = (bf16[4,80,1440]{2,1,0:T(8,128)(2,1)}, bf16[4,80,1440]{2,1,0:T(8,128)(2,1)}, u32[]{:S(2)}, u32[]{:S(2)}) collective-permute-start(bf16[4,80,1440]{2,1,0:T(8,128)(2,1)} %get-tuple-element.390), channel_id=1, source_target_pairs={{0,2},{1,3},{2,0},{3,1},{4,6},{5,7},{6,4},{7,5},{8,10},{9,11},{10,... | collective-permute-start | bytes 2764808 | tf_op jit(solution)/shard_map/ppermute | solution.py:25
  378.3 20.8 %collective-permute-start.42 = (bf16[4,64,1440]{2,1,0:T(8,128)(2,1)}, bf16[4,64,1440]{2,1,0:T(8,128)(2,1)}, u32[]{:S(2)}, u32[]{:S(2)}) collective-permute-start(bf16[4,64,1440]{2,1,0:T(8,128)(2,1)} %get-tuple-element.392), channel_id=1, source_target_pairs={{0,1},{1,0},{2,3},{3,2},{4,5},{5,4},{6,7},{7,6},{8,9},{9,8},{10,11... | collective-permute-start | bytes 2211848 | tf_op jit(solution)/shard_map/ppermute | solution.py:25
  385.1 22.0 %collective-permute-start.53 = (bf16[4,80,864]{2,1,0:T(8,128)(2,1)}, bf16[4,80,864]{2,1,0:T(8,128)(2,1)}, u32[]{:S(2)}, u32[]{:S(2)}) collective-permute-start(bf16[4,80,864]{2,1,0:T(8,128)(2,1)} %get-tuple-element.398), channel_id=1, source_target_pairs={{0,2},{1,3},{2,0},{3,1},{4,6},{5,7},{6,4},{7,5},{8,10},{9,11},{10,... | collective-permute-start | bytes 1658888 | tf_op jit(solution)/shard_map/ppermute | solution.py:25
  402.9 27.6 %collective-permute-start.56 = (bf16[2,144,1440]{2,1,0:T(8,128)(2,1)}, bf16[2,144,1440]{2,1,0:T(8,128)(2,1)}, u32[]{:S(2)}, u32[]{:S(2)}) collective-permute-start(bf16[2,144,1440]{2,1,0:T(8,128)(2,1)} %pad_maximum_fusion), channel_id=1, source_target_pairs={{0,8},{4,12},{8,0},{12,4},{16,24},{20,28},{24,16},{28,20},{1,9},{5... | collective-permute-start | bytes 2488328 | tf_op jit(solution)/shard_map/ppermute | solution.py:25
  411.6 27.2 %collective-permute-start.58 = (bf16[2,144,864]{2,1,0:T(8,128)(2,1)S(1)}, bf16[2,144,864]{2,1,0:T(8,128)(2,1)S(1)}, u32[]{:S(2)}, u32[]{:S(2)}) collective-permute-start(bf16[2,144,864]{2,1,0:T(8,128)(2,1)S(1)} %pad_maximum_fusion.4), channel_id=1, source_target_pairs={{0,8},{4,12},{8,0},{12,4},{16,24},{20,28},{24,16},{28,20},{1,9},{5... | collective-permute-start | bytes 1493000 | tf_op jit(solution)/shard_map/ppermute | solution.py:25
  432.5 32.2 %collective-permute-start.61 = (bf16[144,1440]{1,0:T(8,128)(2,1)}, bf16[144,1440]{1,0:T(8,128)(2,1)}, u32[]{:S(2)}, u32[]{:S(2)}) collective-permute-start(bf16[144,1440]{1,0:T(8,128)(2,1)} %fusion.10), channel_id=1, source_target_pairs={{0,16},{4,20},{8,24},{12,28},{16,0},{20,4},{24,8},{28,12},{1,17},{... | collective-permute-start | bytes 1244168 | tf_op jit(solution)/shard_map/ppermute | solution.py:25
  439.1 20.2 %collective-permute-start.59 = (f32[4,12,144]{2,1,0:T(8,128)S(1)}, f32[4,12,144]{2,1,0:T(8,128)S(1)}, u32[]{:S(2)}, u32[]{:S(2)}) collective-permute-start(f32[4,12,144]{2,1,0:T(8,128)S(1)} %constant_dynamic-update-slice_fusion.7), channel_id=1, source_target_pairs={{0,16},{4,20},{8,24},{12,28},{16,0},{20,4},{24,8},{28,12},{1,17},{... | collective-permute-start | bytes 82952 | tf_op jit(solution)/shard_map/ppermute | solution.py:25
  439.2 22.9 %collective-permute-start.60 = (bf16[144,864]{1,0:T(8,128)(2,1)S(1)}, bf16[144,864]{1,0:T(8,128)(2,1)}, u32[]{:S(2)}, u32[]{:S(2)}) collective-permute-start(bf16[144,864]{1,0:T(8,128)(2,1)S(1)} %fusion.26), channel_id=1, source_target_pairs={{0,16},{4,20},{8,24},{12,28},{16,0},{20,4},{24,8},{28,12},{1,17},{... | collective-permute-start | bytes 746504 | tf_op jit(solution)/shard_map/ppermute | solution.py:25
  (98 other events, 1129.1 us)
Sparse Core Ops, SparseCore 0:
  105.9 93.9 all-gather.2

commit v4 on v3

--- a/solution.py
+++ b/solution.py
@@ -1194,50 +1194,47 @@
         [],
         3 * part,
     )
-    gelu, *attn_parts = land([down_scatter], gelu, *attn_parts)
+    gelu, *attn_parts = land([up_scatter, down_scatter], gelu, *attn_parts)
     attn_scatter = Scatter(*attn_parts)
     output, sums_g = down_call(
         down_w, gelu, tokens, branch_a, modes, out_bias[1], out_cotangent
     )
-    sums_g, *up_scatter.kept = land([up_scatter.wait()], sums_g, *up_scatter.kept)
+    (sums_g,) = land([up_scatter], sums_g)
 
     lower, upper = pack_call(
         span_clip, narrow_me, clips, sums_a, sums_b, sums_g, merge_bias_grad, down_bias_grad,
         qkv_sums, up_bias_grad,
     )
     sent = hop(upper, "narrow", narrow_bits[-1])
-    up_scatter.go()
-    lower, *attn_scatter.kept = land([sent, attn_scatter.wait()], lower, *attn_scatter.kept)
+    (lower,) = land([sent, attn_scatter, up_scatter], lower)
     packed = lower + sent.got[0]
     for bit in reversed(narrow_bits[:-1]):
         sent = hop(packed[bit:], "narrow", bit)
-        packed, *attn_scatter.kept = land([sent], packed, *attn_scatter.kept)
+        (packed,) = land([sent], packed)
         packed = packed[:bit] + sent.got[0]
     packed = packed[0]
-    attn_scatter.go()
     sent = hop(packed, "wide", 1)
     (packed,) = land([sent], packed)
     packed = packed + sent.got[0]
     for bit in z_bits:
         sent = hop(packed, "wide", bit)
-        (packed,) = land([sent], packed)
+        scatters = {z_bits[0]: [attn_scatter], z_bits[-1]: [up_scatter]}
+        (packed,) = land([sent, *scatters.get(bit, [])], packed)
         packed = packed + sent.got[0]
     clip_slice = packed[:at].reshape(6, clips, part)
     active_grad = jnp.einsum(
         "kci,dki->cd", clip_slice, mod_weight.astype(F32), precision=lax.Precision.HIGHEST
     )
-    (active_grad,) = land([up_scatter], active_grad)
     for bit in narrow_bits:
         sent = hop(active_grad, "narrow", bit)
         (active_grad,) = land(
-            [sent, attn_scatter] if bit == narrow_bits[0] else [sent], active_grad
+            [sent, attn_scatter] if bit == narrow_bits[-1] else [sent], active_grad
         )
         active_grad = active_grad + sent.got[0]
     active_grad = active_grad[None]
     for bit in bits_of(wide_count):
         sent = hop(active_grad, "wide", bit)
-        scatters = {1: [up_scatter], z_bits[0]: [attn_scatter]}
-        (active_grad,) = land([sent, *scatters.get(bit, [])], active_grad)
+        (active_grad,) = land([sent], active_grad)
         active_grad = jnp.concatenate([active_grad, sent.got[0]], axis=0)
     active_grad = turned(active_grad, "wide").transpose(1, 0, 2).reshape(clips, width)
     unused, silu_pullback = jax.vjp(jax.nn.silu, condition)

time: 479 us -> 475 us (level)
  other arithmetic: 31.5 us -> 23.3 us
    convert_element_type x15, other arithmetic: 24.2 us -> 16.1 us  [plus(): return (a.astype(F32) + b.astype(F32)).astype(BF16)]
    unnamed x141 -> x129, local copies, waits for them, and re-layouts: 11.8 us -> 11 us
  transfers between devices with their start and end apart: 63 -> 63, of which waited for: 35 -> 35; matrix products, arithmetic and copies ran while one was open for 8% -> 6% of each run, Pallas kernels for 42% -> 43%
where the time goes in v4:
time: 475 us; the launch traced here: 471 us
  Pallas kernels  201 us (42%)
  waiting for transfers between devices  153 us (32%)
  starting transfers between devices  57.7 us (12%)
  other arithmetic  23.3 us (5%)
  local copies, waits for them, and re-layouts  17.7 us (4%)
  between operations  15.5 us (3%)
    ppermute x62, waiting for transfers between devices, swap(): return lax.ppermute(block, axis, [(i, i ^ bit) for i in range(count)])  153 us
    pallas_call x6, Pallas kernels, weight_call(): pl.pallas_call(kernel, grid_spec=pltpu.PrefetchScalarGridSpec(num_scalar_...  118 us
    ppermute x62, starting transfers between devices, swap(): return lax.ppermute(block, axis, [(i, i ^ bit) for i in range(count)])  57.6 us
    pallas_call x3, Pallas kernels, weight_grad_call(): pl.pallas_call(kernel, grid=(groups,), in_specs=[whole(a) for a in lefts]...  38.9 us
    pallas_call x1, Pallas kernels, attend_back(): pl.pallas_call(functools.partial(attend_back_kernel, heads), grid=(rows /...  19.3 us
    convert_element_type x15, other arithmetic, plus(): return (a.astype(F32) + b.astype(F32)).astype(BF16)  16.1 us
    pallas_call x1, Pallas kernels, attend(): pl.pallas_call(functools.partial(attend_kernel, heads), grid=(rows // PAT...  11.7 us
    unnamed x129, local copies, waits for them, and re-layouts  11 us
  transfers between devices with their start and end apart: 63, of which 35 were waited for; matrix products, arithmetic and copies ran while one was open for 6% of the time, Pallas kernels for 43%

profile of v4, /device:TPU:0, one launch (start us, length us, event | category | flops | bytes accessed | tf_op | source)
XLA Modules:
  0.0 471.0 jit_solution(787954947185489372)
XLA Ops:
  8.9 4.1 collective-permute-start.2
  16.6 6.7 %collective-permute-done.1 = f32[6,12,288]{2,1,0:T(8,128)S(1)} collective-permute-done((f32[6,12,288]{2,1,0:T(8,128)S(1)}, f32[6,12,288]{2,1,0:T(8,128)S(1)}, u32[]{:S(2)}, u32[]{:S(2)}) %collective-permute-start.1) | collective-permute-done | bytes 82976 | tf_op jit(solution)/shard_map/ppermute | solution.py:25
  23.3 4.6 collective-permute-done.2
  28.1 9.1 %collective-permute-done.3 = f32[6,12,288]{2,1,0:T(8,128)S(1)} collective-permute-done((f32[6,12,288]{2,1,0:T(8,128)S(1)}, f32[6,12,288]{2,1,0:T(8,128)S(1)}, u32[]{:S(2)}, u32[]{:S(2)}) %collective-permute-start.3) | collective-permute-done | bytes 82976 | tf_op jit(solution)/shard_map/ppermute | solution.py:25
  46.4 5.1 %collective-permute-done.7 = bf16[2,144,1152]{2,1,0:T(8,128)(2,1)} collective-permute-done((bf16[2,144,1152]{2,1,0:T(8,128)(2,1)S(1)}, bf16[2,144,1152]{2,1,0:T(8,128)(2,1)}, u32[]{:S(2)}, u32[]{:S(2)}) %collective-permute-start.7) | collective-permute-done | bytes 663584 | tf_op jit(solution)/shard_map/ppermute | solution.py:25
  59.6 13.8 %collective-permute-done.10 = bf16[1,144,1152]{2,1,0:T(8,128)(2,1)S(1)} collective-permute-done((bf16[1,144,1152]{2,1,0:T(8,128)(2,1)S(1)}, bf16[1,144,1152]{2,1,0:T(8,128)(2,1)S(1)}, u32[]{:S(2)}, u32[]{:S(2)}) %collective-permute-start.10) | collective-permute-done | bytes 331808 | tf_op jit(solution)/shard_map/ppermute | solution.py:25
  73.4 10.9 %collective-permute-done.8.refs_4_.refs_5_ = bf16[4,144,1152]{2,1,0:T(8,128)(2,1)S(1)} collective-permute-done((bf16[4,144,1152]{2,1,0:T(8,128)(2,1)S(1)}, bf16[4,144,1152]{2,1,0:T(8,128)(2,1)S(1)}, u32[]{:S(2)}, u32[]{:S(2)}) %collective-permute-start.8) | collective-permute-done | bytes 1327136 | tf_op jit(solution)/shard_map/ppermute | solution.py:25
  89.1 13.8 %collective-permute-done.12.refs_6_.refs_7_ = bf16[4,64,1152]{2,1,0:T(8,128)(2,1)} collective-permute-done((bf16[4,64,1152]{2,1,0:T(8,128)(2,1)S(1)}, bf16[4,64,1152]{2,1,0:T(8,128)(2,1)}, u32[]{:S(2)}, u32[]{:S(2)}) %collective-permute-start.12) | collective-permute-done | bytes 589856 | tf_op jit(solution)/shard_map/ppermute | solution.py:25
  112.7 17.3 %project.1 = (bf16[768,1152]{1,0:T(8,128)(2,1)}, bf16[4,768,864]{2,1,0:T(8,128)(2,1)}, bf16[1152,1152]{1,0:T(8,128)(2,1)}) custom-call(s32[2]{0:T(128)} %pad_add_fusion.me_ref, bf16[768,1152]{1,0:T(8,128)(2,1)} %refs_1_.5, f32[3,6,1152]{2,1,0:T(8,128)} %copy-done.2, f32[4,1,864]{2,1,0:T(1,128)} %copy-done.16, bf16[4,144,1152]{2,1,0:T(8,128)(2,1)} %copy-done.24, ...), custom_call_target="tpu_custom_call" | custom-call | flops 1000000000 | bytes 1 | tf_op jit(solution)/shard_map/project/pallas_call | solution.py:362
  130.0 14.7 %collective-permute-done.16.refs_4_.refs_6_ = bf16[4,144,1152]{2,1,0:T(8,128)(2,1)S(1)} collective-permute-done((bf16[4,144,1152]{2,1,0:T(8,128)(2,1)S(1)}, bf16[4,144,1152]{2,1,0:T(8,128)(2,1)S(1)}, u32[]{:S(2)}, u32[]{:S(2)}) %collective-permute-start.16) | collective-permute-done | bytes 1327136 | tf_op jit(solution)/shard_map/ppermute | solution.py:25
  147.3 2.5 collective-permute-start.23
  149.8 11.7 %attend.1.attended_ref.refs_5_ = bf16[768,1152]{1,0:T(8,128)(2,1)} custom-call(bf16[4,768,864]{2,1,0:T(8,128)(2,1)} %get-tuple-element.215.qkv_ref), custom_call_target="tpu_custom_call" | custom-call | flops 1000000000 | bytes 1 | tf_op jit(solution)/shard_map/attend/pallas_call | solution.py:106
  165.9 7.6 %merge.1 = (f32[768,1152]{1,0:T(8,128)}, bf16[768,1152]{1,0:T(8,128)(2,1)}) custom-call(bf16[768,1152]{1,0:T(8,128)(2,1)} %attend.1.attended_ref.refs_5_, bf16[1152,1152]{1,0:T(8,128)(2,1)} %get-tuple-element.220.weight_ref.refs_0_, bf16[768,1152]{1,0:T(8,128)(2,1)} %refs_1_.5, f32[3,6,1152]{2,1,0:T(8,128)} %copy-done.2, f32[1,1152]{1,0:T(1,128)} %get-tuple-element.402.bias_ref), custom_call_target="tpu_custom_call" | custom-call | flops 1000000000 | bytes 1 | tf_op jit(solution)/shard_map/merge/pallas_call | solution.py:444
  175.6 22.6 %up.1 = (bf16[4,768,1152]{2,1,0:T(8,128)(2,1)}, bf16[4,768,1152]{2,1,0:T(8,128)(2,1)}, bf16[4,4,144,1152]{3,2,1,0:T(8,128)(2,1)}) custom-call(s32[2]{0:T(128)} %pad_add_fusion.me_ref, bf16[768,1152]{1,0:T(8,128)(2,1)} %get-tuple-element.240.refs_0_.block_ref, f32[4,1,1152]{2,1,0:T(1,128)} %copy-done.15, bf16[4,144,768]{2,1,0:T(8,128)(2,1)} %copy-done.8, ...), custom_call_target="tpu_custom_call" | custom-call | flops 1000000000 | bytes 1 | tf_op jit(solution)/shard_map/up/pallas_call | solution.py:362
  202.0 21.3 %gelu_back.1 = (bf16[4,768,1152]{2,1,0:T(8,128)(2,1)}, f32[4,1,1152]{2,1,0:T(1,128)}, bf16[4,4,144,1152]{3,2,1,0:T(8,128)(2,1)}) custom-call(s32[2]{0:T(128)} %pad_add_fusion.me_ref, bf16[768,1152]{1,0:T(8,128)(2,1)} %copy-done.3, bf16[4,768,1152]{2,1,0:T(8,128)(2,1)} %get-tuple-element.239.refs_1_, bf16[4,144,768]{2,1,0:T(8,128)(2,1)} %copy-done.11, ...), custom_call_target="tpu_custom_call" | custom-call | flops 1000000000 | bytes 1 | tf_op jit(solution)/shard_map/gelu_back/pallas_call | solution.py:362
  223.4 10.7 %weight_grad.3 = (bf16[2,4,64,1152]{3,2,1,0:T(8,128)(2,1)}, bf16[2,4,64,1152]{3,2,1,0:T(8,128)(2,1)}, bf16[2,4,80,1152]{3,2,1,0:T(8,128)(2,1)}, bf16[2,4,80,1152]{3,2,1,0:T(8,128)(2,1)}) custom-call(bf16[4,144,768]{2,1,0:T(8,128)(2,1)} %copy-done.7, bf16[4,768,1152]{2,1,0:T(8,128)(2,1)} %get-tuple-element.298.refs_1_.refs_0_, ...), custom_call_target="tpu_custom_call" | custom-call | flops 1000000000 | bytes 1 | tf_op jit(solution)/shard_map/weight_grad/pallas_call | solution.py:760
  234.5 2.6 collective-permute-start.32
  239.3 20.9 %up_back.1 = (f32[768,1152]{1,0:T(8,128)}, bf16[768,1152]{1,0:T(8,128)(2,1)}, f32[3,3,1152]{2,1,0:T(4,128)}, f32[1,1152]{1,0:T(1,128)}) custom-call(s32[2]{0:T(128)} %pad_add_fusion.me_ref, bf16[4,768,1152]{2,1,0:T(8,128)(2,1)} %get-tuple-element.273.refs_0_.refs_1_, bf16[768,1152]{1,0:T(8,128)(2,1)} %refs_1_.5, f32[768,1152]{1,0:T(8,128)} %get-tuple-element.263.refs_2_, ...), custom_call_target="tpu_custom_call" | custom-call | flops 1000000000 | bytes 1 | tf_op jit(solution)/shard_map/up_back/pallas_call | solution.py:362
  263.2 19.3 %attend_back.1.refs_0_.refs_2_ = bf16[4,768,896]{2,1,0:T(8,128)(2,1)} custom-call(bf16[4,768,864]{2,1,0:T(8,128)(2,1)} %get-tuple-element.215.qkv_ref, bf16[768,1152]{1,0:T(8,128)(2,1)} %get-tuple-element.265.block_ref.grad_ref, bf16[1152,1152]{1,0:T(8,128)(2,1)} %get-tuple-element.220.weight_ref.refs_0_), custom_call_target="tpu_custom_call" | custom-call | flops 1000000000 | bytes 1 | tf_op jit(solution)/shard_map/attend_back/pallas_call | solution.py:153
  283.0 2.7 add_convert_fusion.4
  287.9 15.5 %weight_grad.4 = (bf16[2,4,64,1440]{3,2,1,0:T(8,128)(2,1)}, bf16[2,4,64,1440]{3,2,1,0:T(8,128)(2,1)}, bf16[2,4,80,1440]{3,2,1,0:T(8,128)(2,1)}, bf16[2,4,80,1440]{3,2,1,0:T(8,128)(2,1)}) custom-call(bf16[4,144,768]{2,1,0:T(8,128)(2,1)} %copy-done.9, bf16[4,768,1152]{2,1,0:T(8,128)(2,1)} %get-tuple-element.273.refs_0_.refs_1_, ...), custom_call_target="tpu_custom_call" | custom-call | flops 1000000000 | bytes 1 | tf_op jit(solution)/shard_map/weight_grad/pallas_call | solution.py:760
  308.8 18.2 %project_back.1 = (f32[768,1152]{1,0:T(8,128)}, f32[3,2,1152]{2,1,0:T(2,128)}, f32[4,1,864]{2,1,0:T(1,128)}) custom-call(s32[2]{0:T(128)} %pad_add_fusion.me_ref, bf16[4,768,896]{2,1,0:T(8,128)(2,1)} %attend_back.1.refs_0_.refs_2_, bf16[768,1152]{1,0:T(8,128)(2,1)} %refs_1_.5, f32[768,1152]{1,0:T(8,128)} %get-tuple-element.287.refs_2_, ...), custom_call_target="tpu_custom_call" | custom-call | flops 1000000000 | bytes 1 | tf_op jit(solution)/shard_map/project_back/pallas_call | solution.py:362
  328.9 12.6 %weight_grad.5 = (bf16[2,4,64,864]{3,2,1,0:T(8,128)(2,1)}, bf16[2,4,64,864]{3,2,1,0:T(8,128)(2,1)}, bf16[2,4,80,864]{3,2,1,0:T(8,128)(2,1)}, bf16[2,4,80,864]{3,2,1,0:T(8,128)(2,1)}) custom-call(bf16[4,144,768]{2,1,0:T(8,128)(2,1)} %copy-done.6, bf16[4,144,768]{2,1,0:T(8,128)(2,1)} %copy-done.47, bf16[4,768,896]{2,1,0:T(8,128)(2,1)} %attend_back.1.refs_0_.refs_2_, ...), custom_call_target="tpu_custom_call" | custom-call | flops 1000000000 | bytes 1 | tf_op jit(solution)/shard_map/weight_grad/pallas_call | solution.py:760
  341.5 2.5 collective-permute-done.41
  344.0 5.3 %collective-permute-done.39 = bf16[2,4,80,1440]{3,2,1,0:T(8,128)(2,1)} collective-permute-done((bf16[2,4,80,1440]{3,2,1,0:T(8,128)(2,1)}, bf16[2,4,80,1440]{3,2,1,0:T(8,128)(2,1)}, u32[]{:S(2)}, u32[]{:S(2)}) %collective-permute-start.39) | collective-permute-done | bytes 1843232 | tf_op jit(solution)/shard_map/ppermute | solution.py:25
  357.7 18.2 %down.1 = (bf16[768,1152]{1,0:T(8,128)(2,1)}, f32[3,1,1152]{2,1,0:T(1,128)}) custom-call(s32[2]{0:T(128)} %pad_add_fusion.me_ref, bf16[4,768,1152]{2,1,0:T(8,128)(2,1)} %get-tuple-element.298.refs_1_.refs_0_, bf16[768,1152]{1,0:T(8,128)(2,1)} %refs_1_.5, f32[768,1152]{1,0:T(8,128)} %get-tuple-element.263.refs_2_, f32[3,6,1152]{2,1,0:T(8,128)} %copy-done.2, ...), custom_call_target="tpu_custom_call" | custom-call | flops 1000000000 | bytes 1 | tf_op jit(solution)/shard_map/down/pallas_call | solution.py:362
  381.8 14.3 %collective-permute-done.45 = bf16[2,4,64,864]{3,2,1,0:T(8,128)(2,1)} collective-permute-done((bf16[2,4,64,864]{3,2,1,0:T(8,128)(2,1)}, bf16[2,4,64,864]{3,2,1,0:T(8,128)(2,1)}, u32[]{:S(2)}, u32[]{:S(2)}) %collective-permute-start.45) | collective-permute-done | bytes 884768 | tf_op jit(solution)/shard_map/ppermute | solution.py:25
  396.1 2.9 collective-permute-done.44
  412.1 10.1 %collective-permute-done.50 = f32[80,288]{1,0:T(8,128)S(1)} collective-permute-done((f32[80,288]{1,0:T(8,128)S(1)}, f32[80,288]{1,0:T(8,128)S(1)}, u32[]{:S(2)}, u32[]{:S(2)}) %collective-permute-start.50) | collective-permute-done | bytes 92192 | tf_op jit(solution)/shard_map/ppermute | solution.py:25
  425.3 5.4 %collective-permute-done.53 = f32[80,288]{1,0:T(8,128)S(1)} collective-permute-done((f32[80,288]{1,0:T(8,128)S(1)}, f32[80,288]{1,0:T(8,128)S(1)}, u32[]{:S(2)}, u32[]{:S(2)}) %collective-permute-start.53) | collective-permute-done | bytes 92192 | tf_op jit(solution)/shard_map/ppermute | solution.py:25
  448.0 9.5 %collective-permute-done.60 = f32[4,12,144]{2,1,0:T(8,128)S(1)} collective-permute-done((f32[4,12,144]{2,1,0:T(8,128)S(1)}, f32[4,12,144]{2,1,0:T(8,128)S(1)}, u32[]{:S(2)}, u32[]{:S(2)}) %collective-permute-start.60) | collective-permute-done | bytes 27680 | tf_op jit(solution)/shard_map/ppermute | solution.py:25
  458.5 3.9 collective-permute-done.61
  (318 shorter events, 115.1 us)
Async XLA Ops:
  7.2 194.8 %all-gather.3.cloned.1.call-start = ((), (), s32[]{:S(2)}) async-start(), calls=%async_computation | async-start | bytes 10948608 | tf_op jit(solution)/shard_map/all_gather | solution.py:293
  8.9 19.0 %collective-permute-start.2 = (bf16[1,144,1152]{2,1,0:T(8,128)(2,1)S(1)}, bf16[1,144,1152]{2,1,0:T(8,128)(2,1)S(1)}, u32[]{:S(2)}, u32[]{:S(2)}) collective-permute-start(bf16[1,144,1152]{2,1,0:T(8,128)(2,1)S(1)} %maximum_bitcast_fusion), channel_id=1, source_target_pairs={{0,16},{4,20},{8,24},{12,28},{16,0},{20,4},{24,8},{28,12},{1,17},{... | collective-permute-start | bytes 995336 | tf_op jit(solution)/shard_map/ppermute | solution.py:25
  52.7 20.8 %collective-permute-start.11 = (bf16[4,144,1152]{2,1,0:T(8,128)(2,1)S(1)}, bf16[4,144,1152]{2,1,0:T(8,128)(2,1)S(1)}, u32[]{:S(2)}, u32[]{:S(2)}) collective-permute-start(bf16[4,144,1152]{2,1,0:T(8,128)(2,1)S(1)} %constant_dynamic-update-slice_fusion.refs_3_.refs_4_), channel_id=1, source_target_pairs={{0,4},{4,0},{8,12},{12,8},{16,20},{20,16},{24,28},{28,24},{1,5},{5... | collective-permute-start | bytes 3981320 | tf_op jit(solution)/shard_map/ppermute | solution.py:25
  52.7 31.5 %collective-permute-start.8 = (bf16[4,144,1152]{2,1,0:T(8,128)(2,1)S(1)}, bf16[4,144,1152]{2,1,0:T(8,128)(2,1)S(1)}, u32[]{:S(2)}, u32[]{:S(2)}) collective-permute-start(bf16[4,144,1152]{2,1,0:T(8,128)(2,1)S(1)} %constant_dynamic-update-slice_fusion.refs_3_.refs_4_), channel_id=1, source_target_pairs={{0,2},{1,3},{2,0},{3,1},{4,6},{5,7},{6,4},{7,5},{8,10},{9,11},{10,... | collective-permute-start | bytes 3981320 | tf_op jit(solution)/shard_map/ppermute | solution.py:25
  54.3 31.2 %collective-permute-start.9 = (bf16[4,144,1152]{2,1,0:T(8,128)(2,1)S(1)}, bf16[4,144,1152]{2,1,0:T(8,128)(2,1)S(1)}, u32[]{:S(2)}, u32[]{:S(2)}) collective-permute-start(bf16[4,144,1152]{2,1,0:T(8,128)(2,1)S(1)} %constant_dynamic-update-slice_fusion.refs_3_.refs_4_), channel_id=1, source_target_pairs={{0,1},{1,0},{2,3},{3,2},{4,5},{5,4},{6,7},{7,6},{8,9},{9,8},{10,11... | collective-permute-start | bytes 3981320 | tf_op jit(solution)/shard_map/ppermute | solution.py:25
  85.5 19.1 %collective-permute-start.15 = (bf16[4,144,1152]{2,1,0:T(8,128)(2,1)S(1)}, bf16[4,144,1152]{2,1,0:T(8,128)(2,1)S(1)}, u32[]{:S(2)}, u32[]{:S(2)}) collective-permute-start(bf16[4,144,1152]{2,1,0:T(8,128)(2,1)S(1)} %collective-permute-done.8.refs_4_.refs_5_), channel_id=1, source_target_pairs={{0,4},{4,0},{8,12},{12,8},{16,20},{20,16},{24,28},{28,24},{1,5},{5... | collective-permute-start | bytes 3981320 | tf_op jit(solution)/shard_map/ppermute | solution.py:25
  85.6 19.1 %collective-permute-start.13 = (bf16[4,80,1152]{2,1,0:T(8,128)(2,1)S(1)}, bf16[4,80,1152]{2,1,0:T(8,128)(2,1)}, u32[]{:S(2)}, u32[]{:S(2)}) collective-permute-start(bf16[4,80,1152]{2,1,0:T(8,128)(2,1)S(1)} %slice.118), channel_id=1, source_target_pairs={{0,2},{1,3},{2,0},{3,1},{4,6},{5,7},{6,4},{7,5},{8,10},{9,11},{10,... | collective-permute-start | bytes 2211848 | tf_op jit(solution)/shard_map/ppermute | solution.py:25
  106.6 38.1 %collective-permute-start.16 = (bf16[4,144,1152]{2,1,0:T(8,128)(2,1)S(1)}, bf16[4,144,1152]{2,1,0:T(8,128)(2,1)S(1)}, u32[]{:S(2)}, u32[]{:S(2)}) collective-permute-start(bf16[4,144,1152]{2,1,0:T(8,128)(2,1)S(1)} %constant_dynamic-update-slice_fusion.2.refs_3_.refs_5_), channel_id=1, source_target_pairs={{0,2},{1,3},{2,0},{3,1},{4,6},{5,7},{6,4},{7,5},{8,10},{9,11},{10,... | collective-permute-start | bytes 3981320 | tf_op jit(solution)/shard_map/ppermute | solution.py:25
  107.2 38.5 %collective-permute-start.17 = (bf16[4,144,1152]{2,1,0:T(8,128)(2,1)S(1)}, bf16[4,144,1152]{2,1,0:T(8,128)(2,1)S(1)}, u32[]{:S(2)}, u32[]{:S(2)}) collective-permute-start(bf16[4,144,1152]{2,1,0:T(8,128)(2,1)S(1)} %constant_dynamic-update-slice_fusion.2.refs_3_.refs_5_), channel_id=1, source_target_pairs={{0,1},{1,0},{2,3},{3,2},{4,5},{5,4},{6,7},{7,6},{8,9},{9,8},{10,11... | collective-permute-start | bytes 3981320 | tf_op jit(solution)/shard_map/ppermute | solution.py:25
  111.8 33.8 %collective-permute-start.21 = (bf16[4,144,1152]{2,1,0:T(8,128)(2,1)S(1)}, bf16[4,144,1152]{2,1,0:T(8,128)(2,1)S(1)}, u32[]{:S(2)}, u32[]{:S(2)}) collective-permute-start(bf16[4,144,1152]{2,1,0:T(8,128)(2,1)S(1)} %constant_dynamic-update-slice_fusion.2.refs_3_.refs_5_), channel_id=1, source_target_pairs={{0,4},{4,0},{8,12},{12,8},{16,20},{20,16},{24,28},{28,24},{1,5},{5... | collective-permute-start | bytes 3981320 | tf_op jit(solution)/shard_map/ppermute | solution.py:25
  145.6 19.0 %collective-permute-start.25 = (bf16[4,144,1152]{2,1,0:T(8,128)(2,1)S(1)}, bf16[4,144,1152]{2,1,0:T(8,128)(2,1)S(1)}, u32[]{:S(2)}, u32[]{:S(2)}) collective-permute-start(bf16[4,144,1152]{2,1,0:T(8,128)(2,1)S(1)} %collective-permute-done.16.refs_4_.refs_6_), channel_id=1, source_target_pairs={{0,4},{4,0},{8,12},{12,8},{16,20},{20,16},{24,28},{28,24},{1,5},{5... | collective-permute-start | bytes 3981320 | tf_op jit(solution)/shard_map/ppermute | solution.py:25
  145.7 19.0 %collective-permute-start.24 = (bf16[4,80,1152]{2,1,0:T(8,128)(2,1)S(1)}, bf16[4,80,1152]{2,1,0:T(8,128)(2,1)S(1)}, u32[]{:S(2)}, u32[]{:S(2)}) collective-permute-start(bf16[4,80,1152]{2,1,0:T(8,128)(2,1)S(1)} %slice.120), channel_id=1, source_target_pairs={{0,2},{1,3},{2,0},{3,1},{4,6},{5,7},{6,4},{7,5},{8,10},{9,11},{10,... | collective-permute-start | bytes 2211848 | tf_op jit(solution)/shard_map/ppermute | solution.py:25
  149.8 23.8 %collective-permute-start.22 = (bf16[4,144,1152]{2,1,0:T(8,128)(2,1)S(1)}, bf16[4,144,1152]{2,1,0:T(8,128)(2,1)}, u32[]{:S(2)}, u32[]{:S(2)}) collective-permute-start(bf16[4,144,1152]{2,1,0:T(8,128)(2,1)S(1)} %collective-permute-done.17.refs_5_.refs_7_), channel_id=1, source_target_pairs={{0,4},{4,0},{8,12},{12,8},{16,20},{20,16},{24,28},{28,24},{1,5},{5... | collective-permute-start | bytes 3981320 | tf_op jit(solution)/shard_map/ppermute | solution.py:25
  175.6 22.6 %collective-permute-start.28 = (bf16[4,144,768]{2,1,0:T(8,128)(2,1)S(1)}, bf16[4,144,768]{2,1,0:T(8,128)(2,1)S(1)}, u32[]{:S(2)}, u32[]{:S(2)}) collective-permute-start(bf16[4,144,768]{2,1,0:T(8,128)(2,1)S(1)} %get-tuple-element.225), channel_id=1, source_target_pairs={{0,4},{4,0},{8,12},{12,8},{16,20},{20,16},{24,28},{28,24},{1,5},{5... | collective-permute-start | bytes 2654216 | tf_op jit(solution)/shard_map/ppermute | solution.py:25
  199.2 24.1 %collective-permute-start.29 = (bf16[4,4,144,1152]{3,2,1,0:T(8,128)(2,1)}, bf16[4,4,144,1152]{3,2,1,0:T(8,128)(2,1)}, u32[]{:S(2)}, u32[]{:S(2)}) collective-permute-start(bf16[4,4,144,1152]{3,2,1,0:T(8,128)(2,1)} %get-tuple-element.237), channel_id=1, source_target_pairs={{0,4},{4,0},{8,12},{12,8},{16,20},{20,16},{24,28},{28,24},{1,5},{5... | collective-permute-start | bytes 15925256 | tf_op jit(solution)/shard_map/ppermute | solution.py:25
  234.1 26.1 %collective-permute-start.33 = (bf16[768,1152]{1,0:T(8,128)(2,1)S(1)}, bf16[768,1152]{1,0:T(8,128)(2,1)}, u32[]{:S(2)}, u32[]{:S(2)}) collective-permute-start(bf16[768,1152]{1,0:T(8,128)(2,1)S(1)} %copy-done.21), channel_id=1, source_target_pairs={{0,4},{4,0},{8,12},{12,8},{16,20},{20,16},{24,28},{28,24},{1,5},{5... | collective-permute-start | bytes 5308424 | tf_op jit(solution)/shard_map/ppermute | solution.py:25
  234.5 47.9 %collective-permute-start.32 = (bf16[2,4,80,1152]{3,2,1,0:T(8,128)(2,1)}, bf16[2,4,80,1152]{3,2,1,0:T(8,128)(2,1)}, u32[]{:S(2)}, u32[]{:S(2)}) collective-permute-start(bf16[2,4,80,1152]{3,2,1,0:T(8,128)(2,1)} %get-tuple-element.260), channel_id=1, source_target_pairs={{0,1},{1,0},{2,3},{3,2},{4,5},{5,4},{6,7},{7,6},{8,9},{9,8},{10,11... | collective-permute-start | bytes 4423688 | tf_op jit(solution)/shard_map/ppermute | solution.py:25
  237.1 45.4 %collective-permute-start.31 = (bf16[2,4,64,1152]{3,2,1,0:T(8,128)(2,1)}, bf16[2,4,64,1152]{3,2,1,0:T(8,128)(2,1)}, u32[]{:S(2)}, u32[]{:S(2)}) collective-permute-start(bf16[2,4,64,1152]{3,2,1,0:T(8,128)(2,1)} %get-tuple-element.259), channel_id=1, source_target_pairs={{0,2},{1,3},{2,0},{3,1},{4,6},{5,7},{6,4},{7,5},{8,10},{9,11},{10,... | collective-permute-start | bytes 3538952 | tf_op jit(solution)/shard_map/ppermute | solution.py:25
  263.2 19.3 %collective-permute-start.34 = (bf16[4,144,768]{2,1,0:T(8,128)(2,1)S(1)}, bf16[4,144,768]{2,1,0:T(8,128)(2,1)S(1)}, u32[]{:S(2)}, u32[]{:S(2)}) collective-permute-start(bf16[4,144,768]{2,1,0:T(8,128)(2,1)S(1)} %get-tuple-element.266), channel_id=1, source_target_pairs={{0,4},{4,0},{8,12},{12,8},{16,20},{20,16},{24,28},{28,24},{1,5},{5... | collective-permute-start | bytes 2654216 | tf_op jit(solution)/shard_map/ppermute | solution.py:25
  282.5 22.2 %collective-permute-start.37 = (bf16[4,768,896]{2,1,0:T(8,128)(2,1)}, bf16[4,768,896]{2,1,0:T(8,128)(2,1)}, u32[]{:S(2)}, u32[]{:S(2)}) collective-permute-start(bf16[4,768,896]{2,1,0:T(8,128)(2,1)} %attend_back.1.refs_0_.refs_2_), channel_id=1, source_target_pairs={{0,4},{4,0},{8,12},{12,8},{16,20},{20,16},{24,28},{28,24},{1,5},{5... | collective-permute-start | bytes 16515080 | tf_op jit(solution)/shard_map/ppermute | solution.py:25
  285.7 19.0 %collective-permute-start.36 = (bf16[4,80,1152]{2,1,0:T(8,128)(2,1)}, bf16[4,80,1152]{2,1,0:T(8,128)(2,1)S(1)}, u32[]{:S(2)}, u32[]{:S(2)}) collective-permute-start(bf16[4,80,1152]{2,1,0:T(8,128)(2,1)} %get-tuple-element.382), channel_id=1, source_target_pairs={{0,2},{1,3},{2,0},{3,1},{4,6},{5,7},{6,4},{7,5},{8,10},{9,11},{10,... | collective-permute-start | bytes 2211848 | tf_op jit(solution)/shard_map/ppermute | solution.py:25
  304.7 44.6 %collective-permute-start.39 = (bf16[2,4,80,1440]{3,2,1,0:T(8,128)(2,1)}, bf16[2,4,80,1440]{3,2,1,0:T(8,128)(2,1)}, u32[]{:S(2)}, u32[]{:S(2)}) collective-permute-start(bf16[2,4,80,1440]{3,2,1,0:T(8,128)(2,1)} %get-tuple-element.283), channel_id=1, source_target_pairs={{0,1},{1,0},{2,3},{3,2},{4,5},{5,4},{6,7},{7,6},{8,9},{9,8},{10,11... | collective-permute-start | bytes 5529608 | tf_op jit(solution)/shard_map/ppermute | solution.py:25
  305.1 38.9 %collective-permute-start.38 = (bf16[2,4,64,1440]{3,2,1,0:T(8,128)(2,1)}, bf16[2,4,64,1440]{3,2,1,0:T(8,128)(2,1)}, u32[]{:S(2)}, u32[]{:S(2)}) collective-permute-start(bf16[2,4,64,1440]{3,2,1,0:T(8,128)(2,1)} %get-tuple-element.282), channel_id=1, source_target_pairs={{0,2},{1,3},{2,0},{3,1},{4,6},{5,7},{6,4},{7,5},{8,10},{9,11},{10,... | collective-permute-start | bytes 4423688 | tf_op jit(solution)/shard_map/ppermute | solution.py:25
  308.6 18.3 %collective-permute-start.40 = (bf16[2,144,1152]{2,1,0:T(8,128)(2,1)S(1)}, bf16[2,144,1152]{2,1,0:T(8,128)(2,1)S(1)}, u32[]{:S(2)}, u32[]{:S(2)}) collective-permute-start(bf16[2,144,1152]{2,1,0:T(8,128)(2,1)S(1)} %pad_maximum_fusion.3), channel_id=1, source_target_pairs={{0,8},{4,12},{8,0},{12,4},{16,24},{20,28},{24,16},{28,20},{1,9},{5... | collective-permute-start | bytes 1990664 | tf_op jit(solution)/shard_map/ppermute | solution.py:25
  351.6 24.9 %collective-permute-start.43 = (bf16[4,80,1440]{2,1,0:T(8,128)(2,1)S(1)}, bf16[4,80,1440]{2,1,0:T(8,128)(2,1)}, u32[]{:S(2)}, u32[]{:S(2)}) collective-permute-start(bf16[4,80,1440]{2,1,0:T(8,128)(2,1)S(1)} %get-tuple-element.378), channel_id=1, source_target_pairs={{0,2},{1,3},{2,0},{3,1},{4,6},{5,7},{6,4},{7,5},{8,10},{9,11},{10,... | collective-permute-start | bytes 2764808 | tf_op jit(solution)/shard_map/ppermute | solution.py:25
  354.6 21.3 %collective-permute-start.42 = (bf16[4,64,1440]{2,1,0:T(8,128)(2,1)S(1)}, bf16[4,64,1440]{2,1,0:T(8,128)(2,1)S(1)}, u32[]{:S(2)}, u32[]{:S(2)}) collective-permute-start(bf16[4,64,1440]{2,1,0:T(8,128)(2,1)S(1)} %get-tuple-element.380), channel_id=1, source_target_pairs={{0,1},{1,0},{2,3},{3,2},{4,5},{5,4},{6,7},{7,6},{8,9},{9,8},{10,11... | collective-permute-start | bytes 2211848 | tf_op jit(solution)/shard_map/ppermute | solution.py:25
  356.3 42.7 %collective-permute-start.46 = (bf16[2,4,80,864]{3,2,1,0:T(8,128)(2,1)}, bf16[2,4,80,864]{3,2,1,0:T(8,128)(2,1)}, u32[]{:S(2)}, u32[]{:S(2)}) collective-permute-start(bf16[2,4,80,864]{3,2,1,0:T(8,128)(2,1)} %get-tuple-element.315), channel_id=1, source_target_pairs={{0,1},{1,0},{2,3},{3,2},{4,5},{5,4},{6,7},{7,6},{8,9},{9,8},{10,11... | collective-permute-start | bytes 3317768 | tf_op jit(solution)/shard_map/ppermute | solution.py:25
  356.7 39.4 %collective-permute-start.45 = (bf16[2,4,64,864]{3,2,1,0:T(8,128)(2,1)}, bf16[2,4,64,864]{3,2,1,0:T(8,128)(2,1)}, u32[]{:S(2)}, u32[]{:S(2)}) collective-permute-start(bf16[2,4,64,864]{3,2,1,0:T(8,128)(2,1)} %get-tuple-element.314), channel_id=1, source_target_pairs={{0,2},{1,3},{2,0},{3,1},{4,6},{5,7},{6,4},{7,5},{8,10},{9,11},{10,... | collective-permute-start | bytes 2654216 | tf_op jit(solution)/shard_map/ppermute | solution.py:25
  379.2 19.8 %collective-permute-start.47 = (bf16[2,144,1440]{2,1,0:T(8,128)(2,1)}, bf16[2,144,1440]{2,1,0:T(8,128)(2,1)}, u32[]{:S(2)}, u32[]{:S(2)}) collective-permute-start(bf16[2,144,1440]{2,1,0:T(8,128)(2,1)} %pad_maximum_fusion), channel_id=1, source_target_pairs={{0,8},{4,12},{8,0},{12,4},{16,24},{20,28},{24,16},{28,20},{1,9},{5... | collective-permute-start | bytes 2488328 | tf_op jit(solution)/shard_map/ppermute | solution.py:25
  380.8 18.2 %collective-permute-start.44 = (f32[2,80,288]{2,1,0:T(8,128)S(1)}, f32[2,80,288]{2,1,0:T(8,128)}, u32[]{:S(2)}, u32[]{:S(2)}) collective-permute-start(f32[2,80,288]{2,1,0:T(8,128)S(1)} %get-tuple-element.313), channel_id=1, source_target_pairs={{0,2},{1,3},{2,0},{3,1},{4,6},{5,7},{6,4},{7,5},{8,10},{9,11},{10,... | collective-permute-start | bytes 552968 | tf_op jit(solution)/shard_map/ppermute | solution.py:25
  400.2 25.1 %collective-permute-start.54 = (bf16[144,1440]{1,0:T(8,128)(2,1)S(1)}, bf16[144,1440]{1,0:T(8,128)(2,1)S(1)}, u32[]{:S(2)}, u32[]{:S(2)}) collective-permute-start(bf16[144,1440]{1,0:T(8,128)(2,1)S(1)} %fusion.9), channel_id=1, source_target_pairs={{0,16},{4,20},{8,24},{12,28},{16,0},{20,4},{24,8},{28,12},{1,17},{... | collective-permute-start | bytes 1244168 | tf_op jit(solution)/shard_map/ppermute | solution.py:25
  404.4 17.8 %collective-permute-start.52 = (bf16[4,80,864]{2,1,0:T(8,128)(2,1)S(1)}, bf16[4,80,864]{2,1,0:T(8,128)(2,1)S(1)}, u32[]{:S(2)}, u32[]{:S(2)}) collective-permute-start(bf16[4,80,864]{2,1,0:T(8,128)(2,1)S(1)} %get-tuple-element.386), channel_id=1, source_target_pairs={{0,2},{1,3},{2,0},{3,1},{4,6},{5,7},{6,4},{7,5},{8,10},{9,11},{10,... | collective-permute-start | bytes 1658888 | tf_op jit(solution)/shard_map/ppermute | solution.py:25
  (92 other events, 960.2 us)
Sparse Core Ops, SparseCore 0:
  105.9 93.9 all-gather.2

commit v5 on v4

--- a/solution.py
+++ b/solution.py
@@ -65,7 +65,7 @@
 
 
 def cost():
-    return pl.CostEstimate(flops=1000000000, bytes_accessed=1, transcendentals=0)
+    return pl.CostEstimate(flops=100000000, bytes_accessed=1, transcendentals=0)
 
 
 def whole(array):
@@ -1234,7 +1234,7 @@
     active_grad = active_grad[None]
     for bit in bits_of(wide_count):
         sent = hop(active_grad, "wide", bit)
-        (active_grad,) = land([sent], active_grad)
+        (active_grad,) = land([sent, attn_scatter] if bit == z_bits[0] else [sent], active_grad)
         active_grad = jnp.concatenate([active_grad, sent.got[0]], axis=0)
     active_grad = turned(active_grad, "wide").transpose(1, 0, 2).reshape(clips, width)
     unused, silu_pullback = jax.vjp(jax.nn.silu, condition)

time: 475 us -> 474 us (level)
  transfers between devices with their start and end apart: 63 -> 63, of which waited for: 35 -> 36; matrix products, arithmetic and copies ran while one was open for 6% -> 6% of each run, Pallas kernels for 43% -> 43%
where the time goes in v5:
time: 474 us; the launch traced here: 470 us
  Pallas kernels  201 us (42%)
  waiting for transfers between devices  151 us (32%)
  starting transfers between devices  58.2 us (12%)
  other arithmetic  24.7 us (5%)
  local copies, waits for them, and re-layouts  17.2 us (4%)
  between operations  15.5 us (3%)
    ppermute x62, waiting for transfers between devices, swap(): return lax.ppermute(block, axis, [(i, i ^ bit) for i in range(count)])  151 us
    pallas_call x6, Pallas kernels, weight_call(): pl.pallas_call(kernel, grid_spec=pltpu.PrefetchScalarGridSpec(num_scalar_...  118 us
    ppermute x62, starting transfers between devices, swap(): return lax.ppermute(block, axis, [(i, i ^ bit) for i in range(count)])  58.2 us
    pallas_call x3, Pallas kernels, weight_grad_call(): pl.pallas_call(kernel, grid=(groups,), in_specs=[whole(a) for a in lefts]...  38.8 us
    pallas_call x1, Pallas kernels, attend_back(): pl.pallas_call(functools.partial(attend_back_kernel, heads), grid=(rows /...  19.3 us
    convert_element_type x15, other arithmetic, plus(): return (a.astype(F32) + b.astype(F32)).astype(BF16)  16.8 us
    pallas_call x1, Pallas kernels, attend(): pl.pallas_call(functools.partial(attend_kernel, heads), grid=(rows // PAT...  11.6 us
    unnamed x129, local copies, waits for them, and re-layouts  10.5 us
  transfers between devices with their start and end apart: 63, of which 36 were waited for; matrix products, arithmetic and copies ran while one was open for 6% of the time, Pallas kernels for 43%

profile of v5, /device:TPU:0, one launch (start us, length us, event | category | flops | bytes accessed | tf_op | source)
XLA Modules:
  0.0 470.0 jit_solution(17069857010027575599)
XLA Ops:
  8.9 4.1 collective-permute-start.2
  16.6 6.7 %collective-permute-done.1 = f32[6,12,288]{2,1,0:T(8,128)S(1)} collective-permute-done((f32[6,12,288]{2,1,0:T(8,128)S(1)}, f32[6,12,288]{2,1,0:T(8,128)S(1)}, u32[]{:S(2)}, u32[]{:S(2)}) %collective-permute-start.1) | collective-permute-done | bytes 82976 | tf_op jit(solution)/shard_map/ppermute | solution.py:25
  23.3 4.6 collective-permute-done.2
  28.1 9.1 %collective-permute-done.3 = f32[6,12,288]{2,1,0:T(8,128)S(1)} collective-permute-done((f32[6,12,288]{2,1,0:T(8,128)S(1)}, f32[6,12,288]{2,1,0:T(8,128)S(1)}, u32[]{:S(2)}, u32[]{:S(2)}) %collective-permute-start.3) | collective-permute-done | bytes 82976 | tf_op jit(solution)/shard_map/ppermute | solution.py:25
  46.4 5.1 %collective-permute-done.7 = bf16[2,144,1152]{2,1,0:T(8,128)(2,1)} collective-permute-done((bf16[2,144,1152]{2,1,0:T(8,128)(2,1)S(1)}, bf16[2,144,1152]{2,1,0:T(8,128)(2,1)}, u32[]{:S(2)}, u32[]{:S(2)}) %collective-permute-start.7) | collective-permute-done | bytes 663584 | tf_op jit(solution)/shard_map/ppermute | solution.py:25
  59.6 13.9 %collective-permute-done.10 = bf16[1,144,1152]{2,1,0:T(8,128)(2,1)S(1)} collective-permute-done((bf16[1,144,1152]{2,1,0:T(8,128)(2,1)S(1)}, bf16[1,144,1152]{2,1,0:T(8,128)(2,1)S(1)}, u32[]{:S(2)}, u32[]{:S(2)}) %collective-permute-start.10) | collective-permute-done | bytes 331808 | tf_op jit(solution)/shard_map/ppermute | solution.py:25
  73.4 10.9 %collective-permute-done.8.refs_4_.refs_5_ = bf16[4,144,1152]{2,1,0:T(8,128)(2,1)S(1)} collective-permute-done((bf16[4,144,1152]{2,1,0:T(8,128)(2,1)S(1)}, bf16[4,144,1152]{2,1,0:T(8,128)(2,1)S(1)}, u32[]{:S(2)}, u32[]{:S(2)}) %collective-permute-start.8) | collective-permute-done | bytes 1327136 | tf_op jit(solution)/shard_map/ppermute | solution.py:25
  89.1 13.8 %collective-permute-done.12.refs_6_.refs_7_ = bf16[4,64,1152]{2,1,0:T(8,128)(2,1)} collective-permute-done((bf16[4,64,1152]{2,1,0:T(8,128)(2,1)S(1)}, bf16[4,64,1152]{2,1,0:T(8,128)(2,1)}, u32[]{:S(2)}, u32[]{:S(2)}) %collective-permute-start.12) | collective-permute-done | bytes 589856 | tf_op jit(solution)/shard_map/ppermute | solution.py:25
  112.7 17.3 %project.1 = (bf16[768,1152]{1,0:T(8,128)(2,1)}, bf16[4,768,864]{2,1,0:T(8,128)(2,1)}, bf16[1152,1152]{1,0:T(8,128)(2,1)}) custom-call(s32[2]{0:T(128)} %pad_add_fusion.me_ref, bf16[768,1152]{1,0:T(8,128)(2,1)} %refs_1_.5, f32[3,6,1152]{2,1,0:T(8,128)} %copy-done.4, f32[4,1,864]{2,1,0:T(1,128)} %copy-done.17, bf16[4,144,1152]{2,1,0:T(8,128)(2,1)} %copy-done.24, ...), custom_call_target="tpu_custom_call" | custom-call | flops 100000000 | bytes 1 | tf_op jit(solution)/shard_map/project/pallas_call | solution.py:362
  130.0 14.7 %collective-permute-done.16.refs_4_.refs_6_ = bf16[4,144,1152]{2,1,0:T(8,128)(2,1)S(1)} collective-permute-done((bf16[4,144,1152]{2,1,0:T(8,128)(2,1)S(1)}, bf16[4,144,1152]{2,1,0:T(8,128)(2,1)S(1)}, u32[]{:S(2)}, u32[]{:S(2)}) %collective-permute-start.16) | collective-permute-done | bytes 1327136 | tf_op jit(solution)/shard_map/ppermute | solution.py:25
  147.3 2.5 collective-permute-start.23
  149.8 11.6 %attend.1.attended_ref.refs_5_ = bf16[768,1152]{1,0:T(8,128)(2,1)} custom-call(bf16[4,768,864]{2,1,0:T(8,128)(2,1)} %get-tuple-element.216.qkv_ref), custom_call_target="tpu_custom_call" | custom-call | flops 100000000 | bytes 1 | tf_op jit(solution)/shard_map/attend/pallas_call | solution.py:106
  165.9 7.7 %merge.1 = (f32[768,1152]{1,0:T(8,128)}, bf16[768,1152]{1,0:T(8,128)(2,1)}) custom-call(bf16[768,1152]{1,0:T(8,128)(2,1)} %attend.1.attended_ref.refs_5_, bf16[1152,1152]{1,0:T(8,128)(2,1)} %get-tuple-element.221.weight_ref.refs_0_, bf16[768,1152]{1,0:T(8,128)(2,1)} %refs_1_.5, f32[3,6,1152]{2,1,0:T(8,128)} %copy-done.4, f32[1,1152]{1,0:T(1,128)} %get-tuple-element.404.bias_ref), custom_call_target="tpu_custom_call" | custom-call | flops 100000000 | bytes 1 | tf_op jit(solution)/shard_map/merge/pallas_call | solution.py:444
  175.1 22.6 %up.1 = (bf16[4,768,1152]{2,1,0:T(8,128)(2,1)}, bf16[4,768,1152]{2,1,0:T(8,128)(2,1)}, bf16[4,4,144,1152]{3,2,1,0:T(8,128)(2,1)}) custom-call(s32[2]{0:T(128)} %pad_add_fusion.me_ref, bf16[768,1152]{1,0:T(8,128)(2,1)} %get-tuple-element.241.refs_0_.block_ref, f32[4,1,1152]{2,1,0:T(1,128)} %copy-done.16, bf16[4,144,768]{2,1,0:T(8,128)(2,1)} %copy-done.9, ...), custom_call_target="tpu_custom_call" | custom-call | flops 100000000 | bytes 1 | tf_op jit(solution)/shard_map/up/pallas_call | solution.py:362
  201.6 21.3 %gelu_back.1 = (bf16[4,768,1152]{2,1,0:T(8,128)(2,1)}, f32[4,1,1152]{2,1,0:T(1,128)}, bf16[4,4,144,1152]{3,2,1,0:T(8,128)(2,1)}) custom-call(s32[2]{0:T(128)} %pad_add_fusion.me_ref, bf16[768,1152]{1,0:T(8,128)(2,1)} %copy-done.5, bf16[4,768,1152]{2,1,0:T(8,128)(2,1)} %get-tuple-element.240.refs_1_, bf16[4,144,768]{2,1,0:T(8,128)(2,1)} %copy-done.12, ...), custom_call_target="tpu_custom_call" | custom-call | flops 100000000 | bytes 1 | tf_op jit(solution)/shard_map/gelu_back/pallas_call | solution.py:362
  223.0 10.7 %weight_grad.3 = (bf16[2,4,64,1152]{3,2,1,0:T(8,128)(2,1)}, bf16[2,4,64,1152]{3,2,1,0:T(8,128)(2,1)}, bf16[2,4,80,1152]{3,2,1,0:T(8,128)(2,1)}, bf16[2,4,80,1152]{3,2,1,0:T(8,128)(2,1)}) custom-call(bf16[4,144,768]{2,1,0:T(8,128)(2,1)} %copy-done.8, bf16[4,768,1152]{2,1,0:T(8,128)(2,1)} %get-tuple-element.299.refs_1_.refs_0_, ...), custom_call_target="tpu_custom_call" | custom-call | flops 100000000 | bytes 1 | tf_op jit(solution)/shard_map/weight_grad/pallas_call | solution.py:760
  234.1 2.5 collective-permute-start.32
  238.9 20.9 %up_back.1 = (f32[768,1152]{1,0:T(8,128)}, bf16[768,1152]{1,0:T(8,128)(2,1)}, f32[3,3,1152]{2,1,0:T(4,128)}, f32[1,1152]{1,0:T(1,128)}) custom-call(s32[2]{0:T(128)} %pad_add_fusion.me_ref, bf16[4,768,1152]{2,1,0:T(8,128)(2,1)} %get-tuple-element.274.refs_0_.refs_1_, bf16[768,1152]{1,0:T(8,128)(2,1)} %refs_1_.5, f32[768,1152]{1,0:T(8,128)} %get-tuple-element.264.refs_2_, ...), custom_call_target="tpu_custom_call" | custom-call | flops 100000000 | bytes 1 | tf_op jit(solution)/shard_map/up_back/pallas_call | solution.py:362
  262.7 19.3 %attend_back.1.refs_0_.refs_2_ = bf16[4,768,896]{2,1,0:T(8,128)(2,1)} custom-call(bf16[4,768,864]{2,1,0:T(8,128)(2,1)} %get-tuple-element.216.qkv_ref, bf16[768,1152]{1,0:T(8,128)(2,1)} %get-tuple-element.266.block_ref.grad_ref, bf16[1152,1152]{1,0:T(8,128)(2,1)} %get-tuple-element.221.weight_ref.refs_0_), custom_call_target="tpu_custom_call" | custom-call | flops 100000000 | bytes 1 | tf_op jit(solution)/shard_map/attend_back/pallas_call | solution.py:153
  282.5 2.7 add_convert_fusion.4
  288.3 15.5 %weight_grad.4 = (bf16[2,4,64,1440]{3,2,1,0:T(8,128)(2,1)}, bf16[2,4,64,1440]{3,2,1,0:T(8,128)(2,1)}, bf16[2,4,80,1440]{3,2,1,0:T(8,128)(2,1)}, bf16[2,4,80,1440]{3,2,1,0:T(8,128)(2,1)}) custom-call(bf16[4,144,768]{2,1,0:T(8,128)(2,1)} %copy-done.10, bf16[4,768,1152]{2,1,0:T(8,128)(2,1)} %get-tuple-element.274.refs_0_.refs_1_, ...), custom_call_target="tpu_custom_call" | custom-call | flops 100000000 | bytes 1 | tf_op jit(solution)/shard_map/weight_grad/pallas_call | solution.py:760
  309.0 18.2 %project_back.1 = (f32[768,1152]{1,0:T(8,128)}, f32[3,2,1152]{2,1,0:T(2,128)}, f32[4,1,864]{2,1,0:T(1,128)}) custom-call(s32[2]{0:T(128)} %pad_add_fusion.me_ref, bf16[4,768,896]{2,1,0:T(8,128)(2,1)} %attend_back.1.refs_0_.refs_2_, bf16[768,1152]{1,0:T(8,128)(2,1)} %refs_1_.5, f32[768,1152]{1,0:T(8,128)} %get-tuple-element.288.refs_2_, ...), custom_call_target="tpu_custom_call" | custom-call | flops 100000000 | bytes 1 | tf_op jit(solution)/shard_map/project_back/pallas_call | solution.py:362
  329.2 12.6 %weight_grad.5 = (bf16[2,4,64,864]{3,2,1,0:T(8,128)(2,1)}, bf16[2,4,64,864]{3,2,1,0:T(8,128)(2,1)}, bf16[2,4,80,864]{3,2,1,0:T(8,128)(2,1)}, bf16[2,4,80,864]{3,2,1,0:T(8,128)(2,1)}) custom-call(bf16[4,144,768]{2,1,0:T(8,128)(2,1)} %copy-done.7, bf16[4,144,768]{2,1,0:T(8,128)(2,1)} %copy-done.47, bf16[4,768,896]{2,1,0:T(8,128)(2,1)} %attend_back.1.refs_0_.refs_2_, ...), custom_call_target="tpu_custom_call" | custom-call | flops 100000000 | bytes 1 | tf_op jit(solution)/shard_map/weight_grad/pallas_call | solution.py:760
  341.8 2.5 collective-permute-done.41
  344.3 4.6 collective-permute-done.39
  357.3 18.2 %down.1 = (bf16[768,1152]{1,0:T(8,128)(2,1)}, f32[3,1,1152]{2,1,0:T(1,128)}) custom-call(s32[2]{0:T(128)} %pad_add_fusion.me_ref, bf16[4,768,1152]{2,1,0:T(8,128)(2,1)} %get-tuple-element.299.refs_1_.refs_0_, bf16[768,1152]{1,0:T(8,128)(2,1)} %refs_1_.5, f32[768,1152]{1,0:T(8,128)} %get-tuple-element.264.refs_2_, f32[3,6,1152]{2,1,0:T(8,128)} %copy-done.4, ...), custom_call_target="tpu_custom_call" | custom-call | flops 100000000 | bytes 1 | tf_op jit(solution)/shard_map/down/pallas_call | solution.py:362
  380.8 14.9 %collective-permute-done.45 = bf16[2,4,64,864]{3,2,1,0:T(8,128)(2,1)} collective-permute-done((bf16[2,4,64,864]{3,2,1,0:T(8,128)(2,1)}, bf16[2,4,64,864]{3,2,1,0:T(8,128)(2,1)}, u32[]{:S(2)}, u32[]{:S(2)}) %collective-permute-start.45) | collective-permute-done | bytes 884768 | tf_op jit(solution)/shard_map/ppermute | solution.py:25
  395.7 3.2 collective-permute-done.44
  411.4 11.1 %collective-permute-done.50 = f32[80,288]{1,0:T(8,128)S(1)} collective-permute-done((f32[80,288]{1,0:T(8,128)S(1)}, f32[80,288]{1,0:T(8,128)S(1)}, u32[]{:S(2)}, u32[]{:S(2)}) %collective-permute-start.50) | collective-permute-done | bytes 92192 | tf_op jit(solution)/shard_map/ppermute | solution.py:25
  426.3 4.6 collective-permute-done.53
  449.1 7.1 %collective-permute-done.60 = bf16[144,864]{1,0:T(8,128)(2,1)S(1)} collective-permute-done((bf16[144,864]{1,0:T(8,128)(2,1)S(1)}, bf16[144,864]{1,0:T(8,128)(2,1)S(1)}, u32[]{:S(2)}, u32[]{:S(2)}) %collective-permute-start.60) | collective-permute-done | bytes 248864 | tf_op jit(solution)/shard_map/ppermute | solution.py:25
  458.7 3.3 collective-permute-done.61
  (318 shorter events, 116.8 us)
Async XLA Ops:
  7.2 194.3 %all-gather.3.cloned.1.call-start = ((), (), s32[]{:S(2)}) async-start(), calls=%async_computation | async-start | bytes 10948608 | tf_op jit(solution)/shard_map/all_gather | solution.py:293
  8.9 19.0 %collective-permute-start.2 = (bf16[1,144,1152]{2,1,0:T(8,128)(2,1)S(1)}, bf16[1,144,1152]{2,1,0:T(8,128)(2,1)S(1)}, u32[]{:S(2)}, u32[]{:S(2)}) collective-permute-start(bf16[1,144,1152]{2,1,0:T(8,128)(2,1)S(1)} %maximum_bitcast_fusion), channel_id=1, source_target_pairs={{0,16},{4,20},{8,24},{12,28},{16,0},{20,4},{24,8},{28,12},{1,17},{... | collective-permute-start | bytes 995336 | tf_op jit(solution)/shard_map/ppermute | solution.py:25
  52.7 20.8 %collective-permute-start.11 = (bf16[4,144,1152]{2,1,0:T(8,128)(2,1)S(1)}, bf16[4,144,1152]{2,1,0:T(8,128)(2,1)S(1)}, u32[]{:S(2)}, u32[]{:S(2)}) collective-permute-start(bf16[4,144,1152]{2,1,0:T(8,128)(2,1)S(1)} %constant_dynamic-update-slice_fusion.refs_3_.refs_4_), channel_id=1, source_target_pairs={{0,4},{4,0},{8,12},{12,8},{16,20},{20,16},{24,28},{28,24},{1,5},{5... | collective-permute-start | bytes 3981320 | tf_op jit(solution)/shard_map/ppermute | solution.py:25
  52.7 31.5 %collective-permute-start.8 = (bf16[4,144,1152]{2,1,0:T(8,128)(2,1)S(1)}, bf16[4,144,1152]{2,1,0:T(8,128)(2,1)S(1)}, u32[]{:S(2)}, u32[]{:S(2)}) collective-permute-start(bf16[4,144,1152]{2,1,0:T(8,128)(2,1)S(1)} %constant_dynamic-update-slice_fusion.refs_3_.refs_4_), channel_id=1, source_target_pairs={{0,2},{1,3},{2,0},{3,1},{4,6},{5,7},{6,4},{7,5},{8,10},{9,11},{10,... | collective-permute-start | bytes 3981320 | tf_op jit(solution)/shard_map/ppermute | solution.py:25
  54.3 31.2 %collective-permute-start.9 = (bf16[4,144,1152]{2,1,0:T(8,128)(2,1)S(1)}, bf16[4,144,1152]{2,1,0:T(8,128)(2,1)S(1)}, u32[]{:S(2)}, u32[]{:S(2)}) collective-permute-start(bf16[4,144,1152]{2,1,0:T(8,128)(2,1)S(1)} %constant_dynamic-update-slice_fusion.refs_3_.refs_4_), channel_id=1, source_target_pairs={{0,1},{1,0},{2,3},{3,2},{4,5},{5,4},{6,7},{7,6},{8,9},{9,8},{10,11... | collective-permute-start | bytes 3981320 | tf_op jit(solution)/shard_map/ppermute | solution.py:25
  85.5 19.2 %collective-permute-start.15 = (bf16[4,144,1152]{2,1,0:T(8,128)(2,1)S(1)}, bf16[4,144,1152]{2,1,0:T(8,128)(2,1)S(1)}, u32[]{:S(2)}, u32[]{:S(2)}) collective-permute-start(bf16[4,144,1152]{2,1,0:T(8,128)(2,1)S(1)} %collective-permute-done.8.refs_4_.refs_5_), channel_id=1, source_target_pairs={{0,4},{4,0},{8,12},{12,8},{16,20},{20,16},{24,28},{28,24},{1,5},{5... | collective-permute-start | bytes 3981320 | tf_op jit(solution)/shard_map/ppermute | solution.py:25
  85.6 19.1 %collective-permute-start.13 = (bf16[4,80,1152]{2,1,0:T(8,128)(2,1)S(1)}, bf16[4,80,1152]{2,1,0:T(8,128)(2,1)}, u32[]{:S(2)}, u32[]{:S(2)}) collective-permute-start(bf16[4,80,1152]{2,1,0:T(8,128)(2,1)S(1)} %slice.118), channel_id=1, source_target_pairs={{0,2},{1,3},{2,0},{3,1},{4,6},{5,7},{6,4},{7,5},{8,10},{9,11},{10,... | collective-permute-start | bytes 2211848 | tf_op jit(solution)/shard_map/ppermute | solution.py:25
  106.6 38.1 %collective-permute-start.16 = (bf16[4,144,1152]{2,1,0:T(8,128)(2,1)S(1)}, bf16[4,144,1152]{2,1,0:T(8,128)(2,1)S(1)}, u32[]{:S(2)}, u32[]{:S(2)}) collective-permute-start(bf16[4,144,1152]{2,1,0:T(8,128)(2,1)S(1)} %constant_dynamic-update-slice_fusion.2.refs_3_.refs_5_), channel_id=1, source_target_pairs={{0,2},{1,3},{2,0},{3,1},{4,6},{5,7},{6,4},{7,5},{8,10},{9,11},{10,... | collective-permute-start | bytes 3981320 | tf_op jit(solution)/shard_map/ppermute | solution.py:25
  107.2 38.5 %collective-permute-start.17 = (bf16[4,144,1152]{2,1,0:T(8,128)(2,1)S(1)}, bf16[4,144,1152]{2,1,0:T(8,128)(2,1)S(1)}, u32[]{:S(2)}, u32[]{:S(2)}) collective-permute-start(bf16[4,144,1152]{2,1,0:T(8,128)(2,1)S(1)} %constant_dynamic-update-slice_fusion.2.refs_3_.refs_5_), channel_id=1, source_target_pairs={{0,1},{1,0},{2,3},{3,2},{4,5},{5,4},{6,7},{7,6},{8,9},{9,8},{10,11... | collective-permute-start | bytes 3981320 | tf_op jit(solution)/shard_map/ppermute | solution.py:25
  111.8 33.8 %collective-permute-start.21 = (bf16[4,144,1152]{2,1,0:T(8,128)(2,1)S(1)}, bf16[4,144,1152]{2,1,0:T(8,128)(2,1)S(1)}, u32[]{:S(2)}, u32[]{:S(2)}) collective-permute-start(bf16[4,144,1152]{2,1,0:T(8,128)(2,1)S(1)} %constant_dynamic-update-slice_fusion.2.refs_3_.refs_5_), channel_id=1, source_target_pairs={{0,4},{4,0},{8,12},{12,8},{16,20},{20,16},{24,28},{28,24},{1,5},{5... | collective-permute-start | bytes 3981320 | tf_op jit(solution)/shard_map/ppermute | solution.py:25
  145.6 19.0 %collective-permute-start.25 = (bf16[4,144,1152]{2,1,0:T(8,128)(2,1)S(1)}, bf16[4,144,1152]{2,1,0:T(8,128)(2,1)S(1)}, u32[]{:S(2)}, u32[]{:S(2)}) collective-permute-start(bf16[4,144,1152]{2,1,0:T(8,128)(2,1)S(1)} %collective-permute-done.16.refs_4_.refs_6_), channel_id=1, source_target_pairs={{0,4},{4,0},{8,12},{12,8},{16,20},{20,16},{24,28},{28,24},{1,5},{5... | collective-permute-start | bytes 3981320 | tf_op jit(solution)/shard_map/ppermute | solution.py:25
  145.7 19.0 %collective-permute-start.24 = (bf16[4,80,1152]{2,1,0:T(8,128)(2,1)S(1)}, bf16[4,80,1152]{2,1,0:T(8,128)(2,1)S(1)}, u32[]{:S(2)}, u32[]{:S(2)}) collective-permute-start(bf16[4,80,1152]{2,1,0:T(8,128)(2,1)S(1)} %slice.120), channel_id=1, source_target_pairs={{0,2},{1,3},{2,0},{3,1},{4,6},{5,7},{6,4},{7,5},{8,10},{9,11},{10,... | collective-permute-start | bytes 2211848 | tf_op jit(solution)/shard_map/ppermute | solution.py:25
  149.8 23.8 %collective-permute-start.22 = (bf16[4,144,1152]{2,1,0:T(8,128)(2,1)S(1)}, bf16[4,144,1152]{2,1,0:T(8,128)(2,1)}, u32[]{:S(2)}, u32[]{:S(2)}) collective-permute-start(bf16[4,144,1152]{2,1,0:T(8,128)(2,1)S(1)} %collective-permute-done.17.refs_5_.refs_7_), channel_id=1, source_target_pairs={{0,4},{4,0},{8,12},{12,8},{16,20},{20,16},{24,28},{28,24},{1,5},{5... | collective-permute-start | bytes 3981320 | tf_op jit(solution)/shard_map/ppermute | solution.py:25
  175.1 22.7 %collective-permute-start.28 = (bf16[4,144,768]{2,1,0:T(8,128)(2,1)S(1)}, bf16[4,144,768]{2,1,0:T(8,128)(2,1)S(1)}, u32[]{:S(2)}, u32[]{:S(2)}) collective-permute-start(bf16[4,144,768]{2,1,0:T(8,128)(2,1)S(1)} %get-tuple-element.226), channel_id=1, source_target_pairs={{0,4},{4,0},{8,12},{12,8},{16,20},{20,16},{24,28},{28,24},{1,5},{5... | collective-permute-start | bytes 2654216 | tf_op jit(solution)/shard_map/ppermute | solution.py:25
  198.7 24.1 %collective-permute-start.29 = (bf16[4,4,144,1152]{3,2,1,0:T(8,128)(2,1)}, bf16[4,4,144,1152]{3,2,1,0:T(8,128)(2,1)}, u32[]{:S(2)}, u32[]{:S(2)}) collective-permute-start(bf16[4,4,144,1152]{3,2,1,0:T(8,128)(2,1)} %get-tuple-element.238), channel_id=1, source_target_pairs={{0,4},{4,0},{8,12},{12,8},{16,20},{20,16},{24,28},{28,24},{1,5},{5... | collective-permute-start | bytes 15925256 | tf_op jit(solution)/shard_map/ppermute | solution.py:25
  233.7 26.1 %collective-permute-start.33 = (bf16[768,1152]{1,0:T(8,128)(2,1)S(1)}, bf16[768,1152]{1,0:T(8,128)(2,1)}, u32[]{:S(2)}, u32[]{:S(2)}) collective-permute-start(bf16[768,1152]{1,0:T(8,128)(2,1)S(1)} %copy-done.21), channel_id=1, source_target_pairs={{0,4},{4,0},{8,12},{12,8},{16,20},{20,16},{24,28},{28,24},{1,5},{5... | collective-permute-start | bytes 5308424 | tf_op jit(solution)/shard_map/ppermute | solution.py:25
  234.1 47.9 %collective-permute-start.32 = (bf16[2,4,80,1152]{3,2,1,0:T(8,128)(2,1)}, bf16[2,4,80,1152]{3,2,1,0:T(8,128)(2,1)}, u32[]{:S(2)}, u32[]{:S(2)}) collective-permute-start(bf16[2,4,80,1152]{3,2,1,0:T(8,128)(2,1)} %get-tuple-element.261), channel_id=1, source_target_pairs={{0,1},{1,0},{2,3},{3,2},{4,5},{5,4},{6,7},{7,6},{8,9},{9,8},{10,11... | collective-permute-start | bytes 4423688 | tf_op jit(solution)/shard_map/ppermute | solution.py:25
  236.7 45.4 %collective-permute-start.31 = (bf16[2,4,64,1152]{3,2,1,0:T(8,128)(2,1)}, bf16[2,4,64,1152]{3,2,1,0:T(8,128)(2,1)}, u32[]{:S(2)}, u32[]{:S(2)}) collective-permute-start(bf16[2,4,64,1152]{3,2,1,0:T(8,128)(2,1)} %get-tuple-element.260), channel_id=1, source_target_pairs={{0,2},{1,3},{2,0},{3,1},{4,6},{5,7},{6,4},{7,5},{8,10},{9,11},{10,... | collective-permute-start | bytes 3538952 | tf_op jit(solution)/shard_map/ppermute | solution.py:25
  262.7 19.3 %collective-permute-start.34 = (bf16[4,144,768]{2,1,0:T(8,128)(2,1)S(1)}, bf16[4,144,768]{2,1,0:T(8,128)(2,1)S(1)}, u32[]{:S(2)}, u32[]{:S(2)}) collective-permute-start(bf16[4,144,768]{2,1,0:T(8,128)(2,1)S(1)} %get-tuple-element.267), channel_id=1, source_target_pairs={{0,4},{4,0},{8,12},{12,8},{16,20},{20,16},{24,28},{28,24},{1,5},{5... | collective-permute-start | bytes 2654216 | tf_op jit(solution)/shard_map/ppermute | solution.py:25
  282.1 22.2 %collective-permute-start.37 = (bf16[4,768,896]{2,1,0:T(8,128)(2,1)}, bf16[4,768,896]{2,1,0:T(8,128)(2,1)}, u32[]{:S(2)}, u32[]{:S(2)}) collective-permute-start(bf16[4,768,896]{2,1,0:T(8,128)(2,1)} %attend_back.1.refs_0_.refs_2_), channel_id=1, source_target_pairs={{0,4},{4,0},{8,12},{12,8},{16,20},{20,16},{24,28},{28,24},{1,5},{5... | collective-permute-start | bytes 16515080 | tf_op jit(solution)/shard_map/ppermute | solution.py:25
  285.3 19.0 %collective-permute-start.36 = (bf16[4,80,1152]{2,1,0:T(8,128)(2,1)}, bf16[4,80,1152]{2,1,0:T(8,128)(2,1)S(1)}, u32[]{:S(2)}, u32[]{:S(2)}) collective-permute-start(bf16[4,80,1152]{2,1,0:T(8,128)(2,1)} %get-tuple-element.384), channel_id=1, source_target_pairs={{0,2},{1,3},{2,0},{3,1},{4,6},{5,7},{6,4},{7,5},{8,10},{9,11},{10,... | collective-permute-start | bytes 2211848 | tf_op jit(solution)/shard_map/ppermute | solution.py:25
  304.3 44.6 %collective-permute-start.39 = (bf16[2,4,80,1440]{3,2,1,0:T(8,128)(2,1)}, bf16[2,4,80,1440]{3,2,1,0:T(8,128)(2,1)}, u32[]{:S(2)}, u32[]{:S(2)}) collective-permute-start(bf16[2,4,80,1440]{3,2,1,0:T(8,128)(2,1)} %get-tuple-element.284), channel_id=1, source_target_pairs={{0,1},{1,0},{2,3},{3,2},{4,5},{5,4},{6,7},{7,6},{8,9},{9,8},{10,11... | collective-permute-start | bytes 5529608 | tf_op jit(solution)/shard_map/ppermute | solution.py:25
  305.4 39.0 %collective-permute-start.38 = (bf16[2,4,64,1440]{3,2,1,0:T(8,128)(2,1)}, bf16[2,4,64,1440]{3,2,1,0:T(8,128)(2,1)}, u32[]{:S(2)}, u32[]{:S(2)}) collective-permute-start(bf16[2,4,64,1440]{3,2,1,0:T(8,128)(2,1)} %get-tuple-element.283), channel_id=1, source_target_pairs={{0,2},{1,3},{2,0},{3,1},{4,6},{5,7},{6,4},{7,5},{8,10},{9,11},{10,... | collective-permute-start | bytes 4423688 | tf_op jit(solution)/shard_map/ppermute | solution.py:25
  308.9 18.3 %collective-permute-start.40 = (bf16[2,144,1152]{2,1,0:T(8,128)(2,1)S(1)}, bf16[2,144,1152]{2,1,0:T(8,128)(2,1)S(1)}, u32[]{:S(2)}, u32[]{:S(2)}) collective-permute-start(bf16[2,144,1152]{2,1,0:T(8,128)(2,1)S(1)} %pad_maximum_fusion.3), channel_id=1, source_target_pairs={{0,8},{4,12},{8,0},{12,4},{16,24},{20,28},{24,16},{28,20},{1,9},{5... | collective-permute-start | bytes 1990664 | tf_op jit(solution)/shard_map/ppermute | solution.py:25
  351.2 24.8 %collective-permute-start.43 = (bf16[4,80,1440]{2,1,0:T(8,128)(2,1)S(1)}, bf16[4,80,1440]{2,1,0:T(8,128)(2,1)S(1)}, u32[]{:S(2)}, u32[]{:S(2)}) collective-permute-start(bf16[4,80,1440]{2,1,0:T(8,128)(2,1)S(1)} %get-tuple-element.380), channel_id=1, source_target_pairs={{0,2},{1,3},{2,0},{3,1},{4,6},{5,7},{6,4},{7,5},{8,10},{9,11},{10,... | collective-permute-start | bytes 2764808 | tf_op jit(solution)/shard_map/ppermute | solution.py:25
  354.8 20.7 %collective-permute-start.42 = (bf16[4,64,1440]{2,1,0:T(8,128)(2,1)S(1)}, bf16[4,64,1440]{2,1,0:T(8,128)(2,1)S(1)}, u32[]{:S(2)}, u32[]{:S(2)}) collective-permute-start(bf16[4,64,1440]{2,1,0:T(8,128)(2,1)S(1)} %get-tuple-element.382), channel_id=1, source_target_pairs={{0,1},{1,0},{2,3},{3,2},{4,5},{5,4},{6,7},{7,6},{8,9},{9,8},{10,11... | collective-permute-start | bytes 2211848 | tf_op jit(solution)/shard_map/ppermute | solution.py:25
  356.5 42.4 %collective-permute-start.46 = (bf16[2,4,80,864]{3,2,1,0:T(8,128)(2,1)}, bf16[2,4,80,864]{3,2,1,0:T(8,128)(2,1)}, u32[]{:S(2)}, u32[]{:S(2)}) collective-permute-start(bf16[2,4,80,864]{3,2,1,0:T(8,128)(2,1)} %get-tuple-element.316), channel_id=1, source_target_pairs={{0,1},{1,0},{2,3},{3,2},{4,5},{5,4},{6,7},{7,6},{8,9},{9,8},{10,11... | collective-permute-start | bytes 3317768 | tf_op jit(solution)/shard_map/ppermute | solution.py:25
  356.9 38.8 %collective-permute-start.45 = (bf16[2,4,64,864]{3,2,1,0:T(8,128)(2,1)}, bf16[2,4,64,864]{3,2,1,0:T(8,128)(2,1)}, u32[]{:S(2)}, u32[]{:S(2)}) collective-permute-start(bf16[2,4,64,864]{3,2,1,0:T(8,128)(2,1)} %get-tuple-element.315), channel_id=1, source_target_pairs={{0,2},{1,3},{2,0},{3,1},{4,6},{5,7},{6,4},{7,5},{8,10},{9,11},{10,... | collective-permute-start | bytes 2654216 | tf_op jit(solution)/shard_map/ppermute | solution.py:25
  377.5 21.4 %collective-permute-start.47 = (bf16[2,144,1440]{2,1,0:T(8,128)(2,1)}, bf16[2,144,1440]{2,1,0:T(8,128)(2,1)}, u32[]{:S(2)}, u32[]{:S(2)}) collective-permute-start(bf16[2,144,1440]{2,1,0:T(8,128)(2,1)} %pad_maximum_fusion), channel_id=1, source_target_pairs={{0,8},{4,12},{8,0},{12,4},{16,24},{20,28},{24,16},{28,20},{1,9},{5... | collective-permute-start | bytes 2488328 | tf_op jit(solution)/shard_map/ppermute | solution.py:25
  379.1 19.8 %collective-permute-start.44 = (f32[2,80,288]{2,1,0:T(8,128)S(1)}, f32[2,80,288]{2,1,0:T(8,128)S(1)}, u32[]{:S(2)}, u32[]{:S(2)}) collective-permute-start(f32[2,80,288]{2,1,0:T(8,128)S(1)} %get-tuple-element.314), channel_id=1, source_target_pairs={{0,2},{1,3},{2,0},{3,1},{4,6},{5,7},{6,4},{7,5},{8,10},{9,11},{10,... | collective-permute-start | bytes 552968 | tf_op jit(solution)/shard_map/ppermute | solution.py:25
  400.1 26.2 %collective-permute-start.54 = (bf16[144,1440]{1,0:T(8,128)(2,1)S(1)}, bf16[144,1440]{1,0:T(8,128)(2,1)S(1)}, u32[]{:S(2)}, u32[]{:S(2)}) collective-permute-start(bf16[144,1440]{1,0:T(8,128)(2,1)S(1)} %fusion.9), channel_id=1, source_target_pairs={{0,16},{4,20},{8,24},{12,28},{16,0},{20,4},{24,8},{28,12},{1,17},{... | collective-permute-start | bytes 1244168 | tf_op jit(solution)/shard_map/ppermute | solution.py:25
  403.6 18.9 %collective-permute-start.52 = (bf16[4,80,864]{2,1,0:T(8,128)(2,1)S(1)}, bf16[4,80,864]{2,1,0:T(8,128)(2,1)S(1)}, u32[]{:S(2)}, u32[]{:S(2)}) collective-permute-start(bf16[4,80,864]{2,1,0:T(8,128)(2,1)S(1)} %get-tuple-element.388), channel_id=1, source_target_pairs={{0,2},{1,3},{2,0},{3,1},{4,6},{5,7},{6,4},{7,5},{8,10},{9,11},{10,... | collective-permute-start | bytes 1658888 | tf_op jit(solution)/shard_map/ppermute | solution.py:25
  (92 other events, 984.7 us)
Sparse Core Ops, SparseCore 0:
  105.9 93.9 all-gather.2
